TPU v7x, 32 devices: a whole 2x2x4 slice. The times are simulated.
32 devices in a mesh: section: 2 (over core), fsdp: 4 (over z), tensor: 4 (over y, x).
Axes of the slice: x: 2, y: 2, z: 4, core: 2. Of those that a mesh axis runs over, the one named last changes fastest.
Arguments:
- inputs: bfloat16 [2, 4096, 640], P(None, ('fsdp', 'tensor')), may hold values from -6 to 6
- out_grad: bfloat16 [2, 4096, 640], P(None, ('fsdp', 'tensor')), may hold values from -6 to 6
- segment_ids: int32 [2, 4096], P(None, 'fsdp'), may hold values from 0 to 1, as said below
- positions: int32 [2, 4096], P(None, 'fsdp'), may hold values from 0 to 1023, as said below
- before_gain: bfloat16 [2, 640], P('section', 'fsdp'), may hold values from 0.25 to 1.75
- query_matrix: bfloat16 [2, 640, 1024], P('section', 'fsdp', 'tensor'), may hold values from -0.25 to 0.25
- key_matrix: bfloat16 [2, 640, 256], P('section', 'fsdp'), may hold values from -0.25 to 0.25
- value_matrix: bfloat16 [2, 640, 256], P('section', 'fsdp'), may hold values from -0.25 to 0.25
- query_gain: bfloat16 [2, 256], P('section', 'fsdp'), may hold values from 0.25 to 1.75
- key_gain: bfloat16 [2, 256], P('section', 'fsdp'), may hold values from 0.25 to 1.75
- output_matrix: bfloat16 [2, 1024, 640], P('section', 'tensor', 'fsdp'), may hold values from -0.1875 to 0.1875
- after_gain: bfloat16 [2, 640], P('section', 'fsdp'), may hold values from 0.25 to 1.75
- feed_gain: bfloat16 [2, 640], P('section', 'fsdp'), may hold values from 0.25 to 1.75
- gate_matrix: bfloat16 [2, 640, 2048], P('section', 'fsdp', 'tensor'), may hold values from -0.25 to 0.25
- up_matrix: bfloat16 [2, 640, 2048], P('section', 'fsdp', 'tensor'), may hold values from -0.25 to 0.25
- down_matrix: bfloat16 [2, 2048, 640], P('section', 'tensor', 'fsdp'), may hold values from -0.125 to 0.125
- final_gain: bfloat16 [2, 640], P('section', 'fsdp'), may hold values from 0.25 to 1.75
Outputs:
- layer_out: bfloat16 [2, 2, 4096, 640], P('section', None, ('fsdp', 'tensor'))
- input_grad: float32 [2, 2, 4096, 640], P('section', None, ('fsdp', 'tensor'))
- grad_before_gain: float32 [2, 640], P('section', 'fsdp')
- grad_query_matrix: float32 [2, 640, 1024], P('section', 'fsdp', 'tensor')
- grad_key_matrix: float32 [2, 640, 256], P('section', 'fsdp')
- grad_value_matrix: float32 [2, 640, 256], P('section', 'fsdp')
- grad_query_gain: float32 [2, 256], P('section', 'fsdp')
- grad_key_gain: float32 [2, 256], P('section', 'fsdp')
- grad_output_matrix: float32 [2, 1024, 640], P('section', 'tensor', 'fsdp')
- grad_after_gain: float32 [2, 640], P('section', 'fsdp')
- grad_feed_gain: float32 [2, 640], P('section', 'fsdp')
- grad_gate_matrix: float32 [2, 640, 2048], P('section', 'fsdp', 'tensor')
- grad_up_matrix: float32 [2, 640, 2048], P('section', 'fsdp', 'tensor')
- grad_down_matrix: float32 [2, 2048, 640], P('section', 'tensor', 'fsdp')
- grad_final_gain: float32 [2, 640], P('section', 'fsdp')
Inputs may be any that keep to these rules, and one draw needn't show every extreme that they name: `segment_ids`: within each aligned block of 1024 tokens of a micro-batch (one data rank's pack) the ids never fall and hold one or two sequences; one of them has more than 768 tokens. Each sequence's positions count 0, 1, 2, ... from its first token.
All inputs are finite; a program needn't handle non-finite values.
Results may differ from a plain program's by a relative error of at most 0.03.
Values may be sent and summed in bfloat16 or wider, within the bound.
No kernel may reach another device: no remote copies, remote signals or barrier semaphores. Data moves between devices by JAX's collectives and lax.ppermute only.
A program may use at most 192 MiB of HBM per device.

v0:
```python
import jax
import jax.numpy as jnp
from jax import lax
from jax.sharding import PartitionSpec as P

WINDOW = 512


EPSILON = 1e-06


def shifted(value, axis, by):
    count = lax.axis_size(axis)
    pairs = [(i, i + by) for i in range(count) if 0 <= i + by < count]
    return lax.ppermute(value, axis, pairs)


def norm_rows(value_rows, gain_value):
    return (
        value_rows
        * lax.rsqrt(jnp.mean(value_rows * value_rows, axis=-1, keepdims=True) + EPSILON)
        * gain_value
    )


def angles(token_positions, head_width):
    half_depth = head_width // 2
    frequency = 10000.0 ** (-(jnp.arange(half_depth, dtype=jnp.float32) * 2.0) / head_width)
    return token_positions.astype(jnp.float32)[..., None] * frequency


def rotate(value_rows, turn_angle):
    half_depth = value_rows.shape[-1] // 2
    cosine = jnp.cos(turn_angle)
    sine_part = jnp.sin(turn_angle)
    first_half = value_rows[..., :half_depth]
    second = value_rows[..., half_depth:]
    return jnp.concatenate(
        [first_half * cosine - second * sine_part, second * cosine + first_half * sine_part],
        axis=-1,
    )


def key_block_rows(rows_in, fill_value):
    pad_rows = jnp.full((WINDOW,) + rows_in.shape[1:], fill_value, rows_in.dtype)
    padded = jnp.concatenate([pad_rows, rows_in]).reshape((-1, WINDOW) + rows_in.shape[1:])
    return jnp.concatenate([padded[:-1], padded[1:]], axis=1)


def window_mask(segments, token_positions):
    block_count = segments.shape[0] // WINDOW
    key_segments = key_block_rows(segments, -1)
    key_positions = key_block_rows(token_positions, 0)
    query_segments = segments.reshape(block_count, WINDOW)
    query_positions = token_positions.reshape(block_count, WINDOW)
    position_gap = query_positions[:, :, None] - key_positions[:, None, :]
    return (
        (query_segments[:, :, None] == key_segments[:, None, :])
        & (position_gap >= 0)
        & (position_gap < WINDOW)
    )


def matmul(left, right):
    return jnp.dot(left, right, preferred_element_type=jnp.float32)


def times_transposed(left, right):
    return lax.dot_general(
        left, right, (((1,), (1,)), ((), ())), preferred_element_type=jnp.float32
    )


def transposed_times(left, right):
    return lax.dot_general(
        left, right, (((0,), (0,)), ((), ())), preferred_element_type=jnp.float32
    )


def unblock(block_grads):
    head_width = block_grads.shape[-1]
    zero_block = jnp.zeros((1, WINDOW, head_width), jnp.float32)
    earlier = jnp.concatenate([block_grads[:, :WINDOW], zero_block])
    later_part = jnp.concatenate([zero_block, block_grads[:, WINDOW:]])
    return (earlier + later_part)[1:].reshape(-1, head_width)


def attend(queries, key_rows, value_rows, allowed, score_scale):
    block_count = allowed.shape[0]
    group_rows, head_count, head_width = queries.shape
    query_block_rows = queries.reshape(block_count, WINDOW, head_count, head_width)
    logit_scores = (
        jnp.einsum(
            "jyre,jwe->jyrw",
            query_block_rows,
            key_block_rows(key_rows, 0.0),
            preferred_element_type=jnp.float32,
        )
        * score_scale
    )
    masked = jnp.where(allowed[:, :, None, :], logit_scores, -1e30)
    largest = jnp.max(masked, axis=-1, keepdims=True)
    exponent = jnp.exp(masked - largest)
    softmax_sum = jnp.sum(exponent, axis=-1, keepdims=True)
    attention_weights = (exponent / softmax_sum).astype(jnp.bfloat16)
    attended_values = jnp.einsum(
        "ytfi,yij->ytfj",
        attention_weights,
        key_block_rows(value_rows, 0.0),
        preferred_element_type=jnp.float32,
    )
    log_total = largest + jnp.log(softmax_sum)
    return (
        attended_values.reshape(group_rows, head_count * head_width).astype(jnp.bfloat16),
        log_total,
    )


def attend_back(queries, key_rows, value_rows, allowed, log_total, grad_attended, score_scale):
    block_count = allowed.shape[0]
    group_rows, head_count, head_width = queries.shape
    query_block_rows = queries.reshape(block_count, WINDOW, head_count, head_width)
    key_tile = key_block_rows(key_rows, 0.0)
    value_tile = key_block_rows(value_rows, 0.0)
    block_gradients = grad_attended.reshape(block_count, WINDOW, head_count, head_width)
    logit_scores = (
        jnp.einsum("jyre,jwe->jyrw", query_block_rows, key_tile, preferred_element_type=jnp.float32)
        * score_scale
    )
    masked = jnp.where(allowed[:, :, None, :], logit_scores, -1e30)
    attention_weights = jnp.exp(masked - log_total)
    grad_values = jnp.einsum(
        "owas,owap->osp",
        attention_weights.astype(jnp.bfloat16),
        block_gradients,
        preferred_element_type=jnp.float32,
    )
    grad_chances = jnp.einsum(
        "jyre,jwe->jyrw", block_gradients, value_tile, preferred_element_type=jnp.float32
    )
    weighted = jnp.sum(attention_weights * grad_chances, axis=-1, keepdims=True)
    score_gradient = (attention_weights * (grad_chances - weighted)).astype(jnp.bfloat16)
    grad_queries = (
        jnp.einsum("ytfi,yij->ytfj", score_gradient, key_tile, preferred_element_type=jnp.float32)
        * score_scale
    )
    grad_keys = (
        jnp.einsum(
            "owas,owap->osp", score_gradient, query_block_rows, preferred_element_type=jnp.float32
        )
        * score_scale
    )
    return (
        grad_queries.reshape(group_rows, head_count, head_width),
        unblock(grad_keys),
        unblock(grad_values),
    )


def layer_forward(inputs_now, params, segments, token_positions):
    (
        before_gain,
        query_matrix,
        key_matrix,
        value_matrix,
        query_gain,
        key_gain,
        output_matrix,
        after_gain,
        feed_gain,
        gate_matrix,
        up_matrix,
        down_matrix,
        final_gain,
    ) = params
    head_width = key_matrix.shape[1]
    head_count = query_matrix.shape[1] // head_width
    normed_low = norm_rows(inputs_now, before_gain.astype(jnp.float32)).astype(jnp.bfloat16)
    gathered = lax.all_gather(normed_low, "tensor", axis=0, tiled=True)
    query_raw = matmul(gathered, query_matrix)
    key_raw = matmul(gathered, key_matrix)
    value_rows = matmul(gathered, value_matrix).astype(jnp.bfloat16)
    turn_angle = angles(token_positions, head_width)
    query_heads = query_raw.reshape(-1, head_count, head_width)
    queries = rotate(
        norm_rows(query_heads, query_gain.astype(jnp.float32)), turn_angle[:, None, :]
    ).astype(jnp.bfloat16)
    key_rows = rotate(norm_rows(key_raw, key_gain.astype(jnp.float32)), turn_angle).astype(
        jnp.bfloat16
    )
    allowed = window_mask(segments, token_positions)
    attended_values, log_total = attend(
        queries, key_rows, value_rows, allowed, head_width ** (-0.5)
    )
    attention_sum = lax.psum_scatter(
        matmul(attended_values, output_matrix), "tensor", scatter_dimension=0, tiled=True
    )
    hidden = inputs_now + norm_rows(attention_sum, after_gain.astype(jnp.float32))
    feed_low = norm_rows(hidden, feed_gain.astype(jnp.float32)).astype(jnp.bfloat16)
    feed_all = lax.all_gather(feed_low, "tensor", axis=0, tiled=True)
    gate_value = matmul(feed_all, gate_matrix)
    up_value = matmul(feed_all, up_matrix)
    product = (jax.nn.gelu(gate_value, approximate=True) * up_value).astype(jnp.bfloat16)
    branch = lax.psum_scatter(
        matmul(product, down_matrix).astype(jnp.bfloat16), "tensor", scatter_dimension=0, tiled=True
    ).astype(jnp.float32)
    result = hidden + norm_rows(branch, final_gain.astype(jnp.float32))
    kept_state = (
        inputs_now,
        gathered,
        queries,
        key_rows,
        value_rows,
        log_total,
        attended_values,
        attention_sum,
        hidden,
        feed_all,
        product,
        branch,
    )
    return (result, kept_state)


def layer_backward(grad_result, kept_state, params, segments, token_positions):
    (
        before_gain,
        query_matrix,
        key_matrix,
        value_matrix,
        query_gain,
        key_gain,
        output_matrix,
        after_gain,
        feed_gain,
        gate_matrix,
        up_matrix,
        down_matrix,
        final_gain,
    ) = params
    (
        inputs_now,
        gathered,
        queries,
        key_rows,
        value_rows,
        log_total,
        attended_values,
        attention_sum,
        hidden,
        feed_all,
        product,
        branch,
    ) = kept_state
    row_count = inputs_now.shape[0]
    head_width = key_matrix.shape[1]
    head_count = query_matrix.shape[1] // head_width
    unused, pullback = jax.vjp(norm_rows, branch, final_gain.astype(jnp.float32))
    grad_branch, grad_final = pullback(grad_result)
    branch_cot = lax.all_gather(grad_branch.astype(jnp.bfloat16), "tensor", axis=0, tiled=True)
    grad_product = times_transposed(branch_cot, down_matrix)
    grad_down = transposed_times(product, branch_cot)
    gate_value = matmul(feed_all, gate_matrix)
    up_value = matmul(feed_all, up_matrix)
    unused, pullback = jax.vjp(
        lambda gate_in, up_in: jax.nn.gelu(gate_in, approximate=True) * up_in, gate_value, up_value
    )
    grad_gate_value, grad_up_value = pullback(grad_product)
    grad_gate_value = grad_gate_value.astype(jnp.bfloat16)
    grad_up_value = grad_up_value.astype(jnp.bfloat16)
    grad_gate = transposed_times(feed_all, grad_gate_value)
    grad_up = transposed_times(feed_all, grad_up_value)
    grad_feed_in = lax.psum_scatter(
        (
            times_transposed(grad_gate_value, gate_matrix)
            + times_transposed(grad_up_value, up_matrix)
        ).astype(jnp.bfloat16),
        "tensor",
        scatter_dimension=0,
        tiled=True,
    ).astype(jnp.float32)
    unused, pullback = jax.vjp(norm_rows, hidden, feed_gain.astype(jnp.float32))
    part_hidden, grad_feed = pullback(grad_feed_in)
    grad_hidden = grad_result + part_hidden
    unused, pullback = jax.vjp(norm_rows, attention_sum, after_gain.astype(jnp.float32))
    grad_sum, grad_after = pullback(grad_hidden)
    sum_cot = lax.all_gather(grad_sum.astype(jnp.bfloat16), "tensor", axis=0, tiled=True)
    grad_output = transposed_times(attended_values, sum_cot)
    grad_attended = times_transposed(sum_cot, output_matrix).astype(jnp.bfloat16)
    allowed = window_mask(segments, token_positions)
    grad_queries, grad_keys, grad_values = attend_back(
        queries, key_rows, value_rows, allowed, log_total, grad_attended, head_width ** (-0.5)
    )
    grad_keys, grad_values = (
        lax.psum(grad_keys.astype(jnp.bfloat16), "tensor").astype(jnp.float32),
        lax.psum(grad_values.astype(jnp.bfloat16), "tensor").astype(jnp.float32),
    )
    query_raw = matmul(gathered, query_matrix)
    key_raw = matmul(gathered, key_matrix)
    turn_angle = angles(token_positions, head_width)
    unused, pullback = jax.vjp(
        lambda raw_value, gain_value: rotate(
            norm_rows(raw_value, gain_value), turn_angle[:, None, :]
        ),
        query_raw.reshape(-1, head_count, head_width),
        query_gain.astype(jnp.float32),
    )
    grad_query_raw, grad_qgain = pullback(grad_queries)
    unused, pullback = jax.vjp(
        lambda raw_value, gain_value: rotate(norm_rows(raw_value, gain_value), turn_angle),
        key_raw,
        key_gain.astype(jnp.float32),
    )
    grad_key_raw, grad_kgain = pullback(grad_keys)
    grad_query_raw = grad_query_raw.reshape(-1, head_count * head_width).astype(jnp.bfloat16)
    grad_key_raw = grad_key_raw.astype(jnp.bfloat16)
    grad_values = grad_values.astype(jnp.bfloat16)
    grad_query = transposed_times(gathered, grad_query_raw)
    grad_key = transposed_times(gathered, grad_key_raw)
    grad_value = transposed_times(gathered, grad_values)
    grad_normed = lax.psum_scatter(
        times_transposed(grad_query_raw, query_matrix).astype(jnp.bfloat16),
        "tensor",
        scatter_dimension=0,
        tiled=True,
    ).astype(jnp.float32)
    first_row = lax.axis_index("tensor") * row_count
    own_keys = lax.dynamic_slice_in_dim(grad_key_raw, first_row, row_count, 0)
    own_values = lax.dynamic_slice_in_dim(grad_values, first_row, row_count, 0)
    grad_normed = (
        grad_normed
        + times_transposed(own_keys, key_matrix)
        + times_transposed(own_values, value_matrix)
    )
    unused, pullback = jax.vjp(norm_rows, inputs_now, before_gain.astype(jnp.float32))
    part_inputs, grad_before = pullback(grad_normed)
    grad_inputs = grad_hidden + part_inputs
    gradients = (
        grad_before,
        grad_query,
        grad_key,
        grad_value,
        grad_qgain,
        grad_kgain,
        grad_output,
        grad_after,
        grad_feed,
        grad_gate,
        grad_up,
        grad_down,
        grad_final,
    )
    return (grad_inputs, gradients)


def fetch_weights(
    before_gain,
    query_matrix,
    key_matrix,
    value_matrix,
    query_gain,
    key_gain,
    output_matrix,
    after_gain,
    feed_gain,
    gate_matrix,
    up_matrix,
    down_matrix,
    final_gain,
):
    fetched = (
        lax.all_gather(before_gain, "fsdp", axis=1, tiled=True),
        lax.all_gather(query_matrix, "fsdp", axis=1, tiled=True),
        lax.all_gather(key_matrix, "fsdp", axis=1, tiled=True),
        lax.all_gather(value_matrix, "fsdp", axis=1, tiled=True),
        lax.all_gather(query_gain, "fsdp", axis=1, tiled=True),
        lax.all_gather(key_gain, "fsdp", axis=1, tiled=True),
        lax.all_gather(output_matrix, "fsdp", axis=2, tiled=True),
        lax.all_gather(after_gain, "fsdp", axis=1, tiled=True),
        lax.all_gather(feed_gain, "fsdp", axis=1, tiled=True),
        lax.all_gather(gate_matrix, "fsdp", axis=1, tiled=True),
        lax.all_gather(up_matrix, "fsdp", axis=1, tiled=True),
        lax.all_gather(down_matrix, "fsdp", axis=2, tiled=True),
        lax.all_gather(final_gain, "fsdp", axis=1, tiled=True),
    )
    return tuple((weight[0] for weight in fetched))


def settle(gradients):
    (
        grad_before,
        grad_query,
        grad_key,
        grad_value,
        grad_qgain,
        grad_kgain,
        grad_output,
        grad_after,
        grad_feed,
        grad_gate,
        grad_up,
        grad_down,
        grad_final,
    ) = gradients
    grad_before, grad_qgain, grad_after, grad_feed, grad_final = lax.psum(
        (grad_before, grad_qgain, grad_after, grad_feed, grad_final), "tensor"
    )
    return (
        lax.psum_scatter(
            grad_before[None].astype(jnp.bfloat16), "fsdp", scatter_dimension=1, tiled=True
        ).astype(jnp.float32),
        lax.psum_scatter(
            grad_query[None].astype(jnp.bfloat16), "fsdp", scatter_dimension=1, tiled=True
        ).astype(jnp.float32),
        lax.psum_scatter(
            grad_key[None].astype(jnp.bfloat16), "fsdp", scatter_dimension=1, tiled=True
        ).astype(jnp.float32),
        lax.psum_scatter(
            grad_value[None].astype(jnp.bfloat16), "fsdp", scatter_dimension=1, tiled=True
        ).astype(jnp.float32),
        lax.psum_scatter(
            grad_qgain[None].astype(jnp.bfloat16), "fsdp", scatter_dimension=1, tiled=True
        ).astype(jnp.float32),
        lax.psum_scatter(
            grad_kgain[None].astype(jnp.bfloat16), "fsdp", scatter_dimension=1, tiled=True
        ).astype(jnp.float32),
        lax.psum_scatter(
            grad_output[None].astype(jnp.bfloat16), "fsdp", scatter_dimension=2, tiled=True
        ).astype(jnp.float32),
        lax.psum_scatter(
            grad_after[None].astype(jnp.bfloat16), "fsdp", scatter_dimension=1, tiled=True
        ).astype(jnp.float32),
        lax.psum_scatter(
            grad_feed[None].astype(jnp.bfloat16), "fsdp", scatter_dimension=1, tiled=True
        ).astype(jnp.float32),
        lax.psum_scatter(
            grad_gate[None].astype(jnp.bfloat16), "fsdp", scatter_dimension=1, tiled=True
        ).astype(jnp.float32),
        lax.psum_scatter(
            grad_up[None].astype(jnp.bfloat16), "fsdp", scatter_dimension=1, tiled=True
        ).astype(jnp.float32),
        lax.psum_scatter(
            grad_down[None].astype(jnp.bfloat16), "fsdp", scatter_dimension=2, tiled=True
        ).astype(jnp.float32),
        lax.psum_scatter(
            grad_final[None].astype(jnp.bfloat16), "fsdp", scatter_dimension=1, tiled=True
        ).astype(jnp.float32),
    )


def body(
    inputs,
    out_grad,
    segment_ids,
    positions,
    before_gain,
    query_matrix,
    key_matrix,
    value_matrix,
    query_gain,
    key_gain,
    output_matrix,
    after_gain,
    feed_gain,
    gate_matrix,
    up_matrix,
    down_matrix,
    final_gain,
):
    stored = (
        before_gain,
        query_matrix,
        key_matrix,
        value_matrix,
        query_gain,
        key_gain,
        output_matrix,
        after_gain,
        feed_gain,
        gate_matrix,
        up_matrix,
        down_matrix,
        final_gain,
    )
    section_index = lax.axis_index("section")
    leading = section_index == 0
    micro_count = inputs.shape[0]
    row_count = inputs.shape[1]
    width = inputs.shape[2]
    params = None
    totals = tuple((jnp.zeros(weight.shape, jnp.float32) for weight in stored))
    layer_out = jnp.zeros(inputs.shape, jnp.bfloat16)
    input_grad = jnp.zeros(inputs.shape, jnp.float32)
    arriving = jnp.zeros((row_count, width), jnp.bfloat16)
    returning = jnp.zeros((row_count, width), jnp.bfloat16)
    buffers = None
    for tick_index in range(micro_count + 2):
        params = fetch_weights(*stored)
        forward_micro = tick_index - section_index
        forward_valid = (forward_micro >= 0) & (forward_micro < micro_count)
        forward_index = jnp.clip(forward_micro, 0, micro_count - 1)
        first_input = lax.dynamic_index_in_dim(inputs, forward_index, 0, keepdims=False)
        layer_input = jnp.where(leading, first_input, arriving).astype(jnp.float32)
        segments = lax.dynamic_index_in_dim(segment_ids, forward_index, 0, keepdims=False)
        token_positions = lax.dynamic_index_in_dim(positions, forward_index, 0, keepdims=False)
        result, kept_state = layer_forward(layer_input, params, segments, token_positions)
        result_low = result.astype(jnp.bfloat16)
        previous = lax.dynamic_index_in_dim(layer_out, forward_index, 0, keepdims=False)
        layer_out = lax.dynamic_update_index_in_dim(
            layer_out, jnp.where(forward_valid, result_low, previous), forward_index, 0
        )
        arriving = shifted(result_low, "section", 1)
        if buffers is None:
            buffers = tuple(
                (
                    jnp.zeros((micro_count,) + piece_state.shape, piece_state.dtype)
                    for piece_state in kept_state
                )
            )
        buffers = tuple(
            (
                lax.dynamic_update_index_in_dim(
                    buffer,
                    jnp.where(
                        forward_valid,
                        piece_state,
                        lax.dynamic_index_in_dim(buffer, forward_index, 0, keepdims=False),
                    ),
                    forward_index,
                    0,
                )
                for buffer, piece_state in zip(buffers, kept_state)
            )
        )
        backward_micro = tick_index - 2 + section_index
        backward_valid = (backward_micro >= 0) & (backward_micro < micro_count)
        backward_index = jnp.clip(backward_micro, 0, micro_count - 1)
        last_cot = lax.dynamic_index_in_dim(out_grad, backward_index, 0, keepdims=False)
        cotangent = jnp.where(leading, returning, last_cot).astype(jnp.float32)
        kept_back = tuple(
            (
                lax.dynamic_index_in_dim(buffer, backward_index, 0, keepdims=False)
                for buffer in buffers
            )
        )
        back_segments = lax.dynamic_index_in_dim(segment_ids, backward_index, 0, keepdims=False)
        back_positions = lax.dynamic_index_in_dim(positions, backward_index, 0, keepdims=False)
        grad_inputs, gradients = layer_backward(
            cotangent, kept_back, params, back_segments, back_positions
        )
        previous_grad = lax.dynamic_index_in_dim(input_grad, backward_index, 0, keepdims=False)
        input_grad = lax.dynamic_update_index_in_dim(
            input_grad, jnp.where(backward_valid, grad_inputs, previous_grad), backward_index, 0
        )
        returning = shifted(grad_inputs.astype(jnp.bfloat16), "section", -1)
        gradients = tuple((jnp.where(backward_valid, gradient, 0.0) for gradient in gradients))
        totals = tuple((total_grad + shard for total_grad, shard in zip(totals, settle(gradients))))
    return (layer_out[None], input_grad[None]) + tuple(totals)


def solution(mesh):
    in_specs = (
        P(None, ("fsdp", "tensor"), None),
        P(None, ("fsdp", "tensor"), None),
        P(None, "fsdp"),
        P(None, "fsdp"),
        P("section", "fsdp"),
        P("section", "fsdp", "tensor"),
        P("section", "fsdp", None),
        P("section", "fsdp", None),
        P("section", "fsdp"),
        P("section", "fsdp"),
        P("section", "tensor", "fsdp"),
        P("section", "fsdp"),
        P("section", "fsdp"),
        P("section", "fsdp", "tensor"),
        P("section", "fsdp", "tensor"),
        P("section", "tensor", "fsdp"),
        P("section", "fsdp"),
    )
    out_specs = (
        P("section", None, ("fsdp", "tensor"), None),
        P("section", None, ("fsdp", "tensor"), None),
        P("section", "fsdp"),
        P("section", "fsdp", "tensor"),
        P("section", "fsdp", None),
        P("section", "fsdp", None),
        P("section", "fsdp"),
        P("section", "fsdp"),
        P("section", "tensor", "fsdp"),
        P("section", "fsdp"),
        P("section", "fsdp"),
        P("section", "fsdp", "tensor"),
        P("section", "fsdp", "tensor"),
        P("section", "tensor", "fsdp"),
        P("section", "fsdp"),
    )
    return jax.shard_map(body, mesh=mesh, in_specs=in_specs, out_specs=out_specs, check_vma=False)
```

profile of v0, /device:TPU:0, one launch (start us, length us, event | category | flops | bytes accessed | tf_op | source)
XLA Modules:
  0.0 2552.8 jit_solution(14406928254367347805)
XLA Ops:
  112.6 38.4 %reduce-scatter.133.cloned.1.call-done = f32[256,640]{1,0:T(8,128)} async-done(((f32[1024,640]{1,0:T(8,128)}), f32[256,640]{1,0:T(8,128)}) %reduce-scatter.133.cloned.1.call-update) | async-done | bytes 655376 | tf_op jit(solution)/shard_map/reduce_scatter | solution.py:195
  217.2 26.2 %reduce-scatter.135.cloned.1.call-done = bf16[256,640]{1,0:T(8,128)(2,1)} async-done(((bf16[1024,640]{1,0:T(8,128)(2,1)}), bf16[256,640]{1,0:T(8,128)(2,1)}) %reduce-scatter.135.cloned.1.call-update) | async-done | bytes 327696 | tf_op jit(solution)/shard_map/reduce_scatter | solution.py:204
  285.2 21.5 all-gather.21.cloned.1.call-done
  351.0 31.2 %reduce-scatter.137.cloned.1.call-done = f32[256,640]{1,0:T(8,128)} async-done(((f32[1024,640]{1,0:T(8,128)}), f32[256,640]{1,0:T(8,128)}) %reduce-scatter.137.cloned.1.call-update) | async-done | bytes 655376 | tf_op jit(solution)/shard_map/reduce_scatter | solution.py:195
  507.1 28.2 %reduce-scatter.139.cloned.1.call-done = bf16[256,640]{1,0:T(8,128)(2,1)} async-done(((bf16[1024,640]{1,0:T(8,128)(2,1)}), bf16[256,640]{1,0:T(8,128)(2,1)}) %reduce-scatter.139.cloned.1.call-update) | async-done | bytes 327696 | tf_op jit(solution)/shard_map/reduce_scatter | solution.py:204
  542.8 24.8 reduce-scatter.151.cloned.1.call-done
  612.3 21.4 all-gather.37.cloned.1.call-done
  686.4 28.4 %reduce-scatter.141.cloned.1.call-done = f32[256,640]{1,0:T(8,128)} async-done(((f32[1024,640]{1,0:T(8,128)}), f32[256,640]{1,0:T(8,128)}) %reduce-scatter.141.cloned.1.call-update) | async-done | bytes 655376 | tf_op jit(solution)/shard_map/reduce_scatter | solution.py:195
  841.0 27.8 %reduce-scatter.143.cloned.1.call-done = bf16[256,640]{1,0:T(8,128)(2,1)} async-done(((bf16[1024,640]{1,0:T(8,128)(2,1)}), bf16[256,640]{1,0:T(8,128)(2,1)}) %reduce-scatter.143.cloned.1.call-update) | async-done | bytes 327696 | tf_op jit(solution)/shard_map/reduce_scatter | solution.py:204
  876.7 24.4 reduce-scatter.155.cloned.1.call-done
  945.7 21.5 all-gather.41.cloned.1.call-done
  1014.7 33.5 %reduce-scatter.145.cloned.1.call-done = f32[256,640]{1,0:T(8,128)} async-done(((f32[1024,640]{1,0:T(8,128)}), f32[256,640]{1,0:T(8,128)}) %reduce-scatter.145.cloned.1.call-update) | async-done | bytes 655376 | tf_op jit(solution)/shard_map/reduce_scatter | solution.py:195
  1128.3 41.0 %all-reduce.83.cloned.1.call-done = (bf16[1024,256]{1,0:T(8,128)(2,1)}, bf16[1024,256]{1,0:T(8,128)(2,1)}) async-done(((bf16[1024,256]{1,0:T(8,128)(2,1)}, bf16[1024,256]{1,0:T(8,128)(2,1)}), (bf16[1024,256]{1,0:T(8,128)(2,1)}, bf16[1024,256]{1,0:T(8,128)(2,1)})) %all-reduce.83.cloned.1.call-update) | async-done | bytes 1048592 | tf_op jit(solution)/shard_map/psum | solution.py:295
  1174.5 27.0 %reduce-scatter.159.cloned.1.call-done = bf16[256,640]{1,0:T(8,128)(2,1)} async-done(((bf16[1024,640]{1,0:T(8,128)(2,1)}), bf16[256,640]{1,0:T(8,128)(2,1)}) %reduce-scatter.159.cloned.1.call-update) | async-done | bytes 327696 | tf_op jit(solution)/shard_map/reduce_scatter | solution.py:321
  1207.7 26.1 %reduce-scatter.147.cloned.1.call-done = bf16[256,640]{1,0:T(8,128)(2,1)} async-done(((bf16[1024,640]{1,0:T(8,128)(2,1)}), bf16[256,640]{1,0:T(8,128)(2,1)}) %reduce-scatter.147.cloned.1.call-update) | async-done | bytes 327696 | tf_op jit(solution)/shard_map/reduce_scatter | solution.py:204
  1284.7 23.8 reduce-scatter.161.cloned.1.call-done
  1647.0 23.3 reduce-scatter.199.cloned.1.call-done
  1670.3 23.3 reduce-scatter.201.cloned.1.call-done
  1693.6 23.3 reduce-scatter.203.cloned.1.call-done
  1718.8 21.5 reduce-scatter.189.cloned.1.call-done
  1740.3 23.3 reduce-scatter.191.cloned.1.call-done
  1763.7 23.5 reduce-scatter.193.cloned.1.call-done
  1787.1 23.3 reduce-scatter.195.cloned.1.call-done
  1852.5 20.8 reduce-scatter.167.cloned.1.call-done
  1873.3 20.8 reduce-scatter.169.cloned.1.call-done
  1894.0 20.6 reduce-scatter.171.cloned.1.call-done
  1954.7 20.6 reduce-scatter.183.cloned.1.call-done
  1975.3 20.6 reduce-scatter.185.cloned.1.call-done
  1995.9 20.4 reduce-scatter.187.cloned.1.call-done
  2036.8 20.6 reduce-scatter.175.cloned.1.call-done
  2057.4 20.4 reduce-scatter.177.cloned.1.call-done
  2099.9 28.8 %reduce-scatter.163.cloned.1.call-done = bf16[256,640]{1,0:T(8,128)(2,1)} async-done(((bf16[1024,640]{1,0:T(8,128)(2,1)}), bf16[256,640]{1,0:T(8,128)(2,1)}) %reduce-scatter.163.cloned.1.call-update) | async-done | bytes 327696 | tf_op jit(solution)/shard_map/reduce_scatter | solution.py:321
  (1742 shorter events, 1730.5 us)
Async XLA Ops:
  1410.8 236.1 %reduce-scatter.197.cloned.1.call-start = ((), (), s32[]{:S(2)}) async-start(), calls=%async_computation.116 | async-start | bytes 819200 | tf_op jit(solution)/shard_map/reduce_scatter | solution.py:439
  1411.4 258.8 %reduce-scatter.199.cloned.1.call-start = ((), (), s32[]{:S(2)}) async-start(), calls=%async_computation.117 | async-start | bytes 819200 | tf_op jit(solution)/shard_map/reduce_scatter | solution.py:439
  1412.0 281.5 %reduce-scatter.201.cloned.1.call-start = ((), (), s32[]{:S(2)}) async-start(), calls=%async_computation.118 | async-start | bytes 819200 | tf_op jit(solution)/shard_map/reduce_scatter | solution.py:439
  1412.6 304.3 %reduce-scatter.203.cloned.1.call-start = ((), (), s32[]{:S(2)}) async-start(), calls=%async_computation.119 | async-start | bytes 819200 | tf_op jit(solution)/shard_map/reduce_scatter | solution.py:439
  1416.1 324.3 %reduce-scatter.189.cloned.1.call-start = ((), (), s32[]{:S(2)}) async-start(), calls=%async_computation.112 | async-start | bytes 819200 | tf_op jit(solution)/shard_map/reduce_scatter | solution.py:436
  1416.8 346.8 %reduce-scatter.191.cloned.1.call-start = ((), (), s32[]{:S(2)}) async-start(), calls=%async_computation.113 | async-start | bytes 819200 | tf_op jit(solution)/shard_map/reduce_scatter | solution.py:436
  1417.4 369.7 %reduce-scatter.193.cloned.1.call-start = ((), (), s32[]{:S(2)}) async-start(), calls=%async_computation.114 | async-start | bytes 819200 | tf_op jit(solution)/shard_map/reduce_scatter | solution.py:436
  1418.1 392.3 %reduce-scatter.195.cloned.1.call-start = ((), (), s32[]{:S(2)}) async-start(), calls=%async_computation.115 | async-start | bytes 819200 | tf_op jit(solution)/shard_map/reduce_scatter | solution.py:436
  1421.5 410.2 %reduce-scatter.235.cloned.1.call-start = ((), (), s32[]{:S(2)}) async-start(), calls=%async_computation.135 | async-start | bytes 409600
  1430.4 422.1 %reduce-scatter.165.cloned.1.call-start = ((), (), s32[]{:S(2)}) async-start(), calls=%async_computation.100 | async-start | bytes 409600 | tf_op jit(solution)/shard_map/reduce_scatter | solution.py:412
  1431.1 442.1 %reduce-scatter.167.cloned.1.call-start = ((), (), s32[]{:S(2)}) async-start(), calls=%async_computation.101 | async-start | bytes 409600 | tf_op jit(solution)/shard_map/reduce_scatter | solution.py:412
  1431.9 462.2 %reduce-scatter.169.cloned.1.call-start = ((), (), s32[]{:S(2)}) async-start(), calls=%async_computation.102 | async-start | bytes 409600 | tf_op jit(solution)/shard_map/reduce_scatter | solution.py:412
  1434.4 480.2 %reduce-scatter.171.cloned.1.call-start = ((), (), s32[]{:S(2)}) async-start(), calls=%async_computation.103 | async-start | bytes 409600 | tf_op jit(solution)/shard_map/reduce_scatter | solution.py:412
  1457.5 476.7 %reduce-scatter.227.cloned.1.call-start = ((), (), s32[]{:S(2)}) async-start(), calls=%async_computation.131 | async-start | bytes 81920
  1463.3 491.4 %reduce-scatter.181.cloned.1.call-start = ((), (), s32[]{:S(2)}) async-start(), calls=%async_computation.108 | async-start | bytes 409600 | tf_op jit(solution)/shard_map/reduce_scatter | solution.py:418
  1464.0 511.2 %reduce-scatter.183.cloned.1.call-start = ((), (), s32[]{:S(2)}) async-start(), calls=%async_computation.109 | async-start | bytes 409600 | tf_op jit(solution)/shard_map/reduce_scatter | solution.py:418
  1464.8 531.1 %reduce-scatter.185.cloned.1.call-start = ((), (), s32[]{:S(2)}) async-start(), calls=%async_computation.110 | async-start | bytes 409600 | tf_op jit(solution)/shard_map/reduce_scatter | solution.py:418
  1465.5 550.8 %reduce-scatter.187.cloned.1.call-start = ((), (), s32[]{:S(2)}) async-start(), calls=%async_computation.111 | async-start | bytes 409600 | tf_op jit(solution)/shard_map/reduce_scatter | solution.py:418
  1471.5 565.3 %reduce-scatter.173.cloned.1.call-start = ((), (), s32[]{:S(2)}) async-start(), calls=%async_computation.104 | async-start | bytes 409600 | tf_op jit(solution)/shard_map/reduce_scatter | solution.py:415
  1476.6 580.8 %reduce-scatter.175.cloned.1.call-start = ((), (), s32[]{:S(2)}) async-start(), calls=%async_computation.105 | async-start | bytes 409600 | tf_op jit(solution)/shard_map/reduce_scatter | solution.py:415
  1520.3 557.5 %reduce-scatter.177.cloned.1.call-start = ((), (), s32[]{:S(2)}) async-start(), calls=%async_computation.106 | async-start | bytes 409600 | tf_op jit(solution)/shard_map/reduce_scatter | solution.py:415
  1584.9 513.3 %reduce-scatter.179.cloned.1.call-start = ((), (), s32[]{:S(2)}) async-start(), calls=%async_computation.107 | async-start | bytes 409600 | tf_op jit(solution)/shard_map/reduce_scatter | solution.py:415
  1610.6 518.1 %reduce-scatter.163.cloned.1.call-start = ((), (), s32[]{:S(2)}) async-start(), calls=%async_computation.99 | async-start | bytes 1638400 | tf_op jit(solution)/shard_map/reduce_scatter | solution.py:321
  1626.7 542.1 %reduce-scatter.219.cloned.1.call-start = ((), (), s32[]{:S(2)}) async-start(), calls=%async_computation.127 | async-start | bytes 81920
  2159.5 245.3 %reduce-scatter.251.cloned.1.call-start = ((), (), s32[]{:S(2)}) async-start(), calls=%async_computation.143 | async-start | bytes 204800
  2160.4 264.0 %reduce-scatter.249.cloned.1.call-start = ((), (), s32[]{:S(2)}) async-start(), calls=%async_computation.142 | async-start | bytes 204800
  2161.3 282.9 %reduce-scatter.247.cloned.1.call-start = ((), (), s32[]{:S(2)}) async-start(), calls=%async_computation.141 | async-start | bytes 204800
  2162.2 301.7 %reduce-scatter.245.cloned.1.call-start = ((), (), s32[]{:S(2)}) async-start(), calls=%async_computation.140 | async-start | bytes 204800
  2163.1 320.6 %reduce-scatter.267.cloned.1.call-start = ((), (), s32[]{:S(2)}) async-start(), calls=%async_computation.151 | async-start | bytes 204800
  2164.0 339.4 %reduce-scatter.265.cloned.1.call-start = ((), (), s32[]{:S(2)}) async-start(), calls=%async_computation.150 | async-start | bytes 204800
  2164.9 358.1 %reduce-scatter.263.cloned.1.call-start = ((), (), s32[]{:S(2)}) async-start(), calls=%async_computation.149 | async-start | bytes 204800
  2165.8 376.8 %reduce-scatter.261.cloned.1.call-start = ((), (), s32[]{:S(2)}) async-start(), calls=%async_computation.148 | async-start | bytes 204800
  (479 other events, 13355.0 us)
Sparse Core Ops, SparseCore 0:
  112.7 38.2 reduce-scatter.132
  154.8 28.7 all-gather.18
  214.6 28.8 reduce-scatter.134
  246.8 28.7 all-gather.32
  277.9 28.7 all-gather.20
  310.2 29.2 reduce-scatter.148
  342.5 39.5 reduce-scatter.136
  387.4 28.7 all-gather.34
  418.0 28.7 all-gather.22
  449.9 52.7 all-reduce.86
  506.0 29.3 reduce-scatter.138
  538.3 29.3 reduce-scatter.150
  604.9 28.7 all-gather.36
  643.0 29.3 reduce-scatter.152
  675.2 39.5 reduce-scatter.140
  720.6 28.8 all-gather.38
  751.9 28.7 all-gather.26
  783.6 52.7 all-reduce.84
  839.4 29.3 reduce-scatter.142
  871.7 29.3 reduce-scatter.154
  907.8 28.7 all-gather.28
  938.3 28.7 all-gather.40
  976.4 29.3 reduce-scatter.156
  1008.6 39.5 reduce-scatter.144
  1054.0 28.7 all-gather.42
  1084.7 28.8 all-gather.30
  1116.6 52.7 all-reduce.82
  1172.1 29.3 reduce-scatter.158
  1204.4 29.3 reduce-scatter.146
  1241.1 28.7 all-gather.44
  1279.1 29.3 reduce-scatter.160
  1354.8 52.7 all-reduce.80
  (56 shorter events, 1074.4 us)
where the time goes:
time: 2570 us; the launch traced here: 2550 us
  waiting for transfers between devices  1580 us (61%)
  local copies, waits for them, and re-layouts  285 us (11%)
  other arithmetic  255 us (10%)
  matrix products  254 us (10%)
  blocking collectives  139 us (5%)
    unnamed x120, waiting for transfers between devices  508 us
    unnamed x934, local copies, waits for them, and re-layouts  153 us
    reduce_scatter x4, waiting for transfers between devices, layer_forward(): lax.psum_scatter(matmul(attended_values, output_matrix), 'tensor', scatte...  131 us
    reduce_scatter x4, waiting for transfers between devices, layer_forward(): lax.psum_scatter(matmul(product, down_matrix).astype(jnp.bfloat16), 'tens...  108 us
    reduce_scatter x4, waiting for transfers between devices, layer_backward(): lax.psum_scatter(times_transposed(grad_query_raw, query_matrix).astype(jn...  105 us
    reduce_scatter x4, waiting for transfers between devices, settle(): lax.psum_scatter(grad_gate[None].astype(jnp.bfloat16), 'fsdp', scatter_di...  91.6 us
    reduce_scatter x4, waiting for transfers between devices, settle(): lax.psum_scatter(grad_up[None].astype(jnp.bfloat16), 'fsdp', scatter_dime...  89 us
    dot_general x44, matrix products, matmul(): return jnp.dot(left, right, preferred_element_type=jnp.float32)  87.8 us
  transfers between devices with their start and end apart: 94, of which 80 were waited for; matrix products, arithmetic and copies ran while one was open for 25% of the time, Pallas kernels for 0%

commit v1 on v0

v1 whole, which is shorter than its diff:
```python
import jax
import jax.numpy as jnp
from jax import lax
from jax.sharding import PartitionSpec as P

WINDOW = 512
EPSILON = 1e-06
LOW = jnp.bfloat16
WIDE = jnp.float32


def flip(value, axis, bit):
    count = lax.axis_size(axis)
    return lax.ppermute(value, axis, [(i, i ^ bit) for i in range(count)])


def ring(value, axis):
    count = lax.axis_size(axis)
    return lax.ppermute(value, axis, [(i, (i + 1) % count) for i in range(count)])


def shifted(value, axis, by):
    count = lax.axis_size(axis)
    pairs = [(i, i + by) for i in range(count) if 0 <= i + by < count]
    return lax.ppermute(value, axis, pairs)


def add(*parts):
    total = parts[0].astype(WIDE)
    for part in parts[1:]:
        total = total + part.astype(WIDE)
    return total


def dot(left, right):
    return jnp.dot(left, right, preferred_element_type=WIDE)


def dot_nt(left, right):
    return lax.dot_general(left, right, (((1,), (1,)), ((), ())), preferred_element_type=WIDE)


def dot_tn(left, right):
    return lax.dot_general(left, right, (((0,), (0,)), ((), ())), preferred_element_type=WIDE)


def gather_slabs(slab):
    ranks = lax.axis_size("fsdp")
    section = lax.axis_index("section")
    data = lax.axis_index("fsdp")
    head = lax.axis_index("tensor")
    rows, columns = slab.shape
    half = rows // 2
    current = slab
    if ranks > 4:
        current = lax.all_gather(slab, "fsdp", axis=0, tiled=True)
        data, ranks, rows, half = 0, 1, rows * ranks, rows * ranks // 2
    whole = jnp.zeros((2, 4, ranks, rows, columns), slab.dtype)
    for step in range(ranks):
        chunk = current
        place = (data - step) % ranks
        if step < ranks - 1:
            current = ring(current, "fsdp")
        near = flip(chunk, "tensor", 1)
        far = flip(chunk, "tensor", 2)
        across = jnp.concatenate([flip(far[:half], "tensor", 1), flip(near[half:], "tensor", 2)])
        for piece, bit in ((chunk, 0), (near, 1), (far, 2), (across, 3)):
            other = flip(piece, "section", 1)
            whole = lax.dynamic_update_slice(
                whole, piece[None, None, None], (section, head ^ bit, place, 0, 0)
            )
            whole = lax.dynamic_update_slice(
                whole, other[None, None, None], (1 - section, head ^ bit, place, 0, 0)
            )
    return whole


def scatter_slabs(whole):
    ranks = lax.axis_size("fsdp")
    section = lax.axis_index("section")
    data = lax.axis_index("fsdp")
    head = lax.axis_index("tensor")
    rows, columns = whole.shape[3:]
    spread = ranks > 4
    if spread:
        data, ranks, rows = 0, 1, rows * ranks
        whole = whole.reshape(2, 4, 1, rows, columns)
    half = rows // 2
    arriving = None
    total = None
    for step in range(ranks):
        place = (data - 1 - step) % ranks

        def piece(bit):
            own = lax.dynamic_slice(
                whole, (section, head ^ bit, place, 0, 0), (1, 1, 1, rows, columns)
            )[0, 0, 0]
            other = lax.dynamic_slice(
                whole, (1 - section, head ^ bit, place, 0, 0), (1, 1, 1, rows, columns)
            )[0, 0, 0]
            return add(own, flip(other, "section", 1)).astype(LOW)

        across = piece(3)
        upper = flip(across[:half], "tensor", 1)
        lower = flip(across[half:], "tensor", 2)
        near = piece(1)
        far = piece(2)
        far = jnp.concatenate([add(far[:half], upper).astype(LOW), far[half:]])
        near = jnp.concatenate([near[:half], add(near[half:], lower).astype(LOW)])
        total = add(piece(0), flip(near, "tensor", 1), flip(far, "tensor", 2))
        if arriving is not None:
            total = total + arriving.astype(WIDE)
        if step < ranks - 1:
            arriving = ring(total.astype(LOW), "fsdp")
    if spread:
        total = lax.psum_scatter(total.astype(LOW), "fsdp", scatter_dimension=0, tiled=True)
    return total.astype(WIDE)


def norm_rows(value_rows, gain_value):
    return (
        value_rows
        * lax.rsqrt(jnp.mean(value_rows * value_rows, axis=-1, keepdims=True) + EPSILON)
        * gain_value
    )


def norm_back(value_rows, gain_value, cotangent):
    scale = lax.rsqrt(jnp.mean(value_rows * value_rows, axis=-1, keepdims=True) + EPSILON)
    unit = value_rows * scale
    weighted = cotangent * gain_value
    rows_grad = scale * (weighted - unit * jnp.mean(weighted * unit, axis=-1, keepdims=True))
    gain_grad = jnp.sum(cotangent * unit, axis=0)
    return rows_grad, gain_grad


def turns(token_positions, head_width):
    half_depth = head_width // 2
    frequency = 10000.0 ** (-(jnp.arange(half_depth, dtype=WIDE) * 2.0) / head_width)
    turn = token_positions.astype(WIDE)[:, None] * frequency
    return jnp.cos(turn), jnp.sin(turn)


def rotate(value_rows, cosine, sine):
    half_depth = value_rows.shape[-1] // 2
    first = value_rows[..., :half_depth]
    second = value_rows[..., half_depth:]
    return jnp.concatenate(
        [first * cosine - second * sine, second * cosine + first * sine], axis=-1
    )


def gelu_parts(gate):
    root = (2.0 / jnp.pi) ** 0.5
    tanh = jnp.tanh(root * (gate + 0.044715 * gate * gate * gate))
    value = 0.5 * gate * (1.0 + tanh)
    slope = 0.5 * (1.0 + tanh) + 0.5 * gate * (1.0 - tanh * tanh) * root * (
        1.0 + 3.0 * 0.044715 * gate * gate
    )
    return value, slope


def keys_of(normed, layer, cosine, sine):
    key_raw = dot(normed, layer["key"])
    key_rows = rotate(norm_rows(key_raw, layer["key_gain"]), cosine, sine).astype(LOW)
    value_rows = dot(normed, layer["value"]).astype(LOW)
    return key_raw, key_rows, value_rows


def layer_forward(x, earlier, layer, allowed, window_turns):
    rows = x.shape[0]
    head_width = layer["key"].shape[1]
    heads = len(layer["query"])
    scale = head_width ** (-0.5)
    window_cos, window_sin = window_turns
    cosine, sine = window_cos[-rows:], window_sin[-rows:]
    normed = norm_rows(x, layer["before_gain"]).astype(LOW)
    if earlier is not None:
        everyone = jnp.concatenate(
            [norm_rows(earlier.astype(WIDE), layer["before_gain"]).astype(LOW), normed]
        )
        key_raw, key_rows, value_rows = keys_of(everyone, layer, window_cos, window_sin)
        key_raw = key_raw[-rows:]
    else:
        key_raw, own_keys, own_values = keys_of(normed, layer, cosine, sine)
        pair = jnp.concatenate([own_keys, own_values], axis=1)
        back = window_cos.shape[0] // rows - 1
        pair = jnp.concatenate([shifted(pair, "tensor", by) for by in range(back, 0, -1)] + [pair])
        key_rows, value_rows = pair[:, :head_width], pair[:, head_width:]
    query_raw, queries, chances, attended = [], [], [], []
    attention_sum = 0.0
    for head in range(heads):
        raw = dot(normed, layer["query"][head])
        query = rotate(norm_rows(raw, layer["query_gain"]), cosine, sine).astype(LOW)
        scores = jnp.where(allowed, dot_nt(query, key_rows) * scale, -1e30)
        exponent = jnp.exp(scores - jnp.max(scores, axis=-1, keepdims=True))
        chance = exponent / jnp.sum(exponent, axis=-1, keepdims=True)
        mixed = dot(chance.astype(LOW), value_rows).astype(LOW)
        attention_sum = attention_sum + dot_nt(mixed, layer["output"][head])
        query_raw.append(raw)
        queries.append(query)
        chances.append(chance)
        attended.append(mixed)
    hidden = x + norm_rows(attention_sum, layer["after_gain"])
    feed_in = norm_rows(hidden, layer["feed_gain"]).astype(LOW)
    gates, ups, products = [], [], []
    branch = 0.0
    for part in range(len(layer["gate"])):
        gate = dot(feed_in, layer["gate"][part])
        up = dot(feed_in, layer["up"][part])
        product = (gelu_parts(gate)[0] * up).astype(LOW)
        branch = branch + dot_nt(product, layer["down"][part])
        gates.append(gate)
        ups.append(up)
        products.append(product)
    result = hidden + norm_rows(branch, layer["final_gain"])
    kept = (
        x, normed, key_raw, key_rows, value_rows, query_raw, queries, chances, attended,
        attention_sum, hidden, feed_in, gates, ups, products, branch,
    )
    return result, kept


def layer_backward(dy, kept, layer, window_turns):
    (
        x, normed, key_raw, key_rows, value_rows, query_raw, queries, chances, attended,
        attention_sum, hidden, feed_in, gates, ups, products, branch,
    ) = kept
    rows = x.shape[0]
    head_width = layer["key"].shape[1]
    heads = len(layer["query"])
    scale = head_width ** (-0.5)
    window_cos, window_sin = window_turns
    cosine, sine = window_cos[-rows:], window_sin[-rows:]
    back = window_cos.shape[0] // rows - 1
    grads = {}
    d_branch, grads["final_gain"] = norm_back(branch, layer["final_gain"], dy)
    d_branch = d_branch.astype(LOW)
    d_feed = 0.0
    grads["gate"], grads["up"], grads["down"] = [], [], []
    for part in range(len(gates)):
        d_product = dot(d_branch, layer["down"][part])
        value, slope = gelu_parts(gates[part])
        d_gate = (d_product * ups[part] * slope).astype(LOW)
        d_up = (d_product * value).astype(LOW)
        d_feed = d_feed + dot_nt(d_gate, layer["gate"][part]) + dot_nt(d_up, layer["up"][part])
        grads["down"].append(dot_tn(d_branch, products[part]).astype(LOW))
        grads["gate"].append(dot_tn(feed_in, d_gate).astype(LOW))
        grads["up"].append(dot_tn(feed_in, d_up).astype(LOW))
    part_hidden, grads["feed_gain"] = norm_back(hidden, layer["feed_gain"], d_feed)
    d_hidden = dy + part_hidden
    d_sum, grads["after_gain"] = norm_back(attention_sum, layer["after_gain"], d_hidden)
    d_sum = d_sum.astype(LOW)
    d_keys, d_values = 0.0, 0.0
    d_normed = 0.0
    query_gain = 0.0
    grads["query"], grads["output"] = [], []
    for head in range(heads):
        d_mixed = dot(d_sum, layer["output"][head]).astype(LOW)
        grads["output"].append(dot_tn(d_sum, attended[head]).astype(LOW))
        chance = chances[head]
        d_chance = dot_nt(d_mixed, value_rows)
        weighted = jnp.sum(chance * d_chance, axis=-1, keepdims=True)
        d_scores = (chance * (d_chance - weighted)).astype(LOW)
        d_values = d_values + dot_tn(chance.astype(LOW), d_mixed)
        d_keys = d_keys + dot_tn(d_scores, queries[head]) * scale
        d_query = rotate(dot(d_scores, key_rows) * scale, cosine, -sine)
        d_raw, gain_part = norm_back(query_raw[head], layer["query_gain"], d_query)
        d_raw = d_raw.astype(LOW)
        query_gain = query_gain + gain_part
        grads["query"].append(dot_tn(normed, d_raw).astype(LOW))
        d_normed = d_normed + dot_nt(d_raw, layer["query"][head])
    grads["query_gain"] = query_gain
    pair = jnp.concatenate([d_keys, d_values], axis=1)
    own = pair[-rows:]
    for by in range(1, back + 1):
        first = (back - by) * rows
        own = own + shifted(pair[first : first + rows].astype(LOW), "tensor", -by).astype(WIDE)
    d_keys, d_values = own[:, :head_width], own[:, head_width:].astype(LOW)
    d_keys, grads["key_gain"] = norm_back(
        key_raw, layer["key_gain"], rotate(d_keys, cosine, -sine)
    )
    d_keys = d_keys.astype(LOW)
    grads["key"] = dot_tn(normed, d_keys).astype(LOW)
    grads["value"] = dot_tn(normed, d_values).astype(LOW)
    d_normed = d_normed + dot_nt(d_keys, layer["key"]) + dot_nt(d_values, layer["value"])
    part_inputs, grads["before_gain"] = norm_back(x, layer["before_gain"], d_normed)
    return d_hidden + part_inputs, grads


GAINS = ("before_gain", "query_gain", "key_gain", "after_gain", "feed_gain", "final_gain")


def body(
    inputs,
    out_grad,
    segment_ids,
    positions,
    before_gain,
    query_matrix,
    key_matrix,
    value_matrix,
    query_gain,
    key_gain,
    output_matrix,
    after_gain,
    feed_gain,
    gate_matrix,
    up_matrix,
    down_matrix,
    final_gain,
):
    section = lax.axis_index("section")
    data = lax.axis_index("fsdp")
    head = lax.axis_index("tensor")
    ranks = lax.axis_size("fsdp")
    heads = lax.axis_size("tensor")
    rows, width = inputs.shape[1:]
    head_width = key_matrix.shape[2]
    depth = gate_matrix.shape[1]
    piece_width = head_width // heads
    hidden_width = gate_matrix.shape[2]
    back = min(-(-(WINDOW - 1) // rows), heads - 1)

    own_key = lax.dynamic_slice_in_dim(key_matrix[0], head * piece_width, piece_width, 1)
    own_value = lax.dynamic_slice_in_dim(value_matrix[0], head * piece_width, piece_width, 1)
    slab = jnp.concatenate(
        [
            query_matrix[0],
            gate_matrix[0],
            up_matrix[0],
            down_matrix[0].T,
            output_matrix[0].T,
            own_key,
            own_value,
        ],
        axis=1,
    )
    widths = (
        head_width, hidden_width, hidden_width, hidden_width, head_width, piece_width, piece_width,
    )
    starts = [0]
    for step in widths:
        starts.append(starts[-1] + step)

    gain_list = (before_gain, query_gain, key_gain, after_gain, feed_gain, final_gain)
    gain_flat = jnp.concatenate([gain[0] for gain in gain_list])
    gain_all = lax.all_gather(gain_flat, ("section", "fsdp"), axis=0, tiled=False)
    gain_all = gain_all.reshape(2, ranks, -1).astype(WIDE)

    first_input = lax.dynamic_index_in_dim(inputs, section, 0, keepdims=False)
    last_cot = lax.dynamic_index_in_dim(out_grad, section, 0, keepdims=False)
    segments = lax.dynamic_index_in_dim(segment_ids, section, 0, keepdims=False)
    token_positions = lax.dynamic_index_in_dim(positions, section, 0, keepdims=False)
    earlier = jnp.concatenate([shifted(first_input, "tensor", by) for by in range(back, 0, -1)])
    padded_segments = jnp.concatenate([jnp.full((back * rows,), -1, jnp.int32), segments])
    padded_positions = jnp.concatenate([jnp.zeros((back * rows,), jnp.int32), token_positions])
    key_segments = lax.dynamic_slice_in_dim(padded_segments, head * rows, (back + 1) * rows)
    key_positions = lax.dynamic_slice_in_dim(padded_positions, head * rows, (back + 1) * rows)
    gap = key_positions[-rows:, None] - key_positions[None, :]
    allowed = (
        (key_segments[-rows:, None] == key_segments[None, :]) & (gap >= 0) & (gap < WINDOW)
    )
    window_turns = turns(key_positions, head_width)

    whole = gather_slabs(slab)
    layers = []
    for index in range(2):
        parts = [whole[index, t].reshape(ranks * depth, slab.shape[1]) for t in range(heads)]
        cut = [[part[:, a:b] for a, b in zip(starts[:-1], starts[1:])] for part in parts]
        layer = {
            "query": [c[0] for c in cut],
            "gate": [c[1] for c in cut],
            "up": [c[2] for c in cut],
            "down": [c[3] for c in cut],
            "output": [c[4] for c in cut],
            "key": jnp.concatenate([c[5] for c in cut], axis=1),
            "value": jnp.concatenate([c[6] for c in cut], axis=1),
        }
        first = 0
        for name, gain in zip(GAINS, gain_list):
            size = gain.shape[1]
            layer[name] = gain_all[index, :, first : first + size].reshape(-1)
            first += size
        layers.append(layer)

    out_first, kept_first = layer_forward(
        first_input.astype(WIDE), earlier, layers[0], allowed, window_turns
    )
    out_first = out_first.astype(LOW)
    out_second, kept_second = layer_forward(
        out_first.astype(WIDE), None, layers[1], allowed, window_turns
    )
    out_second = out_second.astype(LOW)
    grad_second, grads_second = layer_backward(
        last_cot.astype(WIDE), kept_second, layers[1], window_turns
    )
    grad_first, grads_first = layer_backward(
        grad_second.astype(LOW).astype(WIDE), kept_first, layers[0], window_turns
    )

    def settle(first, second):
        own = jnp.where(section == 0, first, second)
        sent = jnp.where(section == 0, second, first)
        other = flip(sent, "section", 1)
        return jnp.where(
            section == 0, jnp.stack([own, other]), jnp.stack([other, own])
        )[None]

    layer_out = settle(out_first, out_second)
    input_grad = settle(grad_first, grad_second)

    both = []
    gain_sums = []
    for grads in (grads_first, grads_second):
        per_head = []
        for t in range(heads):
            columns = slice(t * piece_width, (t + 1) * piece_width)
            per_head.append(
                jnp.concatenate(
                    [
                        grads["query"][t],
                        grads["gate"][t],
                        grads["up"][t],
                        grads["down"][t],
                        grads["output"][t],
                        grads["key"][:, columns],
                        grads["value"][:, columns],
                    ],
                    axis=1,
                ).reshape(ranks, depth, -1)
            )
        both.append(jnp.stack(per_head))
        gain_sums.append(
            jnp.concatenate([grads[name].reshape(ranks, -1) for name in GAINS], axis=1)
        )
    gain_sum = lax.psum(jnp.stack(gain_sums), ("section", "fsdp", "tensor"))
    gain_own = lax.dynamic_slice(gain_sum, (section, data, 0), (1, 1, gain_sum.shape[2]))[0]
    gain_grads = {}
    first = 0
    for name, gain in zip(GAINS, gain_list):
        size = gain.shape[1]
        gain_grads[name] = gain_own[:, first : first + size]
        first += size

    own = scatter_slabs(jnp.stack(both))
    cut = [own[:, a:b] for a, b in zip(starts[:-1], starts[1:])]
    pair = jnp.concatenate(cut[5:], axis=1).astype(LOW)
    shared = jnp.zeros((heads,) + pair.shape, LOW)
    for bit in range(heads):
        piece = pair if bit == 0 else flip(pair, "tensor", bit)
        shared = lax.dynamic_update_slice(shared, piece[None], (head ^ bit, 0, 0))
    shared = shared.astype(WIDE)
    key_grad = jnp.concatenate([shared[t, :, :piece_width] for t in range(heads)], axis=1)
    value_grad = jnp.concatenate([shared[t, :, piece_width:] for t in range(heads)], axis=1)
    return (
        layer_out,
        input_grad,
        gain_grads["before_gain"],
        cut[0][None],
        key_grad[None],
        value_grad[None],
        gain_grads["query_gain"],
        gain_grads["key_gain"],
        cut[4].T[None],
        gain_grads["after_gain"],
        gain_grads["feed_gain"],
        cut[1][None],
        cut[2][None],
        cut[3].T[None],
        gain_grads["final_gain"],
    )


def solution(mesh):
    in_specs = (
        P(None, ("fsdp", "tensor"), None),
        P(None, ("fsdp", "tensor"), None),
        P(None, "fsdp"),
        P(None, "fsdp"),
        P("section", "fsdp"),
        P("section", "fsdp", "tensor"),
        P("section", "fsdp", None),
        P("section", "fsdp", None),
        P("section", "fsdp"),
        P("section", "fsdp"),
        P("section", "tensor", "fsdp"),
        P("section", "fsdp"),
        P("section", "fsdp"),
        P("section", "fsdp", "tensor"),
        P("section", "fsdp", "tensor"),
        P("section", "tensor", "fsdp"),
        P("section", "fsdp"),
    )
    out_specs = (
        P("section", None, ("fsdp", "tensor"), None),
        P("section", None, ("fsdp", "tensor"), None),
        P("section", "fsdp"),
        P("section", "fsdp", "tensor"),
        P("section", "fsdp", None),
        P("section", "fsdp", None),
        P("section", "fsdp"),
        P("section", "fsdp"),
        P("section", "tensor", "fsdp"),
        P("section", "fsdp"),
        P("section", "fsdp"),
        P("section", "fsdp", "tensor"),
        P("section", "fsdp", "tensor"),
        P("section", "tensor", "fsdp"),
        P("section", "fsdp"),
    )
    return jax.shard_map(body, mesh=mesh, in_specs=in_specs, out_specs=out_specs, check_vma=False)
```

time: 2570 us -> 701 us (0.27)
  waiting for transfers between devices: 1580 us -> 186 us
  other arithmetic: 255 us -> 86.5 us
  local copies, waits for them, and re-layouts: 285 us -> 132 us
  matrix products: 254 us -> 140 us
  blocking collectives: 139 us -> 69 us
  starting transfers between devices: 19 us -> 65.1 us
    reduce_scatter x36 -> x0, waiting for transfers between devices: 790 us -> none  [the longest x4 131 us: layer_forward(): lax.psum_scatter(matmul(attended_values, output_matrix), 'tensor', scatte...]
    unnamed x120 -> x0, waiting for transfers between devices: 508 us -> none
    all_gather x16 -> x0, waiting for transfers between devices: 207 us -> none  [the longest x4 58.8 us: layer_backward(): lax.all_gather(grad_branch.astype(jnp.bfloat16), 'tensor', axis=0, tiled=...]
    ppermute x0 -> x75, waiting for transfers between devices: none -> 178 us  [the longest x69 137 us: flip(): return lax.ppermute(value, axis, [(i, i ^ bit) for i in range(count)])]
    unnamed x934 -> x609, local copies, waits for them, and re-layouts: 153 us -> 17.3 us
    dot_general x128 -> x176, matrix products: 254 us -> 140 us  [the longest x60 54.1 us: dot_tn(): lax.dot_general(left, right, (((0,), (0,)), ((), ())), preferred_element_...]
    all_gather x7 -> x1, blocking collectives: 108 us -> 23.9 us  [body(): lax.all_gather(gain_flat, ('section', 'fsdp'), axis=0, tiled=False)]
    dynamic_update_slice x46 -> x0, other arithmetic: 70.2 us -> none  [the longest x38 54.8 us: body(): lax.dynamic_update_index_in_dim(buffer, jnp.where(forward_valid, piece_st...]
  transfers between devices with their start and end apart: 94 -> 83, of which waited for: 80 -> 30; matrix products, arithmetic and copies ran while one was open for 25% -> 26% of each run, Pallas kernels for 0% -> 0%
where the time goes in v1:
time: 701 us; the launch traced here: 694 us
  waiting for transfers between devices  186 us (27%)
  matrix products  140 us (20%)
  local copies, waits for them, and re-layouts  132 us (19%)
  other arithmetic  86.5 us (12%)
  blocking collectives  69 us (10%)
  starting transfers between devices  65.1 us (9%)
  Pallas kernels  10.2 us (1%)
    ppermute x69, waiting for transfers between devices, flip(): return lax.ppermute(value, axis, [(i, i ^ bit) for i in range(count)])  137 us
    dot_general x60, matrix products, dot_tn(): lax.dot_general(left, right, (((0,), (0,)), ((), ())), preferred_element_...  54.1 us
    dot_general x60, matrix products, dot_nt(): lax.dot_general(left, right, (((1,), (1,)), ((), ())), preferred_element_...  46 us
    psum x1, blocking collectives, body(): gain_sum = lax.psum(jnp.stack(gain_sums), ('section', 'fsdp', 'tensor'))  45 us
    concatenate x10, local copies, waits for them, and re-layouts, body(): jnp.concatenate([grads['query'][t], grads['gate'][t], grads['up'][t], gra...  44.8 us
    ppermute x69, starting transfers between devices, flip(): return lax.ppermute(value, axis, [(i, i ^ bit) for i in range(count)])  43.3 us
    ppermute x6, waiting for transfers between devices, ring(): lax.ppermute(value, axis, [(i, (i + 1) % count) for i in range(count)])  40.4 us
    dot_general x56, matrix products, dot(): return jnp.dot(left, right, preferred_element_type=WIDE)  39.4 us
  transfers between devices with their start and end apart: 83, of which 30 were waited for; matrix products, arithmetic and copies ran while one was open for 26% of the time, Pallas kernels for 0%

profile of v1, /device:TPU:0, one launch (start us, length us, event | category | flops | bytes accessed | tf_op | source)
XLA Modules:
  0.0 694.1 jit_solution(10805845732327058781)
XLA Ops:
  17.3 23.9 %all-gather.1 = bf16[8,1,768]{2,1,0:T(2,128)(2,1)S(1)} all-gather(bf16[1,1,768]{2,1,0:T(2,128)(2,1)S(1)} %reshape.544), channel_id=2, replica_groups=mesh['section'=2,'fsdp'=4,'tensor'=4] {'section','fsdp'}, dimensions={0}, use_global_device_ids=true | all-gather | bytes 13824 | tf_op jit(solution)/shard_map/all_gather | solution.py:348
  45.7 7.7 %broadcast_in_dim.101 = bf16[2,4,4,160,2176]{4,3,2,1,0:T(8,128)(2,1)} broadcast(bf16[]{:T(256)} %constant.154.clone.1), dimensions={} | broadcast | bytes 22282242 | tf_op jit(solution)/shard_map/broadcast_in_dim | solution.py:58
  58.7 15.8 %collective-permute-done.8 = bf16[160,2176]{1,0:T(8,128)(2,1)S(1)} collective-permute-done((bf16[160,2176]{1,0:T(8,128)(2,1)S(1)}, bf16[160,2176]{1,0:T(8,128)(2,1)S(1)}, u32[]{:S(2)}, u32[]{:S(2)}) %collective-permute-start.8) | collective-permute-done | bytes 696352 | tf_op jit(solution)/shard_map/ppermute | solution.py:19
  77.8 17.0 %collective-permute-done.12 = bf16[160,2176]{1,0:T(8,128)(2,1)S(1)} collective-permute-done((bf16[160,2176]{1,0:T(8,128)(2,1)S(1)}, bf16[160,2176]{1,0:T(8,128)(2,1)S(1)}, u32[]{:S(2)}, u32[]{:S(2)}) %collective-permute-start.12) | collective-permute-done | bytes 696352 | tf_op jit(solution)/shard_map/ppermute | solution.py:14
  103.1 9.8 %collective-permute-done.17 = bf16[160,2176]{1,0:T(8,128)(2,1)S(1)} collective-permute-done((bf16[160,2176]{1,0:T(8,128)(2,1)S(1)}, bf16[160,2176]{1,0:T(8,128)(2,1)S(1)}, u32[]{:S(2)}, u32[]{:S(2)}) %collective-permute-start.17) | collective-permute-done | bytes 696352 | tf_op jit(solution)/shard_map/ppermute | solution.py:19
  117.1 16.1 %collective-permute-done.21 = bf16[160,2176]{1,0:T(8,128)(2,1)S(1)} collective-permute-done((bf16[160,2176]{1,0:T(8,128)(2,1)S(1)}, bf16[160,2176]{1,0:T(8,128)(2,1)S(1)}, u32[]{:S(2)}, u32[]{:S(2)}) %collective-permute-start.21) | collective-permute-done | bytes 696352 | tf_op jit(solution)/shard_map/ppermute | solution.py:14
  138.2 7.6 %collective-permute-done.23 = bf16[80,2176]{1,0:T(8,128)(2,1)S(1)} collective-permute-done((bf16[80,2176]{1,0:T(8,128)(2,1)S(1)}, bf16[80,2176]{1,0:T(8,128)(2,1)S(1)}, u32[]{:S(2)}, u32[]{:S(2)}) %collective-permute-start.23) | collective-permute-done | bytes 348192 | tf_op jit(solution)/shard_map/ppermute | solution.py:14
  145.8 6.2 collective-permute-done.26
  157.3 14.8 %collective-permute-done.30 = bf16[160,2176]{1,0:T(8,128)(2,1)S(1)} collective-permute-done((bf16[160,2176]{1,0:T(8,128)(2,1)S(1)}, bf16[160,2176]{1,0:T(8,128)(2,1)S(1)}, u32[]{:S(2)}, u32[]{:S(2)}) %collective-permute-start.30) | collective-permute-done | bytes 696352 | tf_op jit(solution)/shard_map/ppermute | solution.py:14
  182.7 5.3 collective-permute-done.33
  196.5 12.8 %fusion.445 = (bf16[1,1,4,160,2176]{4,3,2,1,0:T(8,128)(2,1)}, bf16[1,1,4,160,2176]{4,3,2,1,0:T(8,128)(2,1)}, bf16[1,1,4,160,2176]{4,3,2,1,0:T(8,128)(2,1)}, bf16...) fusion(bf16[2,4,4,160,2176]{4,3,2,1,0:T(8,128)(2,1)} %bitcast_d, ...), kind=kLoop, calls=%fused_computation.1006 | loop fusion | bytes 44564480 | tf_op jit(solution)/shard_map/slice | solution.py:369
  267.4 9.7 %convolution_convert_fusion.56 = bf16[256,256]{0,1:T(8,128)(2,1)S(1)} fusion(bf16[640,64]{1,0:T(8,128)(2,1)S(1)} %get-tuple-element.113, bf16[640,64]{1,0:T(8,128)(2,1)S(1)} %get-tuple-element.111, bf16[640,64]{1,0:T(8,128)(2,1)S(1)} %get-tuple-element.109, bf16[640,64]{1,0:T(8,128)(2,1)S(1)} %get-tuple-element.107, ...), kind=kOutput, calls=%fused_computation.286 | convolution fusion | flops 85917696 | bytes 790016 | tf_op jit(solution)/shard_map/dot_general | solution.py:36
  286.9 4.4 collective-permute-done.37
  395.3 5.7 copy.52
  401.1 5.3 copy.53
  406.4 5.3 copy.54
  411.8 5.4 copy.55
  417.2 10.5 %maximum_bitcast_fusion.1 = bf16[1,4,4,160,2176]{4,3,2,1,0:T(8,128)(2,1)} fusion(bf16[1,4,160,2176]{3,2,1,0:T(8,128)(2,1)} %bitcast.529, bf16[1,4,160,2176]{3,2,1,0:T(8,128)(2,1)} %bitcast.527, bf16[1,4,160,2176]{3,2,1,0:T(8,128)(2,1)} %bitcast.525, bf16[1,4,160,2176]{3,2,1,0:T(8,128)(2,1)} %bitcast.523), kind=kLoop, calls=%fused_computation.65 | loop fusion | flops 16711680 | bytes 22282240 | tf_op jit(solution)/shard_map/stack | solution.py:446
  460.6 5.3 copy.48
  465.9 5.3 copy.49
  471.2 5.3 copy.50
  476.6 5.5 copy.51
  482.1 7.4 %maximum_bitcast_fusion = bf16[1,4,4,160,2176]{4,3,2,1,0:T(8,128)(2,1)S(1)} fusion(bf16[1,4,160,2176]{3,2,1,0:T(8,128)(2,1)} %bitcast.530, bf16[1,4,160,2176]{3,2,1,0:T(8,128)(2,1)} %bitcast.528, bf16[1,4,160,2176]{3,2,1,0:T(8,128)(2,1)} %bitcast.526, bf16[1,4,160,2176]{3,2,1,0:T(8,128)(2,1)} %bitcast.524), kind=kLoop, calls=%fused_computation.64 | loop fusion | flops 16711680 | bytes 22282240 | tf_op jit(solution)/shard_map/stack | solution.py:446
  507.6 45.0 %psum.7 = f32[2,4,768]{2,1,0:T(4,128)S(1)} all-reduce(f32[2,4,768]{2,1,0:T(4,128)S(1)} %pad_maximum_fusion.54), channel_id=1, replica_groups=mesh['section'=2,'fsdp'=4,'tensor'=4] {'section','fsdp','tensor'}, use_global_device_ids=true, to_apply=%region_80.81 | all-reduce | flops 6144 | bytes 49152 | tf_op jit(solution)/shard_map/psum | solution.py:437
  574.1 5.7 collective-permute-done.64
  581.6 8.0 %collective-permute-done.72 = bf16[80,2176]{1,0:T(8,128)(2,1)S(1)} collective-permute-done((bf16[80,2176]{1,0:T(8,128)(2,1)S(1)}, bf16[80,2176]{1,0:T(8,128)(2,1)S(1)}, u32[]{:S(2)}, u32[]{:S(2)}) %collective-permute-start.72) | collective-permute-done | bytes 348192 | tf_op jit(solution)/shard_map/ppermute | solution.py:14
  591.3 7.3 %collective-permute-done.75 = bf16[80,2176]{1,0:T(8,128)(2,1)S(1)} collective-permute-done((bf16[80,2176]{1,0:T(8,128)(2,1)S(1)}, bf16[80,2176]{1,0:T(8,128)(2,1)S(1)}, u32[]{:S(2)}, u32[]{:S(2)}) %collective-permute-start.75) | collective-permute-done | bytes 348192 | tf_op jit(solution)/shard_map/ppermute | solution.py:14
  601.4 12.8 %collective-permute-done.73 = bf16[160,2176]{1,0:T(8,128)(2,1)S(1)} collective-permute-done((bf16[160,2176]{1,0:T(8,128)(2,1)S(1)}, bf16[160,2176]{1,0:T(8,128)(2,1)S(1)}, u32[]{:S(2)}, u32[]{:S(2)}) %collective-permute-start.73) | collective-permute-done | bytes 696352 | tf_op jit(solution)/shard_map/ppermute | solution.py:14
  619.6 5.7 collective-permute-done.48
  630.6 7.1 %collective-permute-done.68 = bf16[160,2176]{1,0:T(8,128)(2,1)S(1)} collective-permute-done((bf16[160,2176]{1,0:T(8,128)(2,1)S(1)}, bf16[160,2176]{1,0:T(8,128)(2,1)S(1)}, u32[]{:S(2)}, u32[]{:S(2)}) %collective-permute-start.68) | collective-permute-done | bytes 696352 | tf_op jit(solution)/shard_map/ppermute | solution.py:14
  660.9 9.1 %collective-permute-done.57 = bf16[160,2176]{1,0:T(8,128)(2,1)S(1)} collective-permute-done((bf16[160,2176]{1,0:T(8,128)(2,1)S(1)}, bf16[160,2176]{1,0:T(8,128)(2,1)S(1)}, u32[]{:S(2)}, u32[]{:S(2)}) %collective-permute-start.57) | collective-permute-done | bytes 696352 | tf_op jit(solution)/shard_map/ppermute | solution.py:14
  674.8 6.0 collective-permute-done.49
  (1203 shorter events, 369.1 us)
Async XLA Ops:
  2.8 55.3 %collective-permute-start = (bf16[160,2176]{1,0:T(8,128)(2,1)S(1)}, bf16[160,2176]{1,0:T(8,128)(2,1)}, u32[]{:S(2)}, u32[]{:S(2)}) collective-permute-start(bf16[160,2176]{1,0:T(8,128)(2,1)S(1)} %concatenate.217), channel_id=1, source_target_pairs={{0,16},{16,0},{1,17},{17,1},{2,18},{18,2},{3,19},{19,3},{4,20},{20... | collective-permute-start | bytes 2088968 | tf_op jit(solution)/shard_map/ppermute | solution.py:14
  3.4 54.6 %collective-permute-start.1 = (bf16[160,2176]{1,0:T(8,128)(2,1)S(1)}, bf16[160,2176]{1,0:T(8,128)(2,1)S(1)}, u32[]{:S(2)}, u32[]{:S(2)}) collective-permute-start(bf16[160,2176]{1,0:T(8,128)(2,1)S(1)} %concatenate.217), channel_id=1, source_target_pairs={{0,1},{1,0},{2,3},{3,2},{4,5},{5,4},{6,7},{7,6},{8,9},{9,8},{10,11... | collective-permute-start | bytes 2088968 | tf_op jit(solution)/shard_map/ppermute | solution.py:14
  5.9 51.7 %collective-permute-start.3 = (bf16[160,2176]{1,0:T(8,128)(2,1)S(1)}, bf16[160,2176]{1,0:T(8,128)(2,1)S(1)}, u32[]{:S(2)}, u32[]{:S(2)}) collective-permute-start(bf16[160,2176]{1,0:T(8,128)(2,1)S(1)} %concatenate.217), channel_id=1, source_target_pairs={{0,2},{1,3},{2,0},{3,1},{4,6},{5,7},{6,4},{7,5},{8,10},{9,11},{10,... | collective-permute-start | bytes 2088968 | tf_op jit(solution)/shard_map/ppermute | solution.py:14
  8.6 45.7 %collective-permute-start.35 = (bf16[256,640]{1,0:T(8,128)(2,1)S(1)}, bf16[256,640]{1,0:T(8,128)(2,1)S(1)}, u32[]{:S(2)}, u32[]{:S(2)}) collective-permute-start(bf16[256,640]{1,0:T(8,128)(2,1)S(1)} %get-tuple-element.68), channel_id=1, source_target_pairs={{0,2},{1,3},{4,6},{5,7},{8,10},{9,11},{12,14},{13,15},{16,18},{17,... | collective-permute-start | bytes 983048 | tf_op jit(solution)/shard_map/ppermute | solution.py:25
  11.0 45.3 %collective-permute-start.36 = (bf16[256,640]{1,0:T(8,128)(2,1)S(1)}, bf16[256,640]{1,0:T(8,128)(2,1)S(1)}, u32[]{:S(2)}, u32[]{:S(2)}) collective-permute-start(bf16[256,640]{1,0:T(8,128)(2,1)S(1)} %get-tuple-element.68), channel_id=1, source_target_pairs={{0,1},{1,2},{2,3},{4,5},{5,6},{6,7},{8,9},{9,10},{10,11},{12,13},{... | collective-permute-start | bytes 983048 | tf_op jit(solution)/shard_map/ppermute | solution.py:25
  58.1 36.9 %collective-permute-start.2 = (bf16[160,2176]{1,0:T(8,128)(2,1)S(1)}, bf16[160,2176]{1,0:T(8,128)(2,1)S(1)}, u32[]{:S(2)}, u32[]{:S(2)}) collective-permute-start(bf16[160,2176]{1,0:T(8,128)(2,1)S(1)} %collective-permute-done.1), channel_id=1, source_target_pairs={{0,16},{16,0},{1,17},{17,1},{2,18},{18,2},{3,19},{19,3},{4,20},{20... | collective-permute-start | bytes 2088968 | tf_op jit(solution)/shard_map/ppermute | solution.py:14
  58.2 40.4 %collective-permute-start.4 = (bf16[160,2176]{1,0:T(8,128)(2,1)S(1)}, bf16[160,2176]{1,0:T(8,128)(2,1)S(1)}, u32[]{:S(2)}, u32[]{:S(2)}) collective-permute-start(bf16[160,2176]{1,0:T(8,128)(2,1)S(1)} %collective-permute-done.3), channel_id=1, source_target_pairs={{0,16},{16,0},{1,17},{17,1},{2,18},{18,2},{3,19},{19,3},{4,20},{20... | collective-permute-start | bytes 2088968 | tf_op jit(solution)/shard_map/ppermute | solution.py:14
  74.4 20.4 %collective-permute-start.10 = (bf16[160,2176]{1,0:T(8,128)(2,1)S(1)}, bf16[160,2176]{1,0:T(8,128)(2,1)S(1)}, u32[]{:S(2)}, u32[]{:S(2)}) collective-permute-start(bf16[160,2176]{1,0:T(8,128)(2,1)S(1)} %collective-permute-done.8), channel_id=1, source_target_pairs={{0,1},{1,0},{2,3},{3,2},{4,5},{5,4},{6,7},{7,6},{8,9},{9,8},{10,11... | collective-permute-start | bytes 2088968 | tf_op jit(solution)/shard_map/ppermute | solution.py:14
  77.7 24.8 %collective-permute-start.9 = (bf16[160,2176]{1,0:T(8,128)(2,1)S(1)}, bf16[160,2176]{1,0:T(8,128)(2,1)S(1)}, u32[]{:S(2)}, u32[]{:S(2)}) collective-permute-start(bf16[160,2176]{1,0:T(8,128)(2,1)S(1)} %collective-permute-done.8), channel_id=1, source_target_pairs={{0,16},{16,0},{1,17},{17,1},{2,18},{18,2},{3,19},{19,3},{4,20},{20... | collective-permute-start | bytes 2088968 | tf_op jit(solution)/shard_map/ppermute | solution.py:14
  100.7 32.6 %collective-permute-start.11 = (bf16[160,2176]{1,0:T(8,128)(2,1)S(1)}, bf16[160,2176]{1,0:T(8,128)(2,1)S(1)}, u32[]{:S(2)}, u32[]{:S(2)}) collective-permute-start(bf16[160,2176]{1,0:T(8,128)(2,1)S(1)} %collective-permute-done.10), channel_id=1, source_target_pairs={{0,16},{16,0},{1,17},{17,1},{2,18},{18,2},{3,19},{19,3},{4,20},{20... | collective-permute-start | bytes 2088968 | tf_op jit(solution)/shard_map/ppermute | solution.py:14
  102.5 32.7 %collective-permute-start.13 = (bf16[160,2176]{1,0:T(8,128)(2,1)S(1)}, bf16[160,2176]{1,0:T(8,128)(2,1)S(1)}, u32[]{:S(2)}, u32[]{:S(2)}) collective-permute-start(bf16[160,2176]{1,0:T(8,128)(2,1)S(1)} %collective-permute-done.12), channel_id=1, source_target_pairs={{0,16},{16,0},{1,17},{17,1},{2,18},{18,2},{3,19},{19,3},{4,20},{20... | collective-permute-start | bytes 2088968 | tf_op jit(solution)/shard_map/ppermute | solution.py:14
  112.8 42.0 %collective-permute-start.18 = (bf16[160,2176]{1,0:T(8,128)(2,1)S(1)}, bf16[160,2176]{1,0:T(8,128)(2,1)S(1)}, u32[]{:S(2)}, u32[]{:S(2)}) collective-permute-start(bf16[160,2176]{1,0:T(8,128)(2,1)S(1)} %collective-permute-done.17), channel_id=1, source_target_pairs={{0,16},{16,0},{1,17},{17,1},{2,18},{18,2},{3,19},{19,3},{4,20},{20... | collective-permute-start | bytes 2088968 | tf_op jit(solution)/shard_map/ppermute | solution.py:14
  113.8 23.7 %collective-permute-start.19 = (bf16[160,2176]{1,0:T(8,128)(2,1)S(1)}, bf16[160,2176]{1,0:T(8,128)(2,1)S(1)}, u32[]{:S(2)}, u32[]{:S(2)}) collective-permute-start(bf16[160,2176]{1,0:T(8,128)(2,1)S(1)} %collective-permute-done.17), channel_id=1, source_target_pairs={{0,1},{1,0},{2,3},{3,2},{4,5},{5,4},{6,7},{7,6},{8,9},{9,8},{10,11... | collective-permute-start | bytes 2088968 | tf_op jit(solution)/shard_map/ppermute | solution.py:14
  145.8 26.3 %collective-permute-start.20 = (bf16[160,2176]{1,0:T(8,128)(2,1)S(1)}, bf16[160,2176]{1,0:T(8,128)(2,1)S(1)}, u32[]{:S(2)}, u32[]{:S(2)}) collective-permute-start(bf16[160,2176]{1,0:T(8,128)(2,1)S(1)} %collective-permute-done.19), channel_id=1, source_target_pairs={{0,16},{16,0},{1,17},{17,1},{2,18},{18,2},{3,19},{19,3},{4,20},{20... | collective-permute-start | bytes 2088968 | tf_op jit(solution)/shard_map/ppermute | solution.py:14
  152.0 23.6 %collective-permute-start.22 = (bf16[160,2176]{1,0:T(8,128)(2,1)S(1)}, bf16[160,2176]{1,0:T(8,128)(2,1)S(1)}, u32[]{:S(2)}, u32[]{:S(2)}) collective-permute-start(bf16[160,2176]{1,0:T(8,128)(2,1)S(1)} %collective-permute-done.21), channel_id=1, source_target_pairs={{0,16},{16,0},{1,17},{17,1},{2,18},{18,2},{3,19},{19,3},{4,20},{20... | collective-permute-start | bytes 2088968 | tf_op jit(solution)/shard_map/ppermute | solution.py:14
  152.0 38.0 %collective-permute-start.27 = (bf16[160,2176]{1,0:T(8,128)(2,1)S(1)}, bf16[160,2176]{1,0:T(8,128)(2,1)S(1)}, u32[]{:S(2)}, u32[]{:S(2)}) collective-permute-start(bf16[160,2176]{1,0:T(8,128)(2,1)S(1)} %collective-permute-done.26), channel_id=1, source_target_pairs={{0,16},{16,0},{1,17},{17,1},{2,18},{18,2},{3,19},{19,3},{4,20},{20... | collective-permute-start | bytes 2088968 | tf_op jit(solution)/shard_map/ppermute | solution.py:14
  152.6 24.9 %collective-permute-start.28 = (bf16[160,2176]{1,0:T(8,128)(2,1)S(1)}, bf16[160,2176]{1,0:T(8,128)(2,1)S(1)}, u32[]{:S(2)}, u32[]{:S(2)}) collective-permute-start(bf16[160,2176]{1,0:T(8,128)(2,1)S(1)} %collective-permute-done.26), channel_id=1, source_target_pairs={{0,1},{1,0},{2,3},{3,2},{4,5},{5,4},{6,7},{7,6},{8,9},{9,8},{10,11... | collective-permute-start | bytes 2088968 | tf_op jit(solution)/shard_map/ppermute | solution.py:14
  327.2 102.3 %collective-permute-start.39 = (bf16[256,640]{1,0:T(8,128)(2,1)}, bf16[256,640]{1,0:T(8,128)(2,1)}, u32[]{:S(2)}, u32[]{:S(2)}) collective-permute-start(bf16[256,640]{1,0:T(8,128)(2,1)} %broadcast_select_fusion.1), channel_id=1, source_target_pairs={{0,16},{16,0},{1,17},{17,1},{2,18},{18,2},{3,19},{19,3},{4,20},{20... | collective-permute-start | bytes 983048 | tf_op jit(solution)/shard_map/ppermute | solution.py:14
  370.6 61.3 %collective-permute-start.42 = (bf16[256,512]{0,1:T(8,128)(2,1)}, bf16[256,512]{0,1:T(8,128)(2,1)}, u32[]{:S(2)}, u32[]{:S(2)}) collective-permute-start(bf16[256,512]{0,1:T(8,128)(2,1)} %get-tuple-element.187), channel_id=1, source_target_pairs={{1,0},{2,1},{3,2},{5,4},{6,5},{7,6},{9,8},{10,9},{11,10},{13,12},{... | collective-permute-start | bytes 786440 | tf_op jit(solution)/shard_map/ppermute | solution.py:25
  371.9 60.0 %collective-permute-start.43 = (bf16[256,512]{0,1:T(8,128)(2,1)}, bf16[256,512]{0,1:T(8,128)(2,1)}, u32[]{:S(2)}, u32[]{:S(2)}) collective-permute-start(bf16[256,512]{0,1:T(8,128)(2,1)} %get-tuple-element.188), channel_id=1, source_target_pairs={{2,0},{3,1},{6,4},{7,5},{10,8},{11,9},{14,12},{15,13},{18,16},{19,... | collective-permute-start | bytes 786440 | tf_op jit(solution)/shard_map/ppermute | solution.py:25
  499.9 55.1 %collective-permute-start.46 = (bf16[160,2176]{1,0:T(8,128)(2,1)}, bf16[160,2176]{1,0:T(8,128)(2,1)}, u32[]{:S(2)}, u32[]{:S(2)}) collective-permute-start(bf16[160,2176]{1,0:T(8,128)(2,1)} %get-tuple-element.71), channel_id=1, source_target_pairs={{0,16},{16,0},{1,17},{17,1},{2,18},{18,2},{3,19},{19,3},{4,20},{20... | collective-permute-start | bytes 2088968 | tf_op jit(solution)/shard_map/ppermute | solution.py:14
  500.0 55.1 %collective-permute-start.47 = (bf16[160,2176]{1,0:T(8,128)(2,1)}, bf16[160,2176]{1,0:T(8,128)(2,1)}, u32[]{:S(2)}, u32[]{:S(2)}) collective-permute-start(bf16[160,2176]{1,0:T(8,128)(2,1)} %get-tuple-element.72), channel_id=1, source_target_pairs={{0,16},{16,0},{1,17},{17,1},{2,18},{18,2},{3,19},{19,3},{4,20},{20... | collective-permute-start | bytes 2088968 | tf_op jit(solution)/shard_map/ppermute | solution.py:14
  500.5 55.1 %collective-permute-start.50 = (bf16[160,2176]{1,0:T(8,128)(2,1)}, bf16[160,2176]{1,0:T(8,128)(2,1)}, u32[]{:S(2)}, u32[]{:S(2)}) collective-permute-start(bf16[160,2176]{1,0:T(8,128)(2,1)} %get-tuple-element.73), channel_id=1, source_target_pairs={{0,16},{16,0},{1,17},{17,1},{2,18},{18,2},{3,19},{19,3},{4,20},{20... | collective-permute-start | bytes 2088968 | tf_op jit(solution)/shard_map/ppermute | solution.py:14
  500.6 55.1 %collective-permute-start.54 = (bf16[160,2176]{1,0:T(8,128)(2,1)}, bf16[160,2176]{1,0:T(8,128)(2,1)}, u32[]{:S(2)}, u32[]{:S(2)}) collective-permute-start(bf16[160,2176]{1,0:T(8,128)(2,1)} %get-tuple-element.80), channel_id=1, source_target_pairs={{0,16},{16,0},{1,17},{17,1},{2,18},{18,2},{3,19},{19,3},{4,20},{20... | collective-permute-start | bytes 2088968 | tf_op jit(solution)/shard_map/ppermute | solution.py:14
  501.0 60.2 %collective-permute-start.63 = (bf16[160,2176]{1,0:T(8,128)(2,1)}, bf16[160,2176]{1,0:T(8,128)(2,1)}, u32[]{:S(2)}, u32[]{:S(2)}) collective-permute-start(bf16[160,2176]{1,0:T(8,128)(2,1)} %get-tuple-element.92), channel_id=1, source_target_pairs={{0,16},{16,0},{1,17},{17,1},{2,18},{18,2},{3,19},{19,3},{4,20},{20... | collective-permute-start | bytes 2088968 | tf_op jit(solution)/shard_map/ppermute | solution.py:14
  561.3 40.0 %collective-permute-start.69 = (bf16[160,2176]{1,0:T(8,128)(2,1)S(1)}, bf16[160,2176]{1,0:T(8,128)(2,1)S(1)}, u32[]{:S(2)}, u32[]{:S(2)}) collective-permute-start(bf16[160,2176]{1,0:T(8,128)(2,1)S(1)} %copy-done.160), channel_id=1, source_target_pairs={{0,16},{16,0},{1,17},{17,1},{2,18},{18,2},{3,19},{19,3},{4,20},{20... | collective-permute-start | bytes 2088968 | tf_op jit(solution)/shard_map/ppermute | solution.py:14
  562.2 56.0 %collective-permute-start.55 = (bf16[160,2176]{1,0:T(8,128)(2,1)S(1)}, bf16[160,2176]{1,0:T(8,128)(2,1)S(1)}, u32[]{:S(2)}, u32[]{:S(2)}) collective-permute-start(bf16[160,2176]{1,0:T(8,128)(2,1)S(1)} %copy-done.159), channel_id=1, source_target_pairs={{0,16},{16,0},{1,17},{17,1},{2,18},{18,2},{3,19},{19,3},{4,20},{20... | collective-permute-start | bytes 2088968 | tf_op jit(solution)/shard_map/ppermute | solution.py:14
  563.5 64.7 %collective-permute-start.58 = (bf16[160,2176]{1,0:T(8,128)(2,1)S(1)}, bf16[160,2176]{1,0:T(8,128)(2,1)S(1)}, u32[]{:S(2)}, u32[]{:S(2)}) collective-permute-start(bf16[160,2176]{1,0:T(8,128)(2,1)S(1)} %copy-done.158), channel_id=1, source_target_pairs={{0,16},{16,0},{1,17},{17,1},{2,18},{18,2},{3,19},{19,3},{4,20},{20... | collective-permute-start | bytes 2088968 | tf_op jit(solution)/shard_map/ppermute | solution.py:14
  571.0 29.1 %collective-permute-start.67 = (bf16[80,2176]{1,0:T(8,128)(2,1)S(1)}, bf16[80,2176]{1,0:T(8,128)(2,1)S(1)}, u32[]{:S(2)}, u32[]{:S(2)}) collective-permute-start(bf16[80,2176]{1,0:T(8,128)(2,1)S(1)} %get-tuple-element.210), channel_id=1, source_target_pairs={{0,1},{1,0},{2,3},{3,2},{4,5},{5,4},{6,7},{7,6},{8,9},{9,8},{10,11... | collective-permute-start | bytes 1044488 | tf_op jit(solution)/shard_map/ppermute | solution.py:14
  601.3 27.0 %collective-permute-start.61 = (bf16[160,2176]{1,0:T(8,128)(2,1)S(1)}, bf16[160,2176]{1,0:T(8,128)(2,1)S(1)}, u32[]{:S(2)}, u32[]{:S(2)}) collective-permute-start(bf16[160,2176]{1,0:T(8,128)(2,1)S(1)} %copy-done.157), channel_id=1, source_target_pairs={{0,16},{16,0},{1,17},{17,1},{2,18},{18,2},{3,19},{19,3},{4,20},{20... | collective-permute-start | bytes 2088968 | tf_op jit(solution)/shard_map/ppermute | solution.py:14
  628.2 28.0 %collective-permute-start.53 = (bf16[160,2176]{1,0:T(8,128)(2,1)S(1)}, bf16[160,2176]{1,0:T(8,128)(2,1)S(1)}, u32[]{:S(2)}, u32[]{:S(2)}) collective-permute-start(bf16[160,2176]{1,0:T(8,128)(2,1)S(1)} %copy-done.156), channel_id=1, source_target_pairs={{0,16},{16,0},{1,17},{17,1},{2,18},{18,2},{3,19},{19,3},{4,20},{20... | collective-permute-start | bytes 2088968 | tf_op jit(solution)/shard_map/ppermute | solution.py:14
  628.3 46.4 %collective-permute-start.45 = (bf16[160,2176]{1,0:T(8,128)(2,1)S(1)}, bf16[160,2176]{1,0:T(8,128)(2,1)S(1)}, u32[]{:S(2)}, u32[]{:S(2)}) collective-permute-start(bf16[160,2176]{1,0:T(8,128)(2,1)S(1)} %copy-done.155), channel_id=1, source_target_pairs={{0,16},{16,0},{1,17},{17,1},{2,18},{18,2},{3,19},{19,3},{4,20},{20... | collective-permute-start | bytes 2088968 | tf_op jit(solution)/shard_map/ppermute | solution.py:14
  (352 other events, 2750.2 us)

commit v2 on v1

v2 whole, which is shorter than its diff:
```python
import jax
import jax.numpy as jnp
from jax import lax
from jax.experimental import pallas as pl
from jax.experimental.pallas import tpu as pltpu
from jax.sharding import PartitionSpec as P

WINDOW = 512
EPSILON = 1e-06
LOW = jnp.bfloat16
WIDE = jnp.float32
SECTION = "section"
DATA = "fsdp"
HEAD = "tensor"
CORES = 2
HEADS = 4
VMEM_BYTES = 56 * 1024 * 1024


def flip(value, axis, bit):
    count = lax.axis_size(axis)
    return lax.ppermute(value, axis, [(i, i ^ bit) for i in range(count)])


def ring(value):
    count = lax.axis_size(DATA)
    return lax.ppermute(value, DATA, [(i, (i + 1) % count) for i in range(count)])


def shifted(value, axis, by):
    count = lax.axis_size(axis)
    pairs = [(i, i + by) for i in range(count) if 0 <= i + by < count]
    return lax.ppermute(value, axis, pairs)


def add(*parts):
    total = parts[0].astype(WIDE)
    for part in parts[1:]:
        total = total + part.astype(WIDE)
    return total


def dot(left, right):
    return jnp.dot(left, right, preferred_element_type=WIDE)


def dot_nt(left, right):
    return lax.dot_general(left, right, (((1,), (1,)), ((), ())), preferred_element_type=WIDE)


def dot_tn(left, right):
    return lax.dot_general(left, right, (((0,), (0,)), ((), ())), preferred_element_type=WIDE)


def gather_slab(slab):
    ranks = lax.axis_size(DATA)
    section = lax.axis_index(SECTION)
    data = lax.axis_index(DATA)
    head = lax.axis_index(HEAD)
    rows, columns = slab.shape
    cut = (columns // 256 + 1) * 128
    current = slab[None]
    if ranks > 4:
        current = lax.all_gather(slab, DATA, axis=0, tiled=False)
        steps, data = 1, 0
    else:
        steps = ranks
    whole = jnp.zeros((HEADS, ranks, CORES, rows, columns), slab.dtype)
    for step in range(steps):
        chunk = current
        place = (data - step) % steps
        if step < steps - 1:
            current = ring(current)
        near = flip(chunk, HEAD, 1)
        far = flip(chunk, HEAD, 2)
        across = jnp.concatenate(
            [flip(far[..., :cut], HEAD, 1), flip(near[..., cut:], HEAD, 2)], axis=-1
        )
        for piece, bit in ((chunk, 0), (near, 1), (far, 2), (across, 3)):
            other = flip(piece, SECTION, 1)
            for part, core in ((piece, section), (other, 1 - section)):
                whole = lax.dynamic_update_slice(
                    whole, part[None, :, None], (head ^ bit, place, core, 0, 0)
                )
    return whole.reshape(HEADS, ranks * CORES * rows, columns)


def scatter_slab(whole, ranks):
    section = lax.axis_index(SECTION)
    data = lax.axis_index(DATA)
    head = lax.axis_index(HEAD)
    columns = whole.shape[-1]
    rows = whole.shape[1] // (CORES * ranks)
    whole = whole.reshape(HEADS, ranks, CORES, rows, columns)
    cut = (columns // 256 + 1) * 128
    spread = ranks > 4
    steps = 1 if spread else ranks
    data = 0 if spread else data
    depth = ranks if spread else 1
    arriving = None
    total = None
    for step in range(steps):
        place = (data - 1 - step) % steps

        def piece(bit):
            own, other = (
                lax.dynamic_slice(
                    whole, (head ^ bit, place, core, 0, 0), (1, depth, 1, rows, columns)
                )[0, :, 0]
                for core in (section, 1 - section)
            )
            return add(own, flip(other, SECTION, 1)).astype(LOW)

        across = piece(3)
        left = flip(across[..., :cut], HEAD, 1)
        right = flip(across[..., cut:], HEAD, 2)
        near = piece(1)
        far = piece(2)
        far = jnp.concatenate([add(far[..., :cut], left).astype(LOW), far[..., cut:]], axis=-1)
        near = jnp.concatenate([near[..., :cut], add(near[..., cut:], right).astype(LOW)], axis=-1)
        total = add(piece(0), flip(near, HEAD, 1), flip(far, HEAD, 2))
        if arriving is not None:
            total = total + arriving.astype(WIDE)
        if step < steps - 1:
            arriving = ring(total.astype(LOW))
    if spread:
        return lax.psum_scatter(
            total.astype(LOW), DATA, scatter_dimension=0, tiled=False
        ).astype(WIDE)
    return total[0]


def by_section(own, other):
    section = lax.axis_index(SECTION)
    return jnp.where(section == 0, own, other), jnp.where(section == 0, other, own)


def gather_gains(gains):
    ranks = lax.axis_size(DATA)
    data = lax.axis_index(DATA)
    if ranks > 4:
        full = lax.all_gather(gains, DATA, axis=0, tiled=False)
    else:
        full = jnp.zeros((ranks,) + gains.shape, gains.dtype)
        for step in range(ranks):
            full = lax.dynamic_update_slice(full, gains[None], ((data - step) % ranks, 0))
            if step < ranks - 1:
                gains = ring(gains)
    return by_section(full, flip(full, SECTION, 1))


def scatter_gains(first, second):
    ranks = lax.axis_size(DATA)
    data = lax.axis_index(DATA)
    own, sent = by_section(first, second)
    total = own + flip(sent, SECTION, 1)
    total = total + flip(total, HEAD, 1)
    total = total + flip(total, HEAD, 2)
    if ranks > 4:
        return lax.psum_scatter(total, DATA, scatter_dimension=0, tiled=False)
    arriving = None
    for step in range(ranks):
        kept = lax.dynamic_index_in_dim(total, (data - 1 - step) % ranks, 0, keepdims=False)
        if arriving is not None:
            kept = kept + arriving
        if step < ranks - 1:
            arriving = ring(kept)
    return kept


def norm_parts(value_rows):
    scale = lax.rsqrt(jnp.mean(value_rows * value_rows, axis=-1, keepdims=True) + EPSILON)
    return value_rows * scale, scale


def norm_rows(value_rows, gain_value):
    return norm_parts(value_rows)[0] * gain_value


def norm_back(value_rows, gain_value, cotangent):
    unit, scale = norm_parts(value_rows)
    weighted = cotangent * gain_value
    rows_grad = scale * (weighted - unit * jnp.mean(weighted * unit, axis=-1, keepdims=True))
    return rows_grad, jnp.sum(cotangent * unit, axis=0, keepdims=True)


def rotate(value_rows, cosine, sine):
    half_depth = value_rows.shape[-1] // 2
    first = value_rows[:, :half_depth]
    second = value_rows[:, half_depth:]
    return jnp.concatenate(
        [first * cosine - second * sine, second * cosine + first * sine], axis=-1
    )


def gelu_parts(gate):
    root = 0.7978845608028654
    tanh = jnp.tanh(root * (gate + 0.044715 * gate * gate * gate))
    value = 0.5 * gate * (1.0 + tanh)
    slope = 0.5 * (1.0 + tanh) + 0.5 * gate * (1.0 - tanh * tanh) * root * (
        1.0 + 3.0 * 0.044715 * gate * gate
    )
    return value, slope


def softmax(scores):
    exponent = jnp.exp(scores - jnp.max(scores, axis=-1, keepdims=True))
    return exponent / jnp.sum(exponent, axis=-1, keepdims=True)


def shapes(slab_columns, width_pair):
    head_width = width_pair // 2
    hidden = (slab_columns - width_pair - width_pair // HEADS) // 3
    return head_width, hidden


def keys_kernel(x_ref, gain_ref, key_gain_ref, cos_ref, sin_ref, slab_ref, pair_ref, weights, sem):
    width_pair = pair_ref.shape[1]
    quarter = width_pair // HEADS
    copies = []
    for t in range(HEADS):
        copies.append(
            pltpu.make_async_copy(
                slab_ref.at[t, :, pl.ds(width_pair, quarter)],
                weights.at[:, pl.ds(t * quarter, quarter)],
                sem.at[t],
            )
        )
        copies[-1].start()
    normed = norm_rows(x_ref[...].astype(WIDE), gain_ref[...]).astype(LOW)
    for copy in copies:
        copy.wait()
    pair = dot(normed, weights[...])
    half = width_pair // 2
    key = rotate(norm_rows(pair[:, :half], key_gain_ref[...]), cos_ref[...], sin_ref[...])
    pair_ref[:, :half] = key.astype(LOW)
    pair_ref[:, half:] = pair[:, half:].astype(LOW)


def fetch_layer(slab_ref, attn, feed, sems):
    own = attn.shape[2]
    rest = feed.shape[2]
    first, second = [], []
    for t in range(HEADS):
        first.append(
            pltpu.make_async_copy(slab_ref.at[t, :, pl.ds(0, own)], attn.at[t], sems.at[t])
        )
        second.append(
            pltpu.make_async_copy(
                slab_ref.at[t, :, pl.ds(slab_ref.shape[2] - rest, rest)],
                feed.at[t],
                sems.at[HEADS + t],
            )
        )
    return first, second


def forward_kernel(
    x_ref, pair_ref, bias_ref, cos_ref, sin_ref, before_ref, query_gain_ref, after_ref,
    feed_gain_ref, final_ref, slab_ref,
    result_ref, attended_ref, sum_ref, hidden_ref, branch_ref,
    attn, feed, sems,
):
    width = pair_ref.shape[1] // 2
    hidden_width = feed.shape[2] // 3
    scale = width ** (-0.5)
    first, second = fetch_layer(slab_ref, attn, feed, sems)
    for copy in first + second:
        copy.start()
    x = x_ref[...].astype(WIDE)
    cosine, sine, bias = cos_ref[...], sin_ref[...], bias_ref[...]
    normed = norm_rows(x, before_ref[...]).astype(LOW)
    for t in range(HEADS):
        first[t].wait()
        raw = dot(normed, attn[t, :, :width])
        query = rotate(norm_rows(raw, query_gain_ref[...]), cosine, sine).astype(LOW)
        chance = softmax(dot_nt(query, pair_ref[:, :width]) * scale + bias).astype(LOW)
        mixed = dot(chance, pair_ref[:, width:]).astype(LOW)
        attended_ref[:, t * width : (t + 1) * width] = mixed
        part = dot_nt(mixed, attn[t, :, width:])
        sum_ref[...] = part if t == 0 else sum_ref[...] + part
    hidden = x + norm_rows(sum_ref[...], after_ref[...])
    hidden_ref[...] = hidden
    feed_in = norm_rows(hidden, feed_gain_ref[...]).astype(LOW)
    for t in range(HEADS):
        second[t].wait()
        gate = dot(feed_in, feed[t, :, :hidden_width])
        up = dot(feed_in, feed[t, :, hidden_width : 2 * hidden_width])
        product = (gelu_parts(gate)[0] * up).astype(LOW)
        part = dot_nt(product, feed[t, :, 2 * hidden_width :])
        branch_ref[...] = part if t == 0 else branch_ref[...] + part
    result = hidden_ref[...] + norm_rows(branch_ref[...], final_ref[...])
    result_ref[...] = result.astype(LOW)


def backward_kernel(
    dy_ref, x_ref, pair_ref, bias_ref, cos_ref, sin_ref, before_ref, query_gain_ref, after_ref,
    feed_gain_ref, final_ref, attended_ref, sum_ref, hidden_ref, branch_ref, slab_ref,
    grad_ref, own_ref, sent_ref, normed_ref, d_hidden_ref, gains_ref,
    attn, feed, grad_attn, grad_feed, d_pair, sems,
):
    width = pair_ref.shape[1] // 2
    hidden_width = feed.shape[2] // 3
    rows = x_ref.shape[0]
    scale = width ** (-0.5)
    first, second = fetch_layer(slab_ref, attn, feed, sems)
    out_first, out_second = [], []
    for t in range(HEADS):
        out_first.append(
            pltpu.make_async_copy(
                grad_attn.at[t], grad_ref.at[t, :, pl.ds(0, 2 * width)], sems.at[2 * HEADS + t]
            )
        )
        out_second.append(
            pltpu.make_async_copy(
                grad_feed.at[t],
                grad_ref.at[t, :, pl.ds(slab_ref.shape[2] - feed.shape[2], feed.shape[2])],
                sems.at[3 * HEADS + t],
            )
        )
    for copy in second + first:
        copy.start()
    dy = dy_ref[...].astype(WIDE)
    d_branch, final_grad = norm_back(branch_ref[...], final_ref[...], dy)
    d_branch = d_branch.astype(LOW)
    hidden = hidden_ref[...]
    feed_in = norm_rows(hidden, feed_gain_ref[...]).astype(LOW)
    for t in range(HEADS):
        second[t].wait()
        gate = dot(feed_in, feed[t, :, :hidden_width])
        up = dot(feed_in, feed[t, :, hidden_width : 2 * hidden_width])
        value, slope = gelu_parts(gate)
        product = (value * up).astype(LOW)
        d_product = dot(d_branch, feed[t, :, 2 * hidden_width :])
        d_gate = (d_product * up * slope).astype(LOW)
        d_up = (d_product * value).astype(LOW)
        part = dot_nt(d_gate, feed[t, :, :hidden_width]) + dot_nt(
            d_up, feed[t, :, hidden_width : 2 * hidden_width]
        )
        normed_ref[...] = part if t == 0 else normed_ref[...] + part
        grad_feed[t, :, :hidden_width] = dot_tn(feed_in, d_gate).astype(LOW)
        grad_feed[t, :, hidden_width : 2 * hidden_width] = dot_tn(feed_in, d_up).astype(LOW)
        grad_feed[t, :, 2 * hidden_width :] = dot_tn(d_branch, product).astype(LOW)
        out_second[t].start()
    part_hidden, feed_grad = norm_back(hidden, feed_gain_ref[...], normed_ref[...])
    d_hidden = dy + part_hidden
    d_hidden_ref[...] = d_hidden
    d_sum, after_grad = norm_back(sum_ref[...], after_ref[...], d_hidden)
    d_sum = d_sum.astype(LOW)
    cosine, sine, bias = cos_ref[...], sin_ref[...], bias_ref[...]
    normed = norm_rows(x_ref[...].astype(WIDE), before_ref[...]).astype(LOW)
    query_grad = jnp.zeros((1, width), WIDE)
    for t in range(HEADS):
        first[t].wait()
        key = pair_ref[:, :width]
        raw = dot(normed, attn[t, :, :width])
        query = rotate(norm_rows(raw, query_gain_ref[...]), cosine, sine).astype(LOW)
        chance = softmax(dot_nt(query, key) * scale + bias)
        d_mixed = dot(d_sum, attn[t, :, width:]).astype(LOW)
        grad_attn[t, :, width:] = dot_tn(
            d_sum, attended_ref[:, t * width : (t + 1) * width]
        ).astype(LOW)
        d_chance = dot_nt(d_mixed, pair_ref[:, width:])
        weighted = jnp.sum(chance * d_chance, axis=-1, keepdims=True)
        d_scores = (chance * (d_chance - weighted)).astype(LOW)
        d_key = dot_tn(d_scores, query) * scale
        d_value = dot_tn(chance.astype(LOW), d_mixed)
        d_pair[:, :width] = d_key if t == 0 else d_pair[:, :width] + d_key
        d_pair[:, width:] = d_value if t == 0 else d_pair[:, width:] + d_value
        d_query = rotate(dot(d_scores, key) * scale, cosine, -sine)
        d_raw, gain_part = norm_back(raw, query_gain_ref[...], d_query)
        query_grad = query_grad + gain_part
        d_raw = d_raw.astype(LOW)
        grad_attn[t, :, :width] = dot_tn(normed, d_raw).astype(LOW)
        out_first[t].start()
        part = dot_nt(d_raw, attn[t, :, :width])
        normed_ref[...] = part if t == 0 else normed_ref[...] + part
    earlier = d_pair.shape[0] - rows
    own_ref[...] = d_pair[earlier:, :]
    sent_ref[...] = d_pair[:earlier, :].astype(LOW)
    gains_ref[...] = jnp.zeros(gains_ref.shape, WIDE)
    gains_ref[0:1, :] = after_grad
    gains_ref[1:2, :] = feed_grad
    gains_ref[2:3, :] = final_grad
    gains_ref[3:4, :width] = query_grad
    for copy in out_first + out_second:
        copy.wait()


def closing_kernel(
    own_ref, arrived_ref, x_ref, before_ref, key_gain_ref, cos_ref, sin_ref, d_normed_ref,
    d_hidden_ref, slab_ref, grad_in_ref,
    input_ref, gains_ref, grad_ref,
    weights, grad_pair, sems,
):
    width_pair = own_ref.shape[1]
    quarter = width_pair // HEADS
    half = width_pair // 2
    copies, outs = [], []
    for t in range(HEADS):
        columns = pl.ds(t * quarter, quarter)
        copies.append(
            pltpu.make_async_copy(
                slab_ref.at[t, :, pl.ds(width_pair, quarter)], weights.at[:, columns], sems.at[t]
            )
        )
        outs.append(
            pltpu.make_async_copy(
                grad_pair.at[:, columns],
                grad_ref.at[t, :, pl.ds(width_pair, quarter)],
                sems.at[HEADS + t],
            )
        )
        copies[-1].start()
    x = x_ref[...].astype(WIDE)
    normed = norm_rows(x, before_ref[...]).astype(LOW)
    d_pair = own_ref[...]
    for back in range(arrived_ref.shape[0]):
        d_pair = d_pair + arrived_ref[back].astype(WIDE)
    for copy in copies:
        copy.wait()
    raw = dot(normed, weights[:, :half])
    d_key, key_grad = norm_back(
        raw, key_gain_ref[...], rotate(d_pair[:, :half], cos_ref[...], -sin_ref[...])
    )
    low_pair = jnp.concatenate([d_key.astype(LOW), d_pair[:, half:].astype(LOW)], axis=1)
    grad_pair[...] = dot_tn(normed, low_pair).astype(LOW)
    for copy in outs:
        copy.start()
    d_normed = d_normed_ref[...] + dot_nt(low_pair, weights[...])
    part_inputs, before_grad = norm_back(x, before_ref[...], d_normed)
    input_ref[...] = d_hidden_ref[...] + part_inputs
    gains_ref[...] = jnp.zeros(gains_ref.shape, WIDE)
    gains_ref[0:1, :] = before_grad
    gains_ref[1:2, :half] = key_grad
    for copy in outs:
        copy.wait()


def call(kernel, name, args, whole_at, outs, out_whole, scratch, sems, aliases=None):
    anywhere = pl.BlockSpec(memory_space=pl.ANY)
    near = pl.BlockSpec(memory_space=pltpu.VMEM)
    return pl.pallas_call(
        kernel,
        name=name,
        out_shape=[jax.ShapeDtypeStruct(shape, dtype) for shape, dtype in outs],
        in_specs=[anywhere if i in whole_at else near for i in range(len(args))],
        out_specs=[anywhere if i in out_whole else near for i in range(len(outs))],
        scratch_shapes=[pltpu.VMEM(shape, dtype) for shape, dtype in scratch]
        + [pltpu.SemaphoreType.DMA((sems,))],
        input_output_aliases=aliases or {},
        compiler_params=pltpu.CompilerParams(vmem_limit_bytes=VMEM_BYTES),
    )(*args)


def layer_keys(x, layer, turns):
    slab, before, query_gain, key_gain, after, feed_gain, final = layer
    pair = 2 * key_gain.shape[1]
    cosine, sine = turns
    args = (x, before, key_gain, cosine, sine, slab)
    outs = [((x.shape[0], pair), LOW)]
    scratch = [((x.shape[1], pair), LOW)]
    return call(keys_kernel, "keys", args, (5,), outs, (), scratch, HEADS)[0]


def layer_forward(x, pair, layer, bias, turns):
    slab, before, query_gain, key_gain, after, feed_gain, final = layer
    rows, width = x.shape
    own = pair.shape[1]
    rest = slab.shape[2] - own - own // HEADS
    args = (x, pair, bias) + turns + (before, query_gain, after, feed_gain, final, slab)
    token = ((rows, width), WIDE)
    outs = [((rows, width), LOW), ((rows, own // 2 * HEADS), LOW), token, token, token]
    scratch = [((HEADS, width, own), LOW), ((HEADS, width, rest), LOW)]
    return call(
        forward_kernel, "forward", args, (len(args) - 1,), outs, (), scratch, 2 * HEADS
    )


def layer_backward(dy, x, pair, kept, layer, bias, turns):
    slab, before, query_gain, key_gain, after, feed_gain, final = layer
    rows, width = x.shape
    own = pair.shape[1]
    rest = slab.shape[2] - own - own // HEADS
    earlier = pair.shape[0] - rows
    args = (
        (dy, x, pair, bias) + turns + (before, query_gain, after, feed_gain, final)
        + tuple(kept) + (slab,)
    )
    token = ((rows, width), WIDE)
    outs = [
        (slab.shape, LOW), ((rows, own), WIDE), ((earlier, own), LOW), token, token,
        ((8, width), WIDE),
    ]
    scratch = [
        ((HEADS, width, own), LOW), ((HEADS, width, rest), LOW),
        ((HEADS, width, own), LOW), ((HEADS, width, rest), LOW), (pair.shape, WIDE),
    ]
    grads, d_own, sent, d_normed, d_hidden, gains = call(
        backward_kernel, "backward", args, (len(args) - 1,), outs, (0,), scratch, 4 * HEADS
    )
    back = earlier // rows
    arrived = jnp.stack(
        [
            shifted(sent[(back - by) * rows : (back - by + 1) * rows], HEAD, -by)
            for by in range(1, back + 1)
        ]
    )
    args = (d_own, arrived, x, before, key_gain) + turns + (d_normed, d_hidden, slab, grads)
    outs = [token, ((8, width), WIDE), (slab.shape, LOW)]
    scratch = [((width, own), LOW), ((width, own), LOW)]
    input_grad, more, grads = call(
        closing_kernel, "closing", args, (9, 10), outs, (2,), scratch, 2 * HEADS, {10: 2}
    )
    gain_grads = (
        more[0], gains[3, : own // 2], more[1, : own // 2], gains[0], gains[1], gains[2],
    )
    return input_grad, grads, gain_grads


def body(
    inputs,
    out_grad,
    segment_ids,
    positions,
    before_gain,
    query_matrix,
    key_matrix,
    value_matrix,
    query_gain,
    key_gain,
    output_matrix,
    after_gain,
    feed_gain,
    gate_matrix,
    up_matrix,
    down_matrix,
    final_gain,
):
    section = lax.axis_index(SECTION)
    head = lax.axis_index(HEAD)
    ranks = lax.axis_size(DATA)
    rows, width = inputs.shape[1:]
    head_width = key_matrix.shape[2]
    depth = gate_matrix.shape[1]
    hidden_width = gate_matrix.shape[2]
    back = min(-(-(WINDOW - 1) // rows), HEADS - 1)
    quarter = 2 * head_width // HEADS

    shared = jnp.concatenate([key_matrix[0], value_matrix[0]], axis=1)
    slab = jnp.concatenate(
        [
            query_matrix[0],
            output_matrix[0].T,
            lax.dynamic_slice_in_dim(shared, head * quarter, quarter, 1),
            gate_matrix[0],
            up_matrix[0],
            down_matrix[0].T,
        ],
        axis=1,
    )
    half = depth // CORES
    upper, lower = slab[:half], slab[half:]
    traded = flip(jnp.where(section == 0, lower, upper), SECTION, 1)
    halves = jnp.where(section == 0, upper, traded), jnp.where(section == 0, traded, lower)

    gain_list = (before_gain, query_gain, key_gain, after_gain, feed_gain, final_gain)
    sizes = [gain.shape[1] for gain in gain_list]
    gain_both = gather_gains(jnp.concatenate([gain[0] for gain in gain_list]))

    first_input = lax.dynamic_index_in_dim(inputs, section, 0, keepdims=False)
    last_cot = lax.dynamic_index_in_dim(out_grad, section, 0, keepdims=False)
    segments = lax.dynamic_index_in_dim(segment_ids, section, 0, keepdims=False)
    token_positions = lax.dynamic_index_in_dim(positions, section, 0, keepdims=False)
    everyone = jnp.concatenate(
        [shifted(first_input, HEAD, by) for by in range(back, 0, -1)] + [first_input]
    )
    padded_segments = jnp.concatenate([jnp.full((back * rows,), -1, jnp.int32), segments])
    padded_positions = jnp.concatenate([jnp.zeros((back * rows,), jnp.int32), token_positions])
    key_segments = lax.dynamic_slice_in_dim(padded_segments, head * rows, (back + 1) * rows)
    key_positions = lax.dynamic_slice_in_dim(padded_positions, head * rows, (back + 1) * rows)
    gap = key_positions[-rows:, None] - key_positions[None, :]
    allowed = (
        (key_segments[-rows:, None] == key_segments[None, :]) & (gap >= 0) & (gap < WINDOW)
    )
    bias = jnp.where(allowed, 0.0, -1e30).astype(WIDE)
    half_depth = head_width // 2
    frequency = 10000.0 ** (-(jnp.arange(half_depth, dtype=WIDE) * 2.0) / head_width)
    turn = key_positions.astype(WIDE)[:, None] * frequency
    turns_all = jnp.cos(turn), jnp.sin(turn)
    turns = turns_all[0][-rows:], turns_all[1][-rows:]

    layers = []
    for index in range(2):
        gains, first = [], 0
        for size in sizes:
            gains.append(gain_both[index][:, first : first + size].reshape(1, -1).astype(WIDE))
            first += size
        layers.append((gather_slab(halves[index]),) + tuple(gains))

    pair_first = layer_keys(everyone, layers[0], turns_all)
    out_first, *kept_first = layer_forward(first_input, pair_first, layers[0], bias, turns)
    own_pair = layer_keys(out_first, layers[1], turns)
    pair_second = jnp.concatenate(
        [shifted(own_pair, HEAD, by) for by in range(back, 0, -1)] + [own_pair]
    )
    out_second, *kept_second = layer_forward(out_first, pair_second, layers[1], bias, turns)
    grad_second, slab_second, gains_second = layer_backward(
        last_cot, out_first, pair_second, kept_second, layers[1], bias, turns
    )
    total_second = scatter_slab(slab_second, ranks)
    grad_first, slab_first, gains_first = layer_backward(
        grad_second.astype(LOW), first_input, pair_first, kept_first, layers[0], bias, turns
    )
    total_first = scatter_slab(slab_first, ranks)

    def settle(first, second):
        own, sent = by_section(first, second)
        return jnp.stack(by_section(own, flip(sent, SECTION, 1)))[None]

    gain_own = scatter_gains(
        *(
            jnp.concatenate([gain.reshape(ranks, -1) for gain in gains], axis=1)
            for gains in (gains_first, gains_second)
        )
    )
    gain_grads, first = [], 0
    for size in sizes:
        gain_grads.append(gain_own[None, first : first + size])
        first += size

    own, sent = by_section(total_first, total_second)
    own = jnp.concatenate(by_section(own, flip(sent, SECTION, 1)))
    starts = [0]
    for step in (head_width, head_width, quarter, hidden_width, hidden_width, hidden_width):
        starts.append(starts[-1] + step)
    cut = [own[:, a:b] for a, b in zip(starts[:-1], starts[1:])]
    pair = cut[2].astype(LOW)
    shared = jnp.zeros((depth, 2 * head_width), LOW)
    for bit in range(HEADS):
        piece = pair if bit == 0 else flip(pair, HEAD, bit)
        shared = lax.dynamic_update_slice(shared, piece, (0, (head ^ bit) * quarter))
    shared = shared.astype(WIDE)
    return (
        settle(out_first, out_second),
        settle(grad_first, grad_second),
        gain_grads[0],
        cut[0][None],
        shared[None, :, :head_width],
        shared[None, :, head_width:],
        gain_grads[1],
        gain_grads[2],
        cut[1].T[None],
        gain_grads[3],
        gain_grads[4],
        cut[3][None],
        cut[4][None],
        cut[5].T[None],
        gain_grads[5],
    )


def solution(mesh):
    tokens = P(None, (DATA, HEAD), None)
    pack = P(None, DATA)
    gain = P(SECTION, DATA)
    split = P(SECTION, DATA, HEAD)
    plain = P(SECTION, DATA, None)
    turned = P(SECTION, HEAD, DATA)
    outs = P(SECTION, None, (DATA, HEAD), None)
    weights = (
        gain, split, plain, plain, gain, gain, turned, gain, gain, split, split, turned, gain,
    )
    return jax.shard_map(
        body,
        mesh=mesh,
        in_specs=(tokens, tokens, pack, pack) + weights,
        out_specs=(outs, outs) + weights,
        check_vma=False,
    )
```

time: 701 us -> 558 us (0.80)
  matrix products: 140 us -> 0 us
  Pallas kernels: 10.2 us -> 91.7 us
  blocking collectives: 69 us -> 0 us
  other arithmetic: 86.5 us -> 32.3 us
  starting transfers between devices: 65.1 us -> 116 us
  local copies, waits for them, and re-layouts: 132 us -> 94.5 us
  waiting for transfers between devices: 186 us -> 211 us
    dot_general x176 -> x0, matrix products: 140 us -> none  [the longest x60 54.1 us: dot_tn(): lax.dot_general(left, right, (((0,), (0,)), ((), ())), preferred_element_...]
    pallas_call x0 -> x8, Pallas kernels: none -> 91.7 us  [call(): pl.pallas_call(kernel, name=name, out_shape=[jax.ShapeDtypeStruct(shape,...]
    concatenate x18 -> x12, local copies, waits for them, and re-layouts: 47.8 us -> 2.65 us  [the longest x1 1.42 us: body(): gain_both = gather_gains(jnp.concatenate([gain[0] for gain in gain_list]))]
    psum x1 -> x0, blocking collectives: 45 us -> none  [body(): gain_sum = lax.psum(jnp.stack(gain_sums), ('section', 'fsdp', 'tensor'))]
    ppermute x69 -> x139, starting transfers between devices: 43.3 us -> 81.4 us  [flip(): return lax.ppermute(value, axis, [(i, i ^ bit) for i in range(count)])]
    all_gather x1 -> x0, blocking collectives: 23.9 us -> none  [body(): lax.all_gather(gain_flat, ('section', 'fsdp'), axis=0, tiled=False)]
    another operation x13 -> x4, other arithmetic: 26.1 us -> 2.91 us  [the longest x2 1.7 us: layer_backward(): jnp.stack([shifted(sent[(back - by) * rows:(back - by + 1) * rows], HEAD,...]
    dynamic_update_slice x36 -> x68, local copies, waits for them, and re-layouts: 30.7 us -> 47.2 us  [the longest x61 46.9 us: gather_slab(): lax.dynamic_update_slice(whole, part[None, :, None], (head ^ bit, place,...]
  transfers between devices with their start and end apart: 83 -> 165, of which waited for: 30 -> 69; matrix products, arithmetic and copies ran while one was open for 26% -> 21% of each run, Pallas kernels for 0% -> 0%
where the time goes in v2:
time: 558 us; the launch traced here: 549 us
  waiting for transfers between devices  211 us (38%)
  starting transfers between devices  116 us (21%)
  local copies, waits for them, and re-layouts  94.5 us (17%)
  Pallas kernels  91.7 us (16%)
  other arithmetic  32.3 us (6%)
    ppermute x139, waiting for transfers between devices, flip(): return lax.ppermute(value, axis, [(i, i ^ bit) for i in range(count)])  153 us
    pallas_call x8, Pallas kernels, call(): pl.pallas_call(kernel, name=name, out_shape=[jax.ShapeDtypeStruct(shape,...  91.7 us
    ppermute x139, starting transfers between devices, flip(): return lax.ppermute(value, axis, [(i, i ^ bit) for i in range(count)])  81.4 us
    dynamic_update_slice x61, local copies, waits for them, and re-layouts, gather_slab(): lax.dynamic_update_slice(whole, part[None, :, None], (head ^ bit, place,...  46.9 us
    ppermute x18, waiting for transfers between devices, ring(): lax.ppermute(value, DATA, [(i, (i + 1) % count) for i in range(count)])  36.1 us
    ppermute x8, waiting for transfers between devices, shifted(): return lax.ppermute(value, axis, pairs)  21.5 us
    ppermute x8, starting transfers between devices, shifted(): return lax.ppermute(value, axis, pairs)  20.2 us
    ppermute x18, starting transfers between devices, ring(): lax.ppermute(value, DATA, [(i, (i + 1) % count) for i in range(count)])  14.8 us
  transfers between devices with their start and end apart: 165, of which 69 were waited for; matrix products, arithmetic and copies ran while one was open for 21% of the time, Pallas kernels for 0%

profile of v2, /device:TPU:0, one launch (start us, length us, event | category | flops | bytes accessed | tf_op | source)
XLA Modules:
  0.0 548.7 jit_solution(3548189910298062938)
XLA Ops:
  1.8 4.9 collective-permute-start
  25.3 5.4 collective-permute-done.3
  30.9 5.2 collective-permute-done.4
  46.5 4.9 broadcast.35.clone.1
  52.2 5.0 broadcast.35.clone
  64.2 6.8 %collective-permute-done.45 = bf16[1,80,2176]{2,1,0:T(8,128)(2,1)S(1)} collective-permute-done((bf16[1,80,2176]{2,1,0:T(8,128)(2,1)S(1)}, bf16[1,80,2176]{2,1,0:T(8,128)(2,1)S(1)}, u32[]{:S(2)}, u32[]{:S(2)}) %collective-permute-start.45) | collective-permute-done | bytes 348192 | tf_op jit(solution)/shard_map/ppermute | solution.py:22
  91.0 6.1 %collective-permute-done.54 = bf16[1,80,2176]{2,1,0:T(8,128)(2,1)S(1)} collective-permute-done((bf16[1,80,2176]{2,1,0:T(8,128)(2,1)S(1)}, bf16[1,80,2176]{2,1,0:T(8,128)(2,1)S(1)}, u32[]{:S(2)}, u32[]{:S(2)}) %collective-permute-start.54) | collective-permute-done | bytes 348192 | tf_op jit(solution)/shard_map/ppermute | solution.py:22
  124.3 5.3 collective-permute-done.63
  157.5 5.5 %collective-permute-done.72 = bf16[1,80,2176]{2,1,0:T(8,128)(2,1)S(1)} collective-permute-done((bf16[1,80,2176]{2,1,0:T(8,128)(2,1)S(1)}, bf16[1,80,2176]{2,1,0:T(8,128)(2,1)S(1)}, u32[]{:S(2)}, u32[]{:S(2)}) %collective-permute-start.72) | collective-permute-done | bytes 348192 | tf_op jit(solution)/shard_map/ppermute | solution.py:22
  187.2 13.2 %forward.2 = (bf16[256,640]{1,0:T(8,128)(2,1)}, bf16[256,1024]{1,0:T(8,128)(2,1)}, f32[256,640]{1,0:T(8,128)}, f32[256,640]{1,0:T(8,128)}, f32[256,640]{1,0:T(8,128)}) custom-call(bf16[256,640]{1,0:T(8,128)(2,1)} %copy-done.3, bf16[768,512]{1,0:T(8,128)(2,1)} %keys.2.pair_ref, f32[256,768]{1,0:T(8,128)} %fusion.2.bias_ref, f32[256,128]{1,0:T(8,128)} %slice.461.cos_ref, ...), custom_call_target="tpu_custom_call" | custom-call | tf_op jit(solution)/shard_map/forward/pallas_call | solution.py:443
  220.3 13.1 %forward.3 = (bf16[256,640]{1,0:T(8,128)(2,1)}, bf16[256,1024]{1,0:T(8,128)(2,1)}, f32[256,640]{1,0:T(8,128)}, f32[256,640]{1,0:T(8,128)}, f32[256,640]{1,0:T(8,128)}) custom-call(bf16[256,640]{1,0:T(8,128)(2,1)} %get-tuple-element.43.x_ref, bf16[768,512]{1,0:T(8,128)(2,1)} %pad_maximum_fusion.1.pair_ref, f32[256,768]{1,0:T(8,128)} %fusion.2.bias_ref, ...), custom_call_target="tpu_custom_call" | custom-call | tf_op jit(solution)/shard_map/forward/pallas_call | solution.py:443
  233.4 23.1 %backward.2 = (bf16[4,640,2176]{2,1,0:T(8,128)(2,1)}, f32[256,512]{1,0:T(8,128)}, bf16[512,512]{1,0:T(8,128)(2,1)}, f32[256,640]{1,0:T(8,128)}, f32[256,640]{1,0:T(8,128)}, /*index=5*/f32[8,640]{1,0:T(8,128)}) custom-call(bf16[256,640]{1,0:T(8,128)(2,1)} %dynamic-slice_bitcast_fusion.32.dy_ref, bf16[256,640]{1,0:T(8,128)(2,1)} %get-tuple-element.43.x_ref, ...), custom_call_target="tpu_custom_call" | custom-call | tf_op jit(solution)/shard_map/backward/pallas_call | solution.py:443
  269.7 5.8 %closing.2 = (f32[256,640]{1,0:T(8,128)}, f32[8,640]{1,0:T(8,128)}, bf16[4,640,2176]{2,1,0:T(8,128)(2,1)}) custom-call(f32[256,512]{1,0:T(8,128)} %get-tuple-element.49.own_ref, bf16[2,256,512]{2,1,0:T(8,128)(2,1)} %pad_maximum_fusion.2.arrived_ref, bf16[256,640]{1,0:T(8,128)(2,1)} %get-tuple-element.43.x_ref, ...), custom_call_target="tpu_custom_call", output_to_operand_aliasing={{2}: (10, {})} | custom-call | tf_op jit(solution)/shard_map/closing/pallas_call | solution.py:443
  277.3 22.8 %backward.3 = (bf16[4,640,2176]{2,1,0:T(8,128)(2,1)}, f32[256,512]{1,0:T(8,128)}, bf16[512,512]{1,0:T(8,128)(2,1)}, f32[256,640]{1,0:T(8,128)}, f32[256,640]{1,0:T(8,128)}, /*index=5*/f32[8,640]{1,0:T(8,128)}) custom-call(bf16[256,640]{1,0:T(8,128)(2,1)} %convert_element_type.987.dy_ref, bf16[256,640]{1,0:T(8,128)(2,1)} %copy-done.3, ...), custom_call_target="tpu_custom_call" | custom-call | tf_op jit(solution)/shard_map/backward/pallas_call | solution.py:443
  307.5 7.9 %collective-permute-done.82 = bf16[256,512]{1,0:T(8,128)(2,1)S(1)} collective-permute-done((bf16[256,512]{1,0:T(8,128)(2,1)S(1)}, bf16[256,512]{1,0:T(8,128)(2,1)S(1)}, u32[]{:S(2)}, u32[]{:S(2)}) %collective-permute-start.82) | collective-permute-done | bytes 262176 | tf_op jit(solution)/shard_map/ppermute | solution.py:33
  318.7 5.8 %closing.3 = (f32[256,640]{1,0:T(8,128)}, f32[8,640]{1,0:T(8,128)}, bf16[4,640,2176]{2,1,0:T(8,128)(2,1)}) custom-call(f32[256,512]{1,0:T(8,128)} %get-tuple-element.59.own_ref, bf16[2,256,512]{2,1,0:T(8,128)(2,1)} %pad_maximum_fusion.3.arrived_ref, bf16[256,640]{1,0:T(8,128)(2,1)} %copy-done.3, ...), custom_call_target="tpu_custom_call", output_to_operand_aliasing={{2}: (10, {})} | custom-call | tf_op jit(solution)/shard_map/closing/pallas_call | solution.py:443
  327.5 5.8 %collective-permute-start.86 = (f32[4,768]{1,0:T(4,128)S(1)}, f32[4,768]{1,0:T(4,128)S(1)}, u32[]{:S(2)}, u32[]{:S(2)}) collective-permute-start(f32[4,768]{1,0:T(4,128)S(1)} %select_add_fusion), channel_id=1, source_target_pairs={{0,1},{1,0},{2,3},{3,2},{4,5},{5,4},{6,7},{7,6},{8,9},{9,8},{10,11... | collective-permute-start | bytes 36872 | tf_op jit(solution)/shard_map/ppermute | solution.py:22
  363.5 5.0 collective-permute-done.137
  382.6 5.4 collective-permute-done.140
  400.8 5.3 collective-permute-done.118
  406.6 4.8 collective-permute-done.102
  411.9 4.8 collective-permute-done.110
  417.7 6.3 %collective-permute-done.121 = bf16[1,80,1152]{2,1,0:T(8,128)(2,1)S(1)} collective-permute-done((bf16[1,80,1152]{2,1,0:T(8,128)(2,1)S(1)}, bf16[1,80,1152]{2,1,0:T(8,128)(2,1)S(1)}, u32[]{:S(2)}, u32[]{:S(2)}) %collective-permute-start.121) | collective-permute-done | bytes 184352 | tf_op jit(solution)/shard_map/ppermute | solution.py:22
  424.5 6.2 %collective-permute-done.105 = bf16[1,80,1152]{2,1,0:T(8,128)(2,1)S(1)} collective-permute-done((bf16[1,80,1152]{2,1,0:T(8,128)(2,1)S(1)}, bf16[1,80,1152]{2,1,0:T(8,128)(2,1)S(1)}, u32[]{:S(2)}, u32[]{:S(2)}) %collective-permute-start.105) | collective-permute-done | bytes 184352 | tf_op jit(solution)/shard_map/ppermute | solution.py:22
  438.2 6.1 %collective-permute-done.157 = bf16[1,80,2176]{2,1,0:T(8,128)(2,1)S(1)} collective-permute-done((bf16[1,80,2176]{2,1,0:T(8,128)(2,1)S(1)}, bf16[1,80,2176]{2,1,0:T(8,128)(2,1)S(1)}, u32[]{:S(2)}, u32[]{:S(2)}) %collective-permute-start.157) | collective-permute-done | bytes 348192 | tf_op jit(solution)/shard_map/ppermute | solution.py:22
  446.1 5.2 collective-permute-done.129
  451.8 5.1 collective-permute-done.132
  460.0 7.7 %collective-permute-done.122 = bf16[1,80,2176]{2,1,0:T(8,128)(2,1)S(1)} collective-permute-done((bf16[1,80,2176]{2,1,0:T(8,128)(2,1)S(1)}, bf16[1,80,2176]{2,1,0:T(8,128)(2,1)S(1)}, u32[]{:S(2)}, u32[]{:S(2)}) %collective-permute-start.122) | collective-permute-done | bytes 348192 | tf_op jit(solution)/shard_map/ppermute | solution.py:22
  471.7 5.2 collective-permute-done.158
  478.0 4.8 collective-permute-done.94
  490.9 6.7 %collective-permute-done.123 = bf16[1,80,2176]{2,1,0:T(8,128)(2,1)S(1)} collective-permute-done((bf16[1,80,2176]{2,1,0:T(8,128)(2,1)S(1)}, bf16[1,80,2176]{2,1,0:T(8,128)(2,1)S(1)}, u32[]{:S(2)}, u32[]{:S(2)}) %collective-permute-start.123) | collective-permute-done | bytes 348192 | tf_op jit(solution)/shard_map/ppermute | solution.py:27
  501.6 5.6 %collective-permute-done.159 = bf16[1,80,2176]{2,1,0:T(8,128)(2,1)S(1)} collective-permute-done((bf16[1,80,2176]{2,1,0:T(8,128)(2,1)S(1)}, bf16[1,80,2176]{2,1,0:T(8,128)(2,1)S(1)}, u32[]{:S(2)}, u32[]{:S(2)}) %collective-permute-start.159) | collective-permute-done | bytes 348192 | tf_op jit(solution)/shard_map/ppermute | solution.py:27
  (611 shorter events, 314.8 us)
Async XLA Ops:
  1.8 42.7 %collective-permute-start = (bf16[256,640]{1,0:T(8,128)(2,1)S(1)}, bf16[256,640]{1,0:T(8,128)(2,1)S(1)}, u32[]{:S(2)}, u32[]{:S(2)}) collective-permute-start(bf16[256,640]{1,0:T(8,128)(2,1)S(1)} %dynamic-slice_bitcast_fusion.33.x_ref), channel_id=1, source_target_pairs={{0,2},{1,3},{4,6},{5,7},{8,10},{9,11},{12,14},{13,15},{16,18},{17,... | collective-permute-start | bytes 983048 | tf_op jit(solution)/shard_map/ppermute | solution.py:33
  6.7 37.8 %collective-permute-start.1 = (bf16[256,640]{1,0:T(8,128)(2,1)S(1)}, bf16[256,640]{1,0:T(8,128)(2,1)S(1)}, u32[]{:S(2)}, u32[]{:S(2)}) collective-permute-start(bf16[256,640]{1,0:T(8,128)(2,1)S(1)} %dynamic-slice_bitcast_fusion.33.x_ref), channel_id=1, source_target_pairs={{0,1},{1,2},{2,3},{4,5},{5,6},{6,7},{8,9},{9,10},{10,11},{12,13},{... | collective-permute-start | bytes 983048 | tf_op jit(solution)/shard_map/ppermute | solution.py:33
  15.6 30.0 %collective-permute-start.6 = (bf16[80,2176]{1,0:T(8,128)(2,1)S(1)}, bf16[80,2176]{1,0:T(8,128)(2,1)S(1)}, u32[]{:S(2)}, u32[]{:S(2)}) collective-permute-start(bf16[80,2176]{1,0:T(8,128)(2,1)S(1)} %broadcast_select_fusion.3), channel_id=1, source_target_pairs={{0,16},{16,0},{1,17},{17,1},{2,18},{18,2},{3,19},{19,3},{4,20},{20... | collective-permute-start | bytes 1044488 | tf_op jit(solution)/shard_map/ppermute | solution.py:22
  46.2 17.2 %collective-permute-start.8 = (bf16[1,80,2176]{2,1,0:T(8,128)(2,1)S(1)}, bf16[1,80,2176]{2,1,0:T(8,128)(2,1)S(1)}, u32[]{:S(2)}, u32[]{:S(2)}) collective-permute-start(bf16[1,80,2176]{2,1,0:T(8,128)(2,1)S(1)} %get-tuple-element.156), channel_id=1, source_target_pairs={{0,1},{1,0},{2,3},{3,2},{4,5},{5,4},{6,7},{7,6},{8,9},{9,8},{10,11... | collective-permute-start | bytes 1044488 | tf_op jit(solution)/shard_map/ppermute | solution.py:22
  46.2 17.2 %collective-permute-start.10 = (bf16[1,80,2176]{2,1,0:T(8,128)(2,1)S(1)}, bf16[1,80,2176]{2,1,0:T(8,128)(2,1)S(1)}, u32[]{:S(2)}, u32[]{:S(2)}) collective-permute-start(bf16[1,80,2176]{2,1,0:T(8,128)(2,1)S(1)} %get-tuple-element.156), channel_id=1, source_target_pairs={{0,2},{1,3},{2,0},{3,1},{4,6},{5,7},{6,4},{7,5},{8,10},{9,11},{10,... | collective-permute-start | bytes 1044488 | tf_op jit(solution)/shard_map/ppermute | solution.py:22
  46.2 32.4 %collective-permute-start.15 = (bf16[1,80,2176]{2,1,0:T(8,128)(2,1)S(1)}, bf16[1,80,2176]{2,1,0:T(8,128)(2,1)S(1)}, u32[]{:S(2)}, u32[]{:S(2)}) collective-permute-start(bf16[1,80,2176]{2,1,0:T(8,128)(2,1)S(1)} %get-tuple-element.156), channel_id=1, source_target_pairs={{0,4},{4,8},{8,12},{12,0},{1,5},{5,9},{9,13},{13,1},{2,6},{6,10},{... | collective-permute-start | bytes 1044488 | tf_op jit(solution)/shard_map/ppermute | solution.py:27
  58.1 14.8 %collective-permute-start.43 = (bf16[1,80,2176]{2,1,0:T(8,128)(2,1)S(1)}, bf16[1,80,2176]{2,1,0:T(8,128)(2,1)S(1)}, u32[]{:S(2)}, u32[]{:S(2)}) collective-permute-start(bf16[1,80,2176]{2,1,0:T(8,128)(2,1)S(1)} %get-tuple-element.155), channel_id=1, source_target_pairs={{0,1},{1,0},{2,3},{3,2},{4,5},{5,4},{6,7},{7,6},{8,9},{9,8},{10,11... | collective-permute-start | bytes 1044488 | tf_op jit(solution)/shard_map/ppermute | solution.py:22
  63.3 20.1 %collective-permute-start.50 = (bf16[1,80,2176]{2,1,0:T(8,128)(2,1)S(1)}, bf16[1,80,2176]{2,1,0:T(8,128)(2,1)S(1)}, u32[]{:S(2)}, u32[]{:S(2)}) collective-permute-start(bf16[1,80,2176]{2,1,0:T(8,128)(2,1)S(1)} %get-tuple-element.155), channel_id=1, source_target_pairs={{0,4},{4,8},{8,12},{12,0},{1,5},{5,9},{9,13},{13,1},{2,6},{6,10},{... | collective-permute-start | bytes 1044488 | tf_op jit(solution)/shard_map/ppermute | solution.py:27
  91.0 19.5 %collective-permute-start.24 = (bf16[1,80,2176]{2,1,0:T(8,128)(2,1)S(1)}, bf16[1,80,2176]{2,1,0:T(8,128)(2,1)S(1)}, u32[]{:S(2)}, u32[]{:S(2)}) collective-permute-start(bf16[1,80,2176]{2,1,0:T(8,128)(2,1)S(1)} %collective-permute-done.15), channel_id=1, source_target_pairs={{0,4},{4,8},{8,12},{12,0},{1,5},{5,9},{9,13},{13,1},{2,6},{6,10},{... | collective-permute-start | bytes 1044488 | tf_op jit(solution)/shard_map/ppermute | solution.py:27
  97.2 17.8 %collective-permute-start.59 = (bf16[1,80,2176]{2,1,0:T(8,128)(2,1)S(1)}, bf16[1,80,2176]{2,1,0:T(8,128)(2,1)S(1)}, u32[]{:S(2)}, u32[]{:S(2)}) collective-permute-start(bf16[1,80,2176]{2,1,0:T(8,128)(2,1)S(1)} %collective-permute-done.50), channel_id=1, source_target_pairs={{0,4},{4,8},{8,12},{12,0},{1,5},{5,9},{9,13},{13,1},{2,6},{6,10},{... | collective-permute-start | bytes 1044488 | tf_op jit(solution)/shard_map/ppermute | solution.py:27
  123.5 20.9 %collective-permute-start.33 = (bf16[1,80,2176]{2,1,0:T(8,128)(2,1)S(1)}, bf16[1,80,2176]{2,1,0:T(8,128)(2,1)S(1)}, u32[]{:S(2)}, u32[]{:S(2)}) collective-permute-start(bf16[1,80,2176]{2,1,0:T(8,128)(2,1)S(1)} %collective-permute-done.24), channel_id=1, source_target_pairs={{0,4},{4,8},{8,12},{12,0},{1,5},{5,9},{9,13},{13,1},{2,6},{6,10},{... | collective-permute-start | bytes 1044488 | tf_op jit(solution)/shard_map/ppermute | solution.py:27
  129.7 18.7 %collective-permute-start.68 = (bf16[1,80,2176]{2,1,0:T(8,128)(2,1)S(1)}, bf16[1,80,2176]{2,1,0:T(8,128)(2,1)S(1)}, u32[]{:S(2)}, u32[]{:S(2)}) collective-permute-start(bf16[1,80,2176]{2,1,0:T(8,128)(2,1)S(1)} %collective-permute-done.59), channel_id=1, source_target_pairs={{0,4},{4,8},{8,12},{12,0},{1,5},{5,9},{9,13},{13,1},{2,6},{6,10},{... | collective-permute-start | bytes 1044488 | tf_op jit(solution)/shard_map/ppermute | solution.py:27
  156.9 15.0 %collective-permute-start.69 = (bf16[1,80,2176]{2,1,0:T(8,128)(2,1)S(1)}, bf16[1,80,2176]{2,1,0:T(8,128)(2,1)S(1)}, u32[]{:S(2)}, u32[]{:S(2)}) collective-permute-start(bf16[1,80,2176]{2,1,0:T(8,128)(2,1)S(1)} %collective-permute-done.68), channel_id=1, source_target_pairs={{0,16},{16,0},{1,17},{17,1},{2,18},{18,2},{3,19},{19,3},{4,20},{20... | collective-permute-start | bytes 1044488 | tf_op jit(solution)/shard_map/ppermute | solution.py:22
  203.9 14.6 %collective-permute-start.77 = (bf16[256,512]{1,0:T(8,128)(2,1)}, bf16[256,512]{1,0:T(8,128)(2,1)S(1)}, u32[]{:S(2)}, u32[]{:S(2)}) collective-permute-start(bf16[256,512]{1,0:T(8,128)(2,1)} %keys.3), channel_id=1, source_target_pairs={{0,2},{1,3},{4,6},{5,7},{8,10},{9,11},{12,14},{13,15},{16,18},{17,... | collective-permute-start | bytes 786440 | tf_op jit(solution)/shard_map/ppermute | solution.py:33
  302.5 15.3 %collective-permute-start.83 = (bf16[256,512]{1,0:T(8,128)(2,1)S(1)}, bf16[256,512]{1,0:T(8,128)(2,1)S(1)}, u32[]{:S(2)}, u32[]{:S(2)}) collective-permute-start(bf16[256,512]{1,0:T(8,128)(2,1)S(1)} %get-tuple-element.160), channel_id=1, source_target_pairs={{2,0},{3,1},{6,4},{7,5},{10,8},{11,9},{14,12},{15,13},{18,16},{19,... | collective-permute-start | bytes 786440 | tf_op jit(solution)/shard_map/ppermute | solution.py:33
  360.0 33.6 %collective-permute-start.100 = (bf16[1,80,2176]{2,1,0:T(8,128)(2,1)S(1)}, bf16[1,80,2176]{2,1,0:T(8,128)(2,1)S(1)}, u32[]{:S(2)}, u32[]{:S(2)}) collective-permute-start(bf16[1,80,2176]{2,1,0:T(8,128)(2,1)S(1)} %get-tuple-element.128), channel_id=1, source_target_pairs={{0,16},{16,0},{1,17},{17,1},{2,18},{18,2},{3,19},{19,3},{4,20},{20... | collective-permute-start | bytes 1044488 | tf_op jit(solution)/shard_map/ppermute | solution.py:22
  360.2 34.0 %collective-permute-start.101 = (bf16[1,80,2176]{2,1,0:T(8,128)(2,1)S(1)}, bf16[1,80,2176]{2,1,0:T(8,128)(2,1)S(1)}, u32[]{:S(2)}, u32[]{:S(2)}) collective-permute-start(bf16[1,80,2176]{2,1,0:T(8,128)(2,1)S(1)} %get-tuple-element.127), channel_id=1, source_target_pairs={{0,16},{16,0},{1,17},{17,1},{2,18},{18,2},{3,19},{19,3},{4,20},{20... | collective-permute-start | bytes 1044488 | tf_op jit(solution)/shard_map/ppermute | solution.py:22
  360.6 33.7 %collective-permute-start.104 = (bf16[1,80,2176]{2,1,0:T(8,128)(2,1)S(1)}, bf16[1,80,2176]{2,1,0:T(8,128)(2,1)S(1)}, u32[]{:S(2)}, u32[]{:S(2)}) collective-permute-start(bf16[1,80,2176]{2,1,0:T(8,128)(2,1)S(1)} %get-tuple-element.126), channel_id=1, source_target_pairs={{0,16},{16,0},{1,17},{17,1},{2,18},{18,2},{3,19},{19,3},{4,20},{20... | collective-permute-start | bytes 1044488 | tf_op jit(solution)/shard_map/ppermute | solution.py:22
  360.8 34.0 %collective-permute-start.108 = (bf16[1,80,2176]{2,1,0:T(8,128)(2,1)S(1)}, bf16[1,80,2176]{2,1,0:T(8,128)(2,1)S(1)}, u32[]{:S(2)}, u32[]{:S(2)}) collective-permute-start(bf16[1,80,2176]{2,1,0:T(8,128)(2,1)S(1)} %get-tuple-element.124), channel_id=1, source_target_pairs={{0,16},{16,0},{1,17},{17,1},{2,18},{18,2},{3,19},{19,3},{4,20},{20... | collective-permute-start | bytes 1044488 | tf_op jit(solution)/shard_map/ppermute | solution.py:22
  395.7 41.0 %collective-permute-start.128 = (bf16[1,80,2176]{2,1,0:T(8,128)(2,1)S(1)}, bf16[1,80,2176]{2,1,0:T(8,128)(2,1)S(1)}, u32[]{:S(2)}, u32[]{:S(2)}) collective-permute-start(bf16[1,80,2176]{2,1,0:T(8,128)(2,1)S(1)} %get-tuple-element.102), channel_id=1, source_target_pairs={{0,16},{16,0},{1,17},{17,1},{2,18},{18,2},{3,19},{19,3},{4,20},{20... | collective-permute-start | bytes 1044488 | tf_op jit(solution)/shard_map/ppermute | solution.py:22
  396.2 40.6 %collective-permute-start.131 = (bf16[1,80,2176]{2,1,0:T(8,128)(2,1)S(1)}, bf16[1,80,2176]{2,1,0:T(8,128)(2,1)S(1)}, u32[]{:S(2)}, u32[]{:S(2)}) collective-permute-start(bf16[1,80,2176]{2,1,0:T(8,128)(2,1)S(1)} %get-tuple-element.101), channel_id=1, source_target_pairs={{0,16},{16,0},{1,17},{17,1},{2,18},{18,2},{3,19},{19,3},{4,20},{20... | collective-permute-start | bytes 1044488 | tf_op jit(solution)/shard_map/ppermute | solution.py:22
  396.7 40.6 %collective-permute-start.150 = (bf16[1,80,2176]{2,1,0:T(8,128)(2,1)S(1)}, bf16[1,80,2176]{2,1,0:T(8,128)(2,1)S(1)}, u32[]{:S(2)}, u32[]{:S(2)}) collective-permute-start(bf16[1,80,2176]{2,1,0:T(8,128)(2,1)S(1)} %get-tuple-element.92), channel_id=1, source_target_pairs={{0,16},{16,0},{1,17},{17,1},{2,18},{18,2},{3,19},{19,3},{4,20},{20... | collective-permute-start | bytes 1044488 | tf_op jit(solution)/shard_map/ppermute | solution.py:22
  397.2 40.2 %collective-permute-start.154 = (bf16[1,80,2176]{2,1,0:T(8,128)(2,1)S(1)}, bf16[1,80,2176]{2,1,0:T(8,128)(2,1)S(1)}, u32[]{:S(2)}, u32[]{:S(2)}) collective-permute-start(bf16[1,80,2176]{2,1,0:T(8,128)(2,1)S(1)} %pad_maximum_fusion.18), channel_id=1, source_target_pairs={{0,1},{1,0},{2,3},{3,2},{4,5},{5,4},{6,7},{7,6},{8,9},{9,8},{10,11... | collective-permute-start | bytes 1044488 | tf_op jit(solution)/shard_map/ppermute | solution.py:22
  436.7 20.2 %collective-permute-start.115 = (bf16[1,80,2176]{2,1,0:T(8,128)(2,1)S(1)}, bf16[1,80,2176]{2,1,0:T(8,128)(2,1)S(1)}, u32[]{:S(2)}, u32[]{:S(2)}) collective-permute-start(bf16[1,80,2176]{2,1,0:T(8,128)(2,1)S(1)} %get-tuple-element.121), channel_id=1, source_target_pairs={{0,16},{16,0},{1,17},{17,1},{2,18},{18,2},{3,19},{19,3},{4,20},{20... | collective-permute-start | bytes 1044488 | tf_op jit(solution)/shard_map/ppermute | solution.py:22
  436.8 20.2 %collective-permute-start.93 = (bf16[1,80,2176]{2,1,0:T(8,128)(2,1)S(1)}, bf16[1,80,2176]{2,1,0:T(8,128)(2,1)S(1)}, u32[]{:S(2)}, u32[]{:S(2)}) collective-permute-start(bf16[1,80,2176]{2,1,0:T(8,128)(2,1)S(1)} %get-tuple-element.131), channel_id=1, source_target_pairs={{0,16},{16,0},{1,17},{17,1},{2,18},{18,2},{3,19},{19,3},{4,20},{20... | collective-permute-start | bytes 1044488 | tf_op jit(solution)/shard_map/ppermute | solution.py:22
  437.3 20.2 %collective-permute-start.96 = (bf16[1,80,2176]{2,1,0:T(8,128)(2,1)S(1)}, bf16[1,80,2176]{2,1,0:T(8,128)(2,1)S(1)}, u32[]{:S(2)}, u32[]{:S(2)}) collective-permute-start(bf16[1,80,2176]{2,1,0:T(8,128)(2,1)S(1)} %get-tuple-element.130), channel_id=1, source_target_pairs={{0,16},{16,0},{1,17},{17,1},{2,18},{18,2},{3,19},{19,3},{4,20},{20... | collective-permute-start | bytes 1044488 | tf_op jit(solution)/shard_map/ppermute | solution.py:22
  437.4 20.5 %collective-permute-start.119 = (bf16[1,80,2176]{2,1,0:T(8,128)(2,1)S(1)}, bf16[1,80,2176]{2,1,0:T(8,128)(2,1)S(1)}, u32[]{:S(2)}, u32[]{:S(2)}) collective-permute-start(bf16[1,80,2176]{2,1,0:T(8,128)(2,1)S(1)} %pad_maximum_fusion.10), channel_id=1, source_target_pairs={{0,1},{1,0},{2,3},{3,2},{4,5},{5,4},{6,7},{7,6},{8,9},{9,8},{10,11... | collective-permute-start | bytes 1044488 | tf_op jit(solution)/shard_map/ppermute | solution.py:22
  457.1 42.4 %collective-permute-start.134 = (bf16[1,80,2176]{2,1,0:T(8,128)(2,1)S(1)}, bf16[1,80,2176]{2,1,0:T(8,128)(2,1)S(1)}, u32[]{:S(2)}, u32[]{:S(2)}) collective-permute-start(bf16[1,80,2176]{2,1,0:T(8,128)(2,1)S(1)} %get-tuple-element.100), channel_id=1, source_target_pairs={{0,16},{16,0},{1,17},{17,1},{2,18},{18,2},{3,19},{19,3},{4,20},{20... | collective-permute-start | bytes 1044488 | tf_op jit(solution)/shard_map/ppermute | solution.py:22
  468.6 20.0 %collective-permute-start.107 = (bf16[1,80,2176]{2,1,0:T(8,128)(2,1)S(1)}, bf16[1,80,2176]{2,1,0:T(8,128)(2,1)S(1)}, u32[]{:S(2)}, u32[]{:S(2)}) collective-permute-start(bf16[1,80,2176]{2,1,0:T(8,128)(2,1)S(1)} %get-tuple-element.125), channel_id=1, source_target_pairs={{0,16},{16,0},{1,17},{17,1},{2,18},{18,2},{3,19},{19,3},{4,20},{20... | collective-permute-start | bytes 1044488 | tf_op jit(solution)/shard_map/ppermute | solution.py:22
  468.7 20.0 %collective-permute-start.111 = (bf16[1,80,2176]{2,1,0:T(8,128)(2,1)S(1)}, bf16[1,80,2176]{2,1,0:T(8,128)(2,1)S(1)}, u32[]{:S(2)}, u32[]{:S(2)}) collective-permute-start(bf16[1,80,2176]{2,1,0:T(8,128)(2,1)S(1)} %pad_maximum_fusion.8), channel_id=1, source_target_pairs={{0,1},{1,0},{2,3},{3,2},{4,5},{5,4},{6,7},{7,6},{8,9},{9,8},{10,11... | collective-permute-start | bytes 1044488 | tf_op jit(solution)/shard_map/ppermute | solution.py:22
  471.6 18.6 %collective-permute-start.114 = (bf16[1,80,2176]{2,1,0:T(8,128)(2,1)S(1)}, bf16[1,80,2176]{2,1,0:T(8,128)(2,1)S(1)}, u32[]{:S(2)}, u32[]{:S(2)}) collective-permute-start(bf16[1,80,2176]{2,1,0:T(8,128)(2,1)S(1)} %pad_maximum_fusion.9), channel_id=1, source_target_pairs={{0,2},{1,3},{2,0},{3,1},{4,6},{5,7},{6,4},{7,5},{8,10},{9,11},{10,... | collective-permute-start | bytes 1044488 | tf_op jit(solution)/shard_map/ppermute | solution.py:22
  488.6 30.1 %collective-permute-start.126 = (bf16[1,80,2176]{2,1,0:T(8,128)(2,1)S(1)}, bf16[1,80,2176]{2,1,0:T(8,128)(2,1)S(1)}, u32[]{:S(2)}, u32[]{:S(2)}) collective-permute-start(bf16[1,80,2176]{2,1,0:T(8,128)(2,1)S(1)} %get-tuple-element.88), channel_id=1, source_target_pairs={{0,16},{16,0},{1,17},{17,1},{2,18},{18,2},{3,19},{19,3},{4,20},{20... | collective-permute-start | bytes 1044488 | tf_op jit(solution)/shard_map/ppermute | solution.py:22
  (147 other events, 1438.5 us)

commit v3 on v2

v3 whole, which is shorter than its diff:
```python
import functools

import jax
import jax.numpy as jnp
from jax import lax
from jax.experimental import pallas as pl
from jax.experimental.pallas import tpu as pltpu
from jax.sharding import PartitionSpec as P

WINDOW = 512
EPSILON = 1e-06
LOW = jnp.bfloat16
WIDE = jnp.float32
SECTION = "section"
DATA = "fsdp"
HEAD = "tensor"
CORES = 2
HEADS = 4
VMEM_BYTES = 56 * 1024 * 1024


def flip(value, axis, bit):
    count = lax.axis_size(axis)
    return lax.ppermute(value, axis, [(i, i ^ bit) for i in range(count)])


def ring(value):
    count = lax.axis_size(DATA)
    return lax.ppermute(value, DATA, [(i, (i + 1) % count) for i in range(count)])


def shifted(value, axis, by):
    count = lax.axis_size(axis)
    pairs = [(i, i + by) for i in range(count) if 0 <= i + by < count]
    return lax.ppermute(value, axis, pairs)


def add(*parts):
    total = parts[0].astype(WIDE)
    for part in parts[1:]:
        total = total + part.astype(WIDE)
    return total


def dot(left, right):
    return jnp.dot(left, right, preferred_element_type=WIDE)


def dot_nt(left, right):
    return lax.dot_general(left, right, (((1,), (1,)), ((), ())), preferred_element_type=WIDE)


def dot_tn(left, right):
    return lax.dot_general(left, right, (((0,), (0,)), ((), ())), preferred_element_type=WIDE)


def after(value, *others):
    anywhere = pl.BlockSpec(memory_space=pl.ANY)
    return pl.pallas_call(
        lambda *refs: None,
        name="after",
        out_shape=jax.ShapeDtypeStruct(value.shape, value.dtype),
        in_specs=[anywhere] * (1 + len(others)),
        out_specs=anywhere,
        input_output_aliases={0: 0},
    )(value, *others)


def gather_slab(slab):
    ranks = lax.axis_size(DATA)
    if ranks > 4:
        rows, columns = slab.shape
        chunk = lax.all_gather(slab, DATA, axis=0, tiled=False)
        near = flip(chunk, HEAD, 1)
        far = flip(chunk, HEAD, 2)
        piece = jnp.stack([chunk, near, far, flip(near, HEAD, 2)])
        both = jnp.stack(by_section(piece, flip(piece, SECTION, 1)), axis=2)
        return (both.reshape(HEADS, ranks * CORES * rows, columns),), [chunk] * 4
    pieces = ()
    chunks = [slab]
    for step in range(ranks):
        chunk = chunks[-1]
        if step < ranks - 1:
            chunks.append(ring(chunk))
        near = flip(chunk, HEAD, 1)
        far = flip(chunk, HEAD, 2)
        across = flip(far, HEAD, 1) if 2 * step < ranks else flip(near, HEAD, 2)
        own = jnp.stack([chunk, near, far, across])
        pieces += (own, flip(own, SECTION, 1))
    return pieces, chunks


def groups_of(ranks):
    return ((2, 3), (1, 0)) if ranks == 4 else (tuple(range(ranks - 1, -1, -1)),)


def first_sums(grads, ranks):
    if ranks > 4:
        section = lax.axis_index(SECTION)
        whole = jnp.concatenate(grads, axis=-1)
        rows = whole.shape[2] // (CORES * ranks)
        whole = whole.reshape(HEADS, ranks, CORES, rows, whole.shape[3])
        own = lax.dynamic_index_in_dim(whole, section, 2, keepdims=False)
        other = lax.dynamic_index_in_dim(whole, 1 - section, 2, keepdims=False)
        return [add(own, flip(other, SECTION, 1)).astype(LOW)]
    sums = []
    count = len(groups_of(ranks))
    own_pair, other_pair = grads[2 * count :]
    other_pair = flip(other_pair, SECTION, 1)
    first = 0
    for index, group in enumerate(groups_of(ranks)):
        own, other = grads[2 * index], grads[2 * index + 1]
        span = slice(first, first + len(group))
        first += len(group)
        sums.append(
            jnp.concatenate(
                [
                    add(own, flip(other, SECTION, 1)).astype(LOW),
                    add(own_pair[:, span], other_pair[:, span]).astype(LOW),
                ],
                axis=-1,
            )
        )
    return sums


def scatter_sums(sums, ranks):
    if ranks > 4:
        part = sums[0]
        part = add(part[:2], flip(part[2:], HEAD, 2))
        total = add(part[0], flip(part[1].astype(LOW), HEAD, 1))
        total = lax.psum_scatter(total.astype(LOW), DATA, scatter_dimension=0, tiled=False)
        return total.astype(WIDE), total
    kept = None
    mark = None
    for part, group in zip(sums, groups_of(ranks)):
        middle = len(group) // 2
        upper = flip(part[3, :middle], HEAD, 1)
        lower = flip(part[3, middle:], HEAD, 2)
        far = jnp.concatenate([add(part[2, :middle], upper).astype(LOW), part[2, middle:]])
        near = jnp.concatenate([part[1, :middle], add(part[1, middle:], lower).astype(LOW)])
        mark = near if mark is None else mark
        total = add(part[0], flip(near, HEAD, 1), flip(far, HEAD, 2))
        for place, distance in enumerate(group):
            piece = total[place]
            if distance:
                pairs = [(i, (i + distance) % ranks) for i in range(ranks)]
                piece = lax.ppermute(piece.astype(LOW), DATA, pairs)
            kept = piece.astype(WIDE) if kept is None else add(kept, piece)
    return kept, mark


def by_section(own, other):
    section = lax.axis_index(SECTION)
    return jnp.where(section == 0, own, other), jnp.where(section == 0, other, own)


def gather_gains(gains):
    ranks = lax.axis_size(DATA)
    data = lax.axis_index(DATA)
    if ranks > 4:
        full = lax.all_gather(gains, DATA, axis=0, tiled=False)
    else:
        full = jnp.zeros((ranks,) + gains.shape, gains.dtype)
        for step in range(ranks):
            full = lax.dynamic_update_slice(full, gains[None], ((data - step) % ranks, 0))
            if step < ranks - 1:
                gains = ring(gains)
    return by_section(full, flip(full, SECTION, 1))


def scatter_gains(first, second):
    ranks = lax.axis_size(DATA)
    data = lax.axis_index(DATA)
    own, sent = by_section(first, second)
    total = own + flip(sent, SECTION, 1)
    total = total + flip(total, HEAD, 1)
    total = total + flip(total, HEAD, 2)
    if ranks > 4:
        return lax.psum_scatter(total, DATA, scatter_dimension=0, tiled=False)
    arriving = None
    for step in range(ranks):
        kept = lax.dynamic_index_in_dim(total, (data - 1 - step) % ranks, 0, keepdims=False)
        if arriving is not None:
            kept = kept + arriving
        if step < ranks - 1:
            arriving = ring(kept)
    return kept


def norm_parts(value_rows):
    scale = lax.rsqrt(jnp.mean(value_rows * value_rows, axis=-1, keepdims=True) + EPSILON)
    return value_rows * scale, scale


def norm_rows(value_rows, gain_value):
    return norm_parts(value_rows)[0] * gain_value


def norm_back(value_rows, gain_value, cotangent):
    unit, scale = norm_parts(value_rows)
    weighted = cotangent * gain_value
    rows_grad = scale * (weighted - unit * jnp.mean(weighted * unit, axis=-1, keepdims=True))
    return rows_grad, jnp.sum(cotangent * unit, axis=0, keepdims=True)


def rotate(value_rows, cosine, sine):
    half_depth = value_rows.shape[-1] // 2
    first = value_rows[:, :half_depth]
    second = value_rows[:, half_depth:]
    return jnp.concatenate(
        [first * cosine - second * sine, second * cosine + first * sine], axis=-1
    )


def gelu_parts(gate):
    root = 0.7978845608028654
    tanh = jnp.tanh(root * (gate + 0.044715 * gate * gate * gate))
    value = 0.5 * gate * (1.0 + tanh)
    slope = 0.5 * (1.0 + tanh) + 0.5 * gate * (1.0 - tanh * tanh) * root * (
        1.0 + 3.0 * 0.044715 * gate * gate
    )
    return value, slope


def softmax(scores):
    exponent = jnp.exp(scores - jnp.max(scores, axis=-1, keepdims=True))
    return exponent / jnp.sum(exponent, axis=-1, keepdims=True)


def row_table(ranks, depth):
    section = lax.axis_index(SECTION)
    data = lax.axis_index(DATA)
    head = lax.axis_index(HEAD)
    half = depth // CORES
    cores = (section, 1 - section)
    if ranks > 4:
        rows = [jnp.int32(0)] * 3
    else:
        rows = [(data - k) % ranks * depth + core * half for k in range(ranks) for core in cores]
        groups = groups_of(ranks)
        order = [(group, core) for group in groups for core in cores]
        order += [(sum(groups, ()), core) for core in cores]
        for group, core in order:
            rows += [(data + k) % ranks * depth + core * half for k in group]
    return jnp.stack([jnp.int32(row) for row in rows] + [head ^ bit for bit in range(HEADS)])


def fetches(table, pieces, bit, source, target, sems):
    copies = []
    for i, piece in enumerate(pieces):
        rows = piece.shape[1]
        first = pl.multiple_of(table[i], 16)
        copies.append(
            pltpu.make_async_copy(
                piece.at[bit, :, pl.ds(*source)],
                target(pl.ds(first, rows)),
                sems.at[bit * len(pieces) + i],
            )
        )
        copies[-1].start()
    return copies


def sendings(table, first_entry, grads, bit, source, columns, sems):
    copies = []
    for grad in grads:
        for place in range(grad.shape[1]):
            rows = grad.shape[2]
            first = pl.multiple_of(table[first_entry + len(copies)], 16)
            copies.append(
                pltpu.make_async_copy(
                    source(pl.ds(first, rows)),
                    grad.at[bit, place, :, pl.ds(*columns)],
                    sems.at[len(copies)],
                )
            )
            copies[-1].start()
    return copies


def quarter_columns(table, bit, quarter):
    last = table.shape[0] - HEADS + bit
    return pl.ds(pl.multiple_of(table[last] * quarter, quarter), quarter)


def keys_kernel(count, table, x_ref, gain_ref, key_gain_ref, cos_ref, sin_ref, *refs):
    pieces = refs[:count]
    pair_ref, weights, sems = refs[count:]
    width_pair = pair_ref.shape[1]
    quarter = width_pair // HEADS
    copies = []
    for t in range(HEADS):
        columns = quarter_columns(table, t, quarter)
        copies += fetches(
            table, pieces, t, (width_pair, quarter), lambda rows: weights.at[rows, columns], sems
        )
    normed = norm_rows(x_ref[...].astype(WIDE), gain_ref[...]).astype(LOW)
    for copy in copies:
        copy.wait()
    pair = dot(normed, weights[...])
    half = width_pair // 2
    key = rotate(norm_rows(pair[:, :half], key_gain_ref[...]), cos_ref[...], sin_ref[...])
    pair_ref[:, :half] = key.astype(LOW)
    pair_ref[:, half:] = pair[:, half:].astype(LOW)


def fetch_attn(table, pieces, attn, sems):
    return [
        fetches(table, pieces, t, (0, attn.shape[2]), lambda rows: attn.at[t, rows, :], sems)
        for t in range(HEADS)
    ]


def fetch_feed(table, pieces, feed, sems):
    first = pieces[0].shape[2] - feed.shape[2]
    return [
        fetches(table, pieces, t, (first, feed.shape[2]), lambda rows: feed.at[t, rows, :], sems)
        for t in range(HEADS)
    ]


def wait_all(copies):
    for copy in copies:
        copy.wait()


def forward_kernel(
    count, table,
    x_ref, pair_ref, bias_ref, cos_ref, sin_ref, before_ref, query_gain_ref, after_ref,
    feed_gain_ref, final_ref, *refs,
):
    pieces = refs[:count]
    result_ref, attended_ref, sum_ref, hidden_ref, branch_ref, attn, feed, first_sems, second_sems = (
        refs[count:]
    )
    width = pair_ref.shape[1] // 2
    hidden_width = feed.shape[2] // 3
    scale = width ** (-0.5)
    first = fetch_attn(table, pieces, attn, first_sems)
    second = fetch_feed(table, pieces, feed, second_sems)
    x = x_ref[...].astype(WIDE)
    cosine, sine, bias = cos_ref[...], sin_ref[...], bias_ref[...]
    normed = norm_rows(x, before_ref[...]).astype(LOW)
    for t in range(HEADS):
        wait_all(first[t])
        raw = dot(normed, attn[t, :, :width])
        query = rotate(norm_rows(raw, query_gain_ref[...]), cosine, sine).astype(LOW)
        chance = softmax(dot_nt(query, pair_ref[:, :width]) * scale + bias).astype(LOW)
        mixed = dot(chance, pair_ref[:, width:]).astype(LOW)
        attended_ref[:, t * width : (t + 1) * width] = mixed
        part = dot_nt(mixed, attn[t, :, width:])
        sum_ref[...] = part if t == 0 else sum_ref[...] + part
    hidden = x + norm_rows(sum_ref[...], after_ref[...])
    hidden_ref[...] = hidden
    feed_in = norm_rows(hidden, feed_gain_ref[...]).astype(LOW)
    for t in range(HEADS):
        wait_all(second[t])
        gate = dot(feed_in, feed[t, :, :hidden_width])
        up = dot(feed_in, feed[t, :, hidden_width : 2 * hidden_width])
        product = (gelu_parts(gate)[0] * up).astype(LOW)
        part = dot_nt(product, feed[t, :, 2 * hidden_width :])
        branch_ref[...] = part if t == 0 else branch_ref[...] + part
    result = hidden_ref[...] + norm_rows(branch_ref[...], final_ref[...])
    result_ref[...] = result.astype(LOW)


def backward_kernel(
    count, grad_count, table,
    dy_ref, x_ref, pair_ref, bias_ref, cos_ref, sin_ref, before_ref, query_gain_ref, after_ref,
    feed_gain_ref, final_ref, attended_ref, sum_ref, hidden_ref, branch_ref, *refs,
):
    pieces = refs[:count]
    grads = refs[count : count + grad_count]
    own_ref, sent_ref, normed_ref, d_hidden_ref, gains_ref = refs[
        count + grad_count : count + grad_count + 5
    ]
    attn, feed, grad_attn, grad_feed, d_pair, first_sems, second_sems, *out_sems = refs[
        count + grad_count + 5 :
    ]
    entry = len(pieces)
    width = pair_ref.shape[1] // 2
    hidden_width = feed.shape[2] // 3
    rows = x_ref.shape[0]
    scale = width ** (-0.5)
    second = fetch_feed(table, pieces, feed, second_sems)
    first = fetch_attn(table, pieces, attn, first_sems)
    sent = []
    dy = dy_ref[...].astype(WIDE)
    d_branch, final_grad = norm_back(branch_ref[...], final_ref[...], dy)
    d_branch = d_branch.astype(LOW)
    hidden = hidden_ref[...]
    feed_in = norm_rows(hidden, feed_gain_ref[...]).astype(LOW)
    for t in range(HEADS):
        wait_all(second[t])
        gate = dot(feed_in, feed[t, :, :hidden_width])
        up = dot(feed_in, feed[t, :, hidden_width : 2 * hidden_width])
        value, slope = gelu_parts(gate)
        product = (value * up).astype(LOW)
        d_product = dot(d_branch, feed[t, :, 2 * hidden_width :])
        d_gate = (d_product * up * slope).astype(LOW)
        d_up = (d_product * value).astype(LOW)
        part = dot_nt(d_gate, feed[t, :, :hidden_width]) + dot_nt(
            d_up, feed[t, :, hidden_width : 2 * hidden_width]
        )
        normed_ref[...] = part if t == 0 else normed_ref[...] + part
        grad_feed[t, :, :hidden_width] = dot_tn(feed_in, d_gate).astype(LOW)
        grad_feed[t, :, hidden_width : 2 * hidden_width] = dot_tn(feed_in, d_up).astype(LOW)
        grad_feed[t, :, 2 * hidden_width :] = dot_tn(d_branch, product).astype(LOW)
        sent += sendings(
            table, entry, grads, t, lambda at: grad_feed.at[t, at, :],
            (2 * width, feed.shape[2]), out_sems[t],
        )
    part_hidden, feed_grad = norm_back(hidden, feed_gain_ref[...], normed_ref[...])
    d_hidden = dy + part_hidden
    d_hidden_ref[...] = d_hidden
    d_sum, after_grad = norm_back(sum_ref[...], after_ref[...], d_hidden)
    d_sum = d_sum.astype(LOW)
    cosine, sine, bias = cos_ref[...], sin_ref[...], bias_ref[...]
    normed = norm_rows(x_ref[...].astype(WIDE), before_ref[...]).astype(LOW)
    query_grad = jnp.zeros((1, width), WIDE)
    for t in range(HEADS):
        wait_all(first[t])
        key = pair_ref[:, :width]
        raw = dot(normed, attn[t, :, :width])
        query = rotate(norm_rows(raw, query_gain_ref[...]), cosine, sine).astype(LOW)
        chance = softmax(dot_nt(query, key) * scale + bias)
        d_mixed = dot(d_sum, attn[t, :, width:]).astype(LOW)
        grad_attn[t, :, width:] = dot_tn(
            d_sum, attended_ref[:, t * width : (t + 1) * width]
        ).astype(LOW)
        d_chance = dot_nt(d_mixed, pair_ref[:, width:])
        weighted = jnp.sum(chance * d_chance, axis=-1, keepdims=True)
        d_scores = (chance * (d_chance - weighted)).astype(LOW)
        d_key = dot_tn(d_scores, query) * scale
        d_value = dot_tn(chance.astype(LOW), d_mixed)
        d_pair[:, :width] = d_key if t == 0 else d_pair[:, :width] + d_key
        d_pair[:, width:] = d_value if t == 0 else d_pair[:, width:] + d_value
        d_query = rotate(dot(d_scores, key) * scale, cosine, -sine)
        d_raw, gain_part = norm_back(raw, query_gain_ref[...], d_query)
        query_grad = query_grad + gain_part
        d_raw = d_raw.astype(LOW)
        grad_attn[t, :, :width] = dot_tn(normed, d_raw).astype(LOW)
        sent += sendings(
            table, entry, grads, t, lambda at: grad_attn.at[t, at, :], (0, 2 * width),
            out_sems[HEADS + t],
        )
        part = dot_nt(d_raw, attn[t, :, :width])
        normed_ref[...] = part if t == 0 else normed_ref[...] + part
    earlier = d_pair.shape[0] - rows
    own_ref[...] = d_pair[earlier:, :]
    sent_ref[...] = d_pair[:earlier, :].astype(LOW)
    gains_ref[...] = jnp.zeros(gains_ref.shape, WIDE)
    gains_ref[0:1, :] = after_grad
    gains_ref[1:2, :] = feed_grad
    gains_ref[2:3, :] = final_grad
    gains_ref[3:4, :width] = query_grad
    wait_all(sent)


def closing_kernel(
    count, grad_count, table,
    own_ref, arrived_ref, x_ref, before_ref, key_gain_ref, cos_ref, sin_ref, d_normed_ref,
    d_hidden_ref, *refs,
):
    pieces = refs[:count]
    refs = refs[count:]
    grads = refs[:grad_count]
    input_ref, gains_ref, weights, grad_pair, sems, *out_sems = refs[grad_count:]
    width_pair = own_ref.shape[1]
    main = grads[0].shape[1] * len(grads)
    quarter = width_pair // HEADS
    half = width_pair // 2
    copies, sent = [], []
    for t in range(HEADS):
        columns = quarter_columns(table, t, quarter)
        copies += fetches(
            table, pieces, t, (width_pair, quarter), lambda rows: weights.at[rows, columns], sems
        )
    x = x_ref[...].astype(WIDE)
    normed = norm_rows(x, before_ref[...]).astype(LOW)
    d_pair = own_ref[...]
    for back in range(arrived_ref.shape[0]):
        d_pair = d_pair + arrived_ref[back].astype(WIDE)
    wait_all(copies)
    raw = dot(normed, weights[:, :half])
    d_key, key_grad = norm_back(
        raw, key_gain_ref[...], rotate(d_pair[:, :half], cos_ref[...], -sin_ref[...])
    )
    low_pair = jnp.concatenate([d_key.astype(LOW), d_pair[:, half:].astype(LOW)], axis=1)
    grad_pair[...] = dot_tn(normed, low_pair).astype(LOW)
    for t in range(HEADS):
        columns = quarter_columns(table, t, quarter)
        sent += sendings(
            table, len(pieces) + main, grads, t, lambda at: grad_pair.at[at, columns],
            (0, quarter), out_sems[t],
        )
    d_normed = d_normed_ref[...] + dot_nt(low_pair, weights[...])
    part_inputs, before_grad = norm_back(x, before_ref[...], d_normed)
    input_ref[...] = d_hidden_ref[...] + part_inputs
    gains_ref[...] = jnp.zeros(gains_ref.shape, WIDE)
    gains_ref[0:1, :] = before_grad
    gains_ref[1:2, :half] = key_grad
    wait_all(sent)


def call(kernel, name, args, far_args, outs, far_outs, scratch, sems, cost, aliases=None):
    anywhere = pl.BlockSpec(memory_space=pl.ANY)
    near = pl.BlockSpec(memory_space=pltpu.VMEM)
    flops, moved = cost
    return pl.pallas_call(
        kernel,
        name=name,
        out_shape=[jax.ShapeDtypeStruct(shape, dtype) for shape, dtype in far_outs + outs],
        in_specs=[pl.BlockSpec(memory_space=pltpu.SMEM)]
        + [near] * (len(args) - 1)
        + [anywhere] * len(far_args),
        out_specs=[anywhere] * len(far_outs) + [near] * len(outs),
        scratch_shapes=[pltpu.VMEM(shape, dtype) for shape, dtype in scratch]
        + [pltpu.SemaphoreType.DMA((count,)) for count in sems],
        input_output_aliases=aliases or {},
        cost_estimate=pl.CostEstimate(flops=flops, transcendentals=0, bytes_accessed=moved),
        compiler_params=pltpu.CompilerParams(vmem_limit_bytes=VMEM_BYTES),
    )(*args, *far_args)


def layer_keys(x, layer, turns, table):
    pieces, before, query_gain, key_gain, after_gain, feed_gain, final = layer
    far = tuple(pieces)
    pair = 2 * key_gain.shape[1]
    rows, width = x.shape
    args = (table, x, before, key_gain) + turns
    kernel = functools.partial(keys_kernel, len(far))
    cost = (2 * rows * width * pair, 2 * width * pair)
    outs = [((rows, pair), LOW)]
    return call(kernel, "keys", args, far, outs, [], [((width, pair), LOW)], [HEADS * len(far)], cost)[0]


def sizes_of(pieces, own):
    columns = pieces[0].shape[2]
    rest = columns - own - own // HEADS
    return columns, rest


def layer_forward(x, pair, layer, bias, turns, table):
    pieces, before, query_gain, key_gain, after_gain, feed_gain, final = layer
    far = tuple(pieces)
    rows, width = x.shape
    own = pair.shape[1]
    columns, rest = sizes_of(pieces, own)
    args = (table, x, pair, bias) + turns + (before, query_gain, after_gain, feed_gain, final)
    token = ((rows, width), WIDE)
    outs = [((rows, width), LOW), ((rows, own // 2 * HEADS), LOW), token, token, token]
    scratch = [((HEADS, width, own), LOW), ((HEADS, width, rest), LOW)]
    kernel = functools.partial(forward_kernel, len(far))
    cost = (4 * rows * width * columns * HEADS, 2 * width * columns * HEADS)
    return call(kernel, "forward", args, far, outs, [], scratch, [HEADS * len(far)] * 2, cost)


def layer_backward(dy, x, pair, kept, layer, bias, turns, table, ranks):
    pieces, before, query_gain, key_gain, after_gain, feed_gain, final = layer
    far = tuple(pieces)
    rows, width = x.shape
    own = pair.shape[1]
    columns, rest = sizes_of(pieces, own)
    earlier = pair.shape[0] - rows
    args = (
        (table, dy, x, pair, bias) + turns + (before, query_gain, after_gain, feed_gain, final)
        + tuple(kept)
    )
    token = ((rows, width), WIDE)
    if ranks > 4:
        grad_shapes = [((HEADS, 1, width, own + rest), LOW)]
        pair_shapes = [((HEADS, 1, width, own // HEADS), LOW)]
    else:
        half = width // (ranks * CORES)
        grad_shapes = [
            ((HEADS, len(group), half, own + rest), LOW)
            for group in groups_of(ranks)
            for core in range(CORES)
        ]
        pair_shapes = [((HEADS, ranks, half, own // HEADS), LOW)] * CORES
    count = sum(shape[1] for shape, dtype in grad_shapes)
    outs = [((rows, own), WIDE), ((earlier, own), LOW), token, token, ((8, width), WIDE)]
    scratch = [
        ((HEADS, width, own), LOW), ((HEADS, width, rest), LOW),
        ((HEADS, width, own), LOW), ((HEADS, width, rest), LOW), (pair.shape, WIDE),
    ]
    kernel = functools.partial(backward_kernel, len(far), len(grad_shapes))
    cost = (8 * rows * width * columns * HEADS, 4 * width * columns * HEADS)
    result = call(
        kernel, "backward", args, far, outs, grad_shapes, scratch,
        [HEADS * len(far)] * 2 + [count] * 2 * HEADS, cost,
    )
    grads = tuple(result[: len(grad_shapes)])
    d_own, sent, d_normed, d_hidden, gains = result[len(grad_shapes) :]
    back = earlier // rows
    arrived = jnp.stack(
        [
            shifted(sent[(back - by) * rows : (back - by + 1) * rows], HEAD, -by)
            for by in range(1, back + 1)
        ]
    )
    args = (table, d_own, arrived, x, before, key_gain) + turns + (d_normed, d_hidden)
    outs = [token, ((8, width), WIDE)]
    scratch = [((width, own), LOW), ((width, own), LOW)]
    kernel = functools.partial(closing_kernel, len(far), len(pair_shapes))
    cost = (6 * rows * width * own, 4 * width * own)
    result = call(
        kernel, "closing", args, far, outs, pair_shapes, scratch,
        [HEADS * len(far)] + [count] * HEADS, cost,
    )
    input_grad, more = result[len(pair_shapes) :]
    gain_grads = (
        more[0], gains[3, : own // 2], more[1, : own // 2], gains[0], gains[1], gains[2],
    )
    return input_grad, grads + tuple(result[: len(pair_shapes)]), gain_grads


def body(
    inputs,
    out_grad,
    segment_ids,
    positions,
    before_gain,
    query_matrix,
    key_matrix,
    value_matrix,
    query_gain,
    key_gain,
    output_matrix,
    after_gain,
    feed_gain,
    gate_matrix,
    up_matrix,
    down_matrix,
    final_gain,
):
    section = lax.axis_index(SECTION)
    head = lax.axis_index(HEAD)
    ranks = lax.axis_size(DATA)
    rows, width = inputs.shape[1:]
    head_width = key_matrix.shape[2]
    depth = gate_matrix.shape[1]
    hidden_width = gate_matrix.shape[2]
    back = min(-(-(WINDOW - 1) // rows), HEADS - 1)
    quarter = 2 * head_width // HEADS

    shared = jnp.concatenate([key_matrix[0], value_matrix[0]], axis=1)
    slab = jnp.concatenate(
        [
            query_matrix[0],
            output_matrix[0].T,
            lax.dynamic_slice_in_dim(shared, head * quarter, quarter, 1),
            gate_matrix[0],
            up_matrix[0],
            down_matrix[0].T,
        ],
        axis=1,
    )
    half = depth // CORES
    upper, lower = slab[:half], slab[half:]
    traded = flip(jnp.where(section == 0, lower, upper), SECTION, 1)
    halves = jnp.where(section == 0, upper, traded), jnp.where(section == 0, traded, lower)

    first_pieces, chunks = gather_slab(halves[0])
    second_pieces, unused = gather_slab(after(halves[1], chunks[3]))
    pieces = first_pieces, second_pieces

    gain_list = (before_gain, query_gain, key_gain, after_gain, feed_gain, final_gain)
    sizes = [gain.shape[1] for gain in gain_list]
    gain_both = gather_gains(
        after(jnp.concatenate([gain[0] for gain in gain_list]), chunks[2])
    )

    first_input = lax.dynamic_index_in_dim(inputs, section, 0, keepdims=False)
    last_cot = lax.dynamic_index_in_dim(out_grad, section, 0, keepdims=False)
    segments = lax.dynamic_index_in_dim(segment_ids, section, 0, keepdims=False)
    token_positions = lax.dynamic_index_in_dim(positions, section, 0, keepdims=False)
    everyone = jnp.concatenate(
        [shifted(after(first_input, chunks[1]), HEAD, by) for by in range(back, 0, -1)] + [first_input]
    )
    padded_segments = jnp.concatenate([jnp.full((back * rows,), -1, jnp.int32), segments])
    padded_positions = jnp.concatenate([jnp.zeros((back * rows,), jnp.int32), token_positions])
    key_segments = lax.dynamic_slice_in_dim(padded_segments, head * rows, (back + 1) * rows)
    key_positions = lax.dynamic_slice_in_dim(padded_positions, head * rows, (back + 1) * rows)
    gap = key_positions[-rows:, None] - key_positions[None, :]
    allowed = (
        (key_segments[-rows:, None] == key_segments[None, :]) & (gap >= 0) & (gap < WINDOW)
    )
    bias = jnp.where(allowed, 0.0, -1e30).astype(WIDE)
    half_depth = head_width // 2
    frequency = 10000.0 ** (-(jnp.arange(half_depth, dtype=WIDE) * 2.0) / head_width)
    turn = key_positions.astype(WIDE)[:, None] * frequency
    turns_all = jnp.cos(turn), jnp.sin(turn)
    turns = turns_all[0][-rows:], turns_all[1][-rows:]

    layers = []
    for index in range(2):
        gains, first = [], 0
        for size in sizes:
            gains.append(gain_both[index][:, first : first + size].reshape(1, -1).astype(WIDE))
            first += size
        layers.append((pieces[index],) + tuple(gains))

    table = row_table(ranks, depth)
    pair_first = layer_keys(everyone, layers[0], turns_all, table)
    out_first, *kept_first = layer_forward(first_input, pair_first, layers[0], bias, turns, table)
    own_pair = layer_keys(out_first, layers[1], turns, table)
    pair_second = jnp.concatenate(
        [shifted(own_pair, HEAD, by) for by in range(back, 0, -1)] + [own_pair]
    )
    out_second, *kept_second = layer_forward(
        out_first, pair_second, layers[1], bias, turns, table
    )
    grad_second, slab_second, gains_second = layer_backward(
        last_cot, out_first, pair_second, kept_second, layers[1], bias, turns, table, ranks
    )
    sums_second = first_sums(slab_second, ranks)
    grad_first, slab_first, gains_first = layer_backward(
        after(grad_second.astype(LOW), *sums_second), first_input, pair_first, kept_first, layers[0], bias, turns, table, ranks
    )
    total_second, unused = scatter_sums(sums_second, ranks)
    total_first, mark = scatter_sums(first_sums(slab_first, ranks), ranks)

    def settle(first, second):
        own, sent = by_section(first, second)
        return jnp.stack(by_section(own, flip(sent, SECTION, 1)))[None]

    gain_own = scatter_gains(
        *(
            after(jnp.concatenate([gain.reshape(ranks, -1) for gain in gains], axis=1), mark)
            for gains in (gains_first, gains_second)
        )
    )
    gain_grads, first = [], 0
    for size in sizes:
        gain_grads.append(gain_own[None, first : first + size])
        first += size

    own, sent = by_section(total_first, total_second)
    own = jnp.concatenate(by_section(own, flip(sent, SECTION, 1)))
    starts = [0]
    for step in (head_width, head_width, hidden_width, hidden_width, hidden_width, quarter):
        starts.append(starts[-1] + step)
    cut = [own[:, a:b] for a, b in zip(starts[:-1], starts[1:])]
    pair = cut[5].astype(LOW)
    shared = jnp.zeros((depth, 2 * head_width), LOW)
    for bit in range(HEADS):
        piece = pair if bit == 0 else flip(pair, HEAD, bit)
        shared = lax.dynamic_update_slice(shared, piece, (0, (head ^ bit) * quarter))
    shared = shared.astype(WIDE)
    return (
        settle(out_first, out_second),
        settle(grad_first, grad_second),
        gain_grads[0],
        cut[0][None],
        shared[None, :, :head_width],
        shared[None, :, head_width:],
        gain_grads[1],
        gain_grads[2],
        cut[1].T[None],
        gain_grads[3],
        gain_grads[4],
        cut[2][None],
        cut[3][None],
        cut[4].T[None],
        gain_grads[5],
    )


def solution(mesh):
    tokens = P(None, (DATA, HEAD), None)
    pack = P(None, DATA)
    gain = P(SECTION, DATA)
    split = P(SECTION, DATA, HEAD)
    plain = P(SECTION, DATA, None)
    turned = P(SECTION, HEAD, DATA)
    outs = P(SECTION, None, (DATA, HEAD), None)
    weights = (
        gain, split, plain, plain, gain, gain, turned, gain, gain, split, split, turned, gain,
    )
    return jax.shard_map(
        body,
        mesh=mesh,
        in_specs=(tokens, tokens, pack, pack) + weights,
        out_specs=(outs, outs) + weights,
        check_vma=False,
    )
```

time: 558 us -> 490 us (0.88)
  local copies, waits for them, and re-layouts: 94.5 us -> 40.2 us
  waiting for transfers between devices: 211 us -> 182 us
  other arithmetic: 32.3 us -> 60.9 us
  starting transfers between devices: 116 us -> 100 us
  Pallas kernels: 91.7 us -> 97.9 us
    dynamic_update_slice x61 -> x0, local copies, waits for them, and re-layouts: 46.9 us -> none  [gather_slab(): lax.dynamic_update_slice(whole, part[None, :, None], (head ^ bit, place,...]
    ppermute x139 -> x65, waiting for transfers between devices: 153 us -> 123 us  [flip(): return lax.ppermute(value, axis, [(i, i ^ bit) for i in range(count)])]
    ppermute x139 -> x65, starting transfers between devices: 81.4 us -> 59.3 us  [flip(): return lax.ppermute(value, axis, [(i, i ^ bit) for i in range(count)])]
    ppermute x0 -> x6, waiting for transfers between devices: none -> 13.1 us  [scatter_sums(): piece = lax.ppermute(piece.astype(LOW), DATA, pairs)]
    another operation x0 -> x10, other arithmetic: none -> 12.2 us  [the longest x8 10.6 us: gather_slab(): own = jnp.stack([chunk, near, far, across])]
    ppermute x0 -> x6, starting transfers between devices: none -> 9.96 us  [scatter_sums(): piece = lax.ppermute(piece.astype(LOW), DATA, pairs)]
    another operation x2 -> x1, local copies, waits for them, and re-layouts: 9.92 us -> 0.63 us  [row_table(): jnp.stack([jnp.int32(row) for row in rows] + [head ^ bit for bit in range...]
    unnamed x40 -> x117, local copies, waits for them, and re-layouts: 4.91 us -> 12.3 us
  transfers between devices with their start and end apart: 165 -> 91, of which waited for: 69 -> 40; matrix products, arithmetic and copies ran while one was open for 21% -> 16% of each run, Pallas kernels for 0% -> 6%
where the time goes in v3:
time: 490 us; the launch traced here: 483 us
  waiting for transfers between devices  182 us (37%)
  starting transfers between devices  100 us (20%)
  Pallas kernels  97.9 us (20%)
  other arithmetic  60.9 us (12%)
  local copies, waits for them, and re-layouts  40.2 us (8%)
    ppermute x65, waiting for transfers between devices, flip(): return lax.ppermute(value, axis, [(i, i ^ bit) for i in range(count)])  123 us
    pallas_call x8, Pallas kernels, call(): pl.pallas_call(kernel, name=name, out_shape=[jax.ShapeDtypeStruct(shape,...  97.9 us
    ppermute x65, starting transfers between devices, flip(): return lax.ppermute(value, axis, [(i, i ^ bit) for i in range(count)])  59.3 us
    ppermute x12, waiting for transfers between devices, ring(): lax.ppermute(value, DATA, [(i, (i + 1) % count) for i in range(count)])  29.5 us
    ppermute x8, starting transfers between devices, shifted(): return lax.ppermute(value, axis, pairs)  19.4 us
    ppermute x8, waiting for transfers between devices, shifted(): return lax.ppermute(value, axis, pairs)  15.8 us
    ppermute x6, waiting for transfers between devices, scatter_sums(): piece = lax.ppermute(piece.astype(LOW), DATA, pairs)  13.1 us
    unnamed x117, local copies, waits for them, and re-layouts  12.3 us
  transfers between devices with their start and end apart: 91, of which 40 were waited for; matrix products, arithmetic and copies ran while one was open for 16% of the time, Pallas kernels for 6%

profile of v3, /device:TPU:0, one launch (start us, length us, event | category | flops | bytes accessed | tf_op | source)
XLA Modules:
  0.0 483.3 jit_solution(6580420257445042114)
XLA Ops:
  14.4 7.9 %collective-permute-done.1.refs_1_ = bf16[80,2176]{1,0:T(8,128)(2,1)S(1)} collective-permute-done((bf16[80,2176]{1,0:T(8,128)(2,1)S(1)}, bf16[80,2176]{1,0:T(8,128)(2,1)S(1)}, u32[]{:S(2)}, u32[]{:S(2)}) %collective-permute-start.1) | collective-permute-done | bytes 348192 | tf_op jit(solution)/shard_map/ppermute | solution.py:29
  27.4 6.5 %collective-permute-done.4.refs_1_ = bf16[80,2176]{1,0:T(8,128)(2,1)} collective-permute-done((bf16[80,2176]{1,0:T(8,128)(2,1)S(1)}, bf16[80,2176]{1,0:T(8,128)(2,1)}, u32[]{:S(2)}, u32[]{:S(2)}) %collective-permute-start.4) | collective-permute-done | bytes 348192 | tf_op jit(solution)/shard_map/ppermute | solution.py:29
  35.2 9.6 %collective-permute-done.5 = bf16[768]{0:T(1024)(128)(2,1)S(1)} collective-permute-done((bf16[768]{0:T(1024)(128)(2,1)}, bf16[768]{0:T(1024)(128)(2,1)S(1)}, u32[]{:S(2)}, u32[]{:S(2)}) %collective-permute-start.5) | collective-permute-done | bytes 1568 | tf_op jit(solution)/shard_map/ppermute | solution.py:29
  54.5 4.1 collective-permute-start.3
  62.4 4.9 %collective-permute-done.2 = bf16[256,640]{1,0:T(8,128)(2,1)} collective-permute-done((bf16[256,640]{1,0:T(8,128)(2,1)}, bf16[256,640]{1,0:T(8,128)(2,1)}, u32[]{:S(2)}, u32[]{:S(2)}) %collective-permute-start.2) | collective-permute-done | bytes 327712 | tf_op jit(solution)/shard_map/ppermute | solution.py:35
  69.8 4.5 collective-permute-done.13
  74.3 7.4 %collective-permute-done.17 = bf16[80,2176]{1,0:T(8,128)(2,1)S(1)} collective-permute-done((bf16[80,2176]{1,0:T(8,128)(2,1)}, bf16[80,2176]{1,0:T(8,128)(2,1)S(1)}, u32[]{:S(2)}, u32[]{:S(2)}) %collective-permute-start.17) | collective-permute-done | bytes 348192 | tf_op jit(solution)/shard_map/ppermute | solution.py:24
  83.7 5.6 %collective-permute-done.15 = bf16[80,2176]{1,0:T(8,128)(2,1)} collective-permute-done((bf16[80,2176]{1,0:T(8,128)(2,1)S(1)}, bf16[80,2176]{1,0:T(8,128)(2,1)}, u32[]{:S(2)}, u32[]{:S(2)}) %collective-permute-start.15) | collective-permute-done | bytes 348192 | tf_op jit(solution)/shard_map/ppermute | solution.py:24
  107.1 4.4 collective-permute-done.32
  125.2 7.7 %collective-permute-done.33 = bf16[80,2176]{1,0:T(8,128)(2,1)S(1)} collective-permute-done((bf16[80,2176]{1,0:T(8,128)(2,1)S(1)}, bf16[80,2176]{1,0:T(8,128)(2,1)S(1)}, u32[]{:S(2)}, u32[]{:S(2)}) %collective-permute-start.33) | collective-permute-done | bytes 348192 | tf_op jit(solution)/shard_map/ppermute | solution.py:24
  138.1 5.2 %collective-permute-done.42 = bf16[80,2176]{1,0:T(8,128)(2,1)S(1)} collective-permute-done((bf16[80,2176]{1,0:T(8,128)(2,1)S(1)}, bf16[80,2176]{1,0:T(8,128)(2,1)S(1)}, u32[]{:S(2)}, u32[]{:S(2)}) %collective-permute-start.42) | collective-permute-done | bytes 348192 | tf_op jit(solution)/shard_map/ppermute | solution.py:24
  143.3 4.3 collective-permute-done.38
  149.1 5.7 %collective-permute-done.43 = bf16[80,2176]{1,0:T(8,128)(2,1)S(1)} collective-permute-done((bf16[80,2176]{1,0:T(8,128)(2,1)S(1)}, bf16[80,2176]{1,0:T(8,128)(2,1)S(1)}, u32[]{:S(2)}, u32[]{:S(2)}) %collective-permute-start.43) | collective-permute-done | bytes 348192 | tf_op jit(solution)/shard_map/ppermute | solution.py:24
  165.9 4.6 keys.2.pair_ref
  170.4 14.4 %forward.2 = (bf16[256,640]{1,0:T(8,128)(2,1)}, bf16[256,1024]{1,0:T(8,128)(2,1)}, f32[256,640]{1,0:T(8,128)}, f32[256,640]{1,0:T(8,128)}, f32[256,640]{1,0:T(8,128)}) custom-call(s32[28]{0:T(128)} %stack.241.table, bf16[256,640]{1,0:T(8,128)(2,1)} %copy-done.17, bf16[768,512]{1,0:T(8,128)(2,1)} %keys.2.pair_ref, f32[256,768]{1,0:T(8,128)} %fusion.8.bias_ref, ...), custom_call_target="tpu_custom_call" | custom-call | flops 5704253440 | bytes 11141120 | tf_op jit(solution)/shard_map/forward/pallas_call | solution.py:511
  199.5 4.4 collective-permute-done.45
  205.8 14.4 %forward.3 = (bf16[256,640]{1,0:T(8,128)(2,1)}, bf16[256,1024]{1,0:T(8,128)(2,1)}, f32[256,640]{1,0:T(8,128)}, f32[256,640]{1,0:T(8,128)}, f32[256,640]{1,0:T(8,128)}) custom-call(s32[28]{0:T(128)} %stack.241.table, bf16[256,640]{1,0:T(8,128)(2,1)} %get-tuple-element.51.x_ref, bf16[768,512]{1,0:T(8,128)(2,1)} %pad_maximum_fusion.11.pair_ref, ...), custom_call_target="tpu_custom_call" | custom-call | flops 5704253440 | bytes 11141120 | tf_op jit(solution)/shard_map/forward/pallas_call | solution.py:511
  220.2 24.4 %backward.2 = (bf16[4,2,80,2048]{3,2,1,0:T(8,128)(2,1)}, bf16[4,2,80,2048]{3,2,1,0:T(8,128)(2,1)}, bf16[4,2,80,2048]{3,2,1,0:T(8,128)(2,1)}, bf16[4,2,80,2048]{3...) custom-call(s32[28]{0:T(128)} %stack.241.table, ...), custom_call_target="tpu_custom_call" | custom-call | flops 11408506880 | bytes 22282240 | tf_op jit(solution)/shard_map/backward/pallas_call | solution.py:511
  251.8 4.6 collective-permute-done.48
  259.2 6.2 %closing.2 = (bf16[4,4,80,128]{3,2,1,0:T(8,128)(2,1)}, bf16[4,4,80,128]{3,2,1,0:T(8,128)(2,1)}, f32[256,640]{1,0:T(8,128)}, f32[8,640]{1,0:T(8,128)}) custom-call(s32[28]{0:T(128)} %stack.241.table, f32[256,512]{1,0:T(8,128)} %get-tuple-element.57.own_ref, bf16[2,256,512]{2,1,0:T(8,128)(2,1)} %pad_maximum_fusion.20.arrived_ref, ...), custom_call_target="tpu_custom_call" | custom-call | flops 503316480 | bytes 1310720 | tf_op jit(solution)/shard_map/closing/pallas_call | solution.py:511
  285.0 24.1 %backward.3 = (bf16[4,2,80,2048]{3,2,1,0:T(8,128)(2,1)}, bf16[4,2,80,2048]{3,2,1,0:T(8,128)(2,1)}, bf16[4,2,80,2048]{3,2,1,0:T(8,128)(2,1)}, bf16[4,2,80,2048]{3...) custom-call(s32[28]{0:T(128)} %stack.241.table, ...), custom_call_target="tpu_custom_call" | custom-call | flops 11408506880 | bytes 22282240 | tf_op jit(solution)/shard_map/backward/pallas_call | solution.py:511
  315.0 8.6 %collective-permute-start.76 = (bf16[1,80,2176]{2,1,0:T(8,128)(2,1)}, bf16[1,80,2176]{2,1,0:T(8,128)(2,1)}, u32[]{:S(2)}, u32[]{:S(2)}) collective-permute-start(bf16[1,80,2176]{2,1,0:T(8,128)(2,1)} %get-tuple-element.105), channel_id=1, source_target_pairs={{0,2},{1,3},{2,0},{3,1},{4,6},{5,7},{6,4},{7,5},{8,10},{9,11},{10,... | collective-permute-start | bytes 1044488 | tf_op jit(solution)/shard_map/ppermute | solution.py:24
  330.7 6.2 %closing.3 = (bf16[4,4,80,128]{3,2,1,0:T(8,128)(2,1)}, bf16[4,4,80,128]{3,2,1,0:T(8,128)(2,1)}, f32[256,640]{1,0:T(8,128)}, f32[8,640]{1,0:T(8,128)}) custom-call(s32[28]{0:T(128)} %stack.241.table, f32[256,512]{1,0:T(8,128)} %get-tuple-element.72.own_ref, bf16[2,256,512]{2,1,0:T(8,128)(2,1)} %pad_maximum_fusion.21.arrived_ref, bf16[256,640]{1,0:T(8,128)(2,1)} %copy-done.17, ...), custom_call_target="tpu_custom_call" | custom-call | flops 503316480 | bytes 1310720 | tf_op jit(solution)/shard_map/closing/pallas_call | solution.py:511
  343.1 6.0 %collective-permute-start.77 = (bf16[2,80,2176]{2,1,0:T(8,128)(2,1)S(1)}, bf16[2,80,2176]{2,1,0:T(8,128)(2,1)S(1)}, u32[]{:S(2)}, u32[]{:S(2)}) collective-permute-start(bf16[2,80,2176]{2,1,0:T(8,128)(2,1)S(1)} %pad_maximum_fusion.16), channel_id=1, source_target_pairs={{0,1},{1,0},{2,3},{3,2},{4,5},{5,4},{6,7},{7,6},{8,9},{9,8},{10,11... | collective-permute-start | bytes 2088968 | tf_op jit(solution)/shard_map/ppermute | solution.py:24
  351.6 13.9 %collective-permute-done.77 = bf16[2,80,2176]{2,1,0:T(8,128)(2,1)S(1)} collective-permute-done((bf16[2,80,2176]{2,1,0:T(8,128)(2,1)S(1)}, bf16[2,80,2176]{2,1,0:T(8,128)(2,1)S(1)}, u32[]{:S(2)}, u32[]{:S(2)}) %collective-permute-start.77) | collective-permute-done | bytes 696352 | tf_op jit(solution)/shard_map/ppermute | solution.py:24
  369.3 10.6 %collective-permute-done.83 = bf16[2,80,2176]{2,1,0:T(8,128)(2,1)S(1)} collective-permute-done((bf16[2,80,2176]{2,1,0:T(8,128)(2,1)S(1)}, bf16[2,80,2176]{2,1,0:T(8,128)(2,1)S(1)}, u32[]{:S(2)}, u32[]{:S(2)}) %collective-permute-start.83) | collective-permute-done | bytes 696352 | tf_op jit(solution)/shard_map/ppermute | solution.py:24
  395.3 5.2 %collective-permute-done.58 = bf16[1,80,2176]{2,1,0:T(8,128)(2,1)S(1)} collective-permute-done((bf16[1,80,2176]{2,1,0:T(8,128)(2,1)S(1)}, bf16[1,80,2176]{2,1,0:T(8,128)(2,1)S(1)}, u32[]{:S(2)}, u32[]{:S(2)}) %collective-permute-start.58) | collective-permute-done | bytes 348192 | tf_op jit(solution)/shard_map/ppermute | solution.py:24
  406.7 5.2 %collective-permute-done.73 = bf16[1,80,2176]{2,1,0:T(8,128)(2,1)} collective-permute-done((bf16[1,80,2176]{2,1,0:T(8,128)(2,1)}, bf16[1,80,2176]{2,1,0:T(8,128)(2,1)}, u32[]{:S(2)}, u32[]{:S(2)}) %collective-permute-start.73) | collective-permute-done | bytes 348192 | tf_op jit(solution)/shard_map/ppermute | solution.py:24
  415.2 7.6 %collective-permute-done.60 = f32[4,768]{1,0:T(4,128)S(1)} collective-permute-done((f32[4,768]{1,0:T(4,128)S(1)}, f32[4,768]{1,0:T(4,128)S(1)}, u32[]{:S(2)}, u32[]{:S(2)}) %collective-permute-start.60) | collective-permute-done | bytes 12320 | tf_op jit(solution)/shard_map/ppermute | solution.py:24
  430.0 9.5 %collective-permute-done.72 = bf16[2,80,2176]{2,1,0:T(8,128)(2,1)S(1)} collective-permute-done((bf16[2,80,2176]{2,1,0:T(8,128)(2,1)S(1)}, bf16[2,80,2176]{2,1,0:T(8,128)(2,1)S(1)}, u32[]{:S(2)}, u32[]{:S(2)}) %collective-permute-start.72) | collective-permute-done | bytes 696352 | tf_op jit(solution)/shard_map/ppermute | solution.py:24
  450.8 13.1 %collective-permute-done.68 = bf16[80,2176]{1,0:T(8,128)(2,1)S(1)} collective-permute-done((bf16[80,2176]{1,0:T(8,128)(2,1)S(1)}, bf16[80,2176]{1,0:T(8,128)(2,1)S(1)}, u32[]{:S(2)}, u32[]{:S(2)}) %collective-permute-start.68) | collective-permute-done | bytes 348192 | tf_op jit(solution)/shard_map/ppermute | solution.py:148
  465.6 5.0 %collective-permute-start.64 = (f32[768]{0:T(1024)S(1)}, f32[768]{0:T(1024)S(1)}, u32[]{:S(2)}, u32[]{:S(2)}) collective-permute-start(f32[768]{0:T(1024)S(1)} %add.331), channel_id=1, source_target_pairs={{0,4},{4,8},{8,12},{12,0},{1,5},{5,9},{9,13},{13,1},{2,6},{6,10},{... | collective-permute-start | bytes 9224 | tf_op jit(solution)/shard_map/ppermute | solution.py:29
  (423 shorter events, 215.6 us)
Async XLA Ops:
  23.8 27.1 %collective-permute-start.9 = (bf16[80,2176]{1,0:T(8,128)(2,1)S(1)}, bf16[80,2176]{1,0:T(8,128)(2,1)}, u32[]{:S(2)}, u32[]{:S(2)}) collective-permute-start(bf16[80,2176]{1,0:T(8,128)(2,1)S(1)} %get-tuple-element.138), channel_id=1, source_target_pairs={{0,1},{1,0},{2,3},{3,2},{4,5},{5,4},{6,7},{7,6},{8,9},{9,8},{10,11... | collective-permute-start | bytes 1044488 | tf_op jit(solution)/shard_map/ppermute | solution.py:24
  25.4 29.1 %collective-permute-start.14 = (bf16[80,2176]{1,0:T(8,128)(2,1)S(1)}, bf16[80,2176]{1,0:T(8,128)(2,1)S(1)}, u32[]{:S(2)}, u32[]{:S(2)}) collective-permute-start(bf16[80,2176]{1,0:T(8,128)(2,1)S(1)} %collective-permute-done.1.refs_1_), channel_id=1, source_target_pairs={{0,2},{1,3},{2,0},{3,1},{4,6},{5,7},{6,4},{7,5},{8,10},{9,11},{10,... | collective-permute-start | bytes 1044488 | tf_op jit(solution)/shard_map/ppermute | solution.py:24
  26.9 31.7 %collective-permute-start.11 = (bf16[80,2176]{1,0:T(8,128)(2,1)}, bf16[80,2176]{1,0:T(8,128)(2,1)}, u32[]{:S(2)}, u32[]{:S(2)}) collective-permute-start(bf16[80,2176]{1,0:T(8,128)(2,1)} %collective-permute-done.10), channel_id=1, source_target_pairs={{0,1},{1,0},{2,3},{3,2},{4,5},{5,4},{6,7},{7,6},{8,9},{9,8},{10,11... | collective-permute-start | bytes 1044488 | tf_op jit(solution)/shard_map/ppermute | solution.py:24
  33.9 26.7 %collective-permute-start.21 = (bf16[80,2176]{1,0:T(8,128)(2,1)}, bf16[80,2176]{1,0:T(8,128)(2,1)S(1)}, u32[]{:S(2)}, u32[]{:S(2)}) collective-permute-start(bf16[80,2176]{1,0:T(8,128)(2,1)} %collective-permute-done.4.refs_1_), channel_id=1, source_target_pairs={{0,4},{4,8},{8,12},{12,0},{1,5},{5,9},{9,13},{13,1},{2,6},{6,10},{... | collective-permute-start | bytes 1044488 | tf_op jit(solution)/shard_map/ppermute | solution.py:29
  58.7 23.0 %collective-permute-start.17 = (bf16[80,2176]{1,0:T(8,128)(2,1)}, bf16[80,2176]{1,0:T(8,128)(2,1)S(1)}, u32[]{:S(2)}, u32[]{:S(2)}) collective-permute-start(bf16[80,2176]{1,0:T(8,128)(2,1)} %collective-permute-done.4.refs_1_), channel_id=1, source_target_pairs={{0,1},{1,0},{2,3},{3,2},{4,5},{5,4},{6,7},{7,6},{8,9},{9,8},{10,11... | collective-permute-start | bytes 1044488 | tf_op jit(solution)/shard_map/ppermute | solution.py:24
  60.7 28.6 %collective-permute-start.15 = (bf16[80,2176]{1,0:T(8,128)(2,1)S(1)}, bf16[80,2176]{1,0:T(8,128)(2,1)}, u32[]{:S(2)}, u32[]{:S(2)}) collective-permute-start(bf16[80,2176]{1,0:T(8,128)(2,1)S(1)} %collective-permute-done.14), channel_id=1, source_target_pairs={{0,1},{1,0},{2,3},{3,2},{4,5},{5,4},{6,7},{7,6},{8,9},{9,8},{10,11... | collective-permute-start | bytes 1044488 | tf_op jit(solution)/shard_map/ppermute | solution.py:24
  67.3 23.2 %collective-permute-start.18 = (bf16[80,2176]{1,0:T(8,128)(2,1)}, bf16[80,2176]{1,0:T(8,128)(2,1)S(1)}, u32[]{:S(2)}, u32[]{:S(2)}) collective-permute-start(bf16[80,2176]{1,0:T(8,128)(2,1)} %collective-permute-done.4.refs_1_), channel_id=1, source_target_pairs={{0,2},{1,3},{2,0},{3,1},{4,6},{5,7},{6,4},{7,5},{8,10},{9,11},{10,... | collective-permute-start | bytes 1044488 | tf_op jit(solution)/shard_map/ppermute | solution.py:24
  69.8 22.9 %collective-permute-start.30 = (bf16[80,2176]{1,0:T(8,128)(2,1)}, bf16[80,2176]{1,0:T(8,128)(2,1)S(1)}, u32[]{:S(2)}, u32[]{:S(2)}) collective-permute-start(bf16[80,2176]{1,0:T(8,128)(2,1)} %after.8), channel_id=1, source_target_pairs={{0,4},{4,8},{8,12},{12,0},{1,5},{5,9},{9,13},{13,1},{2,6},{6,10},{... | collective-permute-start | bytes 1044488 | tf_op jit(solution)/shard_map/ppermute | solution.py:29
  74.3 20.4 %collective-permute-start.27 = (bf16[80,2176]{1,0:T(8,128)(2,1)}, bf16[80,2176]{1,0:T(8,128)(2,1)S(1)}, u32[]{:S(2)}, u32[]{:S(2)}) collective-permute-start(bf16[80,2176]{1,0:T(8,128)(2,1)} %after.8), channel_id=1, source_target_pairs={{0,2},{1,3},{2,0},{3,1},{4,6},{5,7},{6,4},{7,5},{8,10},{9,11},{10,... | collective-permute-start | bytes 1044488 | tf_op jit(solution)/shard_map/ppermute | solution.py:24
  118.1 38.6 %collective-permute-start.12 = (bf16[4,80,2176]{2,1,0:T(8,128)(2,1)S(1)}, bf16[4,80,2176]{2,1,0:T(8,128)(2,1)S(1)}, u32[]{:S(2)}, u32[]{:S(2)}) collective-permute-start(bf16[4,80,2176]{2,1,0:T(8,128)(2,1)S(1)} %pad_maximum_fusion.2.refs_0_), channel_id=1, source_target_pairs={{0,16},{16,0},{1,17},{17,1},{2,18},{18,2},{3,19},{19,3},{4,20},{20... | collective-permute-start | bytes 4177928 | tf_op jit(solution)/shard_map/ppermute | solution.py:24
  118.1 38.6 %collective-permute-start.16 = (bf16[4,80,2176]{2,1,0:T(8,128)(2,1)S(1)}, bf16[4,80,2176]{2,1,0:T(8,128)(2,1)S(1)}, u32[]{:S(2)}, u32[]{:S(2)}) collective-permute-start(bf16[4,80,2176]{2,1,0:T(8,128)(2,1)S(1)} %pad_maximum_fusion.3.refs_2_), channel_id=1, source_target_pairs={{0,16},{16,0},{1,17},{17,1},{2,18},{18,2},{3,19},{19,3},{4,20},{20... | collective-permute-start | bytes 4177928 | tf_op jit(solution)/shard_map/ppermute | solution.py:24
  118.6 38.6 %collective-permute-start.20 = (bf16[4,80,2176]{2,1,0:T(8,128)(2,1)S(1)}, bf16[4,80,2176]{2,1,0:T(8,128)(2,1)S(1)}, u32[]{:S(2)}, u32[]{:S(2)}) collective-permute-start(bf16[4,80,2176]{2,1,0:T(8,128)(2,1)S(1)} %pad_maximum_fusion.4.refs_4_), channel_id=1, source_target_pairs={{0,16},{16,0},{1,17},{17,1},{2,18},{18,2},{3,19},{19,3},{4,20},{20... | collective-permute-start | bytes 4177928 | tf_op jit(solution)/shard_map/ppermute | solution.py:24
  143.3 22.6 %collective-permute-start.25 = (bf16[4,80,2176]{2,1,0:T(8,128)(2,1)}, bf16[4,80,2176]{2,1,0:T(8,128)(2,1)}, u32[]{:S(2)}, u32[]{:S(2)}) collective-permute-start(bf16[4,80,2176]{2,1,0:T(8,128)(2,1)} %pad_maximum_fusion.5.refs_6_), channel_id=1, source_target_pairs={{0,16},{16,0},{1,17},{17,1},{2,18},{18,2},{3,19},{19,3},{4,20},{20... | collective-permute-start | bytes 4177928 | tf_op jit(solution)/shard_map/ppermute | solution.py:24
  156.1 28.7 %collective-permute-start.29 = (bf16[4,80,2176]{2,1,0:T(8,128)(2,1)}, bf16[4,80,2176]{2,1,0:T(8,128)(2,1)}, u32[]{:S(2)}, u32[]{:S(2)}) collective-permute-start(bf16[4,80,2176]{2,1,0:T(8,128)(2,1)} %pad_maximum_fusion.6.refs_0_), channel_id=1, source_target_pairs={{0,16},{16,0},{1,17},{17,1},{2,18},{18,2},{3,19},{19,3},{4,20},{20... | collective-permute-start | bytes 4177928 | tf_op jit(solution)/shard_map/ppermute | solution.py:24
  156.6 28.2 %collective-permute-start.34 = (bf16[4,80,2176]{2,1,0:T(8,128)(2,1)}, bf16[4,80,2176]{2,1,0:T(8,128)(2,1)S(1)}, u32[]{:S(2)}, u32[]{:S(2)}) collective-permute-start(bf16[4,80,2176]{2,1,0:T(8,128)(2,1)} %pad_maximum_fusion.7.refs_2_), channel_id=1, source_target_pairs={{0,16},{16,0},{1,17},{17,1},{2,18},{18,2},{3,19},{19,3},{4,20},{20... | collective-permute-start | bytes 4177928 | tf_op jit(solution)/shard_map/ppermute | solution.py:24
  156.7 28.1 %collective-permute-start.39 = (bf16[4,80,2176]{2,1,0:T(8,128)(2,1)}, bf16[4,80,2176]{2,1,0:T(8,128)(2,1)S(1)}, u32[]{:S(2)}, u32[]{:S(2)}) collective-permute-start(bf16[4,80,2176]{2,1,0:T(8,128)(2,1)} %pad_maximum_fusion.8.refs_4_), channel_id=1, source_target_pairs={{0,16},{16,0},{1,17},{17,1},{2,18},{18,2},{3,19},{19,3},{4,20},{20... | collective-permute-start | bytes 4177928 | tf_op jit(solution)/shard_map/ppermute | solution.py:24
  157.8 27.0 %collective-permute-start.44 = (bf16[4,80,2176]{2,1,0:T(8,128)(2,1)}, bf16[4,80,2176]{2,1,0:T(8,128)(2,1)}, u32[]{:S(2)}, u32[]{:S(2)}) collective-permute-start(bf16[4,80,2176]{2,1,0:T(8,128)(2,1)} %pad_maximum_fusion.9.refs_6_), channel_id=1, source_target_pairs={{0,16},{16,0},{1,17},{17,1},{2,18},{18,2},{3,19},{19,3},{4,20},{20... | collective-permute-start | bytes 4177928 | tf_op jit(solution)/shard_map/ppermute | solution.py:24
  244.6 28.3 %collective-permute-start.50 = (bf16[4,2,80,2048]{3,2,1,0:T(8,128)(2,1)}, bf16[4,2,80,2048]{3,2,1,0:T(8,128)(2,1)}, u32[]{:S(2)}, u32[]{:S(2)}) collective-permute-start(bf16[4,2,80,2048]{3,2,1,0:T(8,128)(2,1)} %get-tuple-element.63), channel_id=1, source_target_pairs={{0,16},{16,0},{1,17},{17,1},{2,18},{18,2},{3,19},{19,3},{4,20},{20... | collective-permute-start | bytes 7864328 | tf_op jit(solution)/shard_map/ppermute | solution.py:24
  250.2 29.3 %collective-permute-start.52 = (bf16[4,2,80,2048]{3,2,1,0:T(8,128)(2,1)}, bf16[4,2,80,2048]{3,2,1,0:T(8,128)(2,1)}, u32[]{:S(2)}, u32[]{:S(2)}) collective-permute-start(bf16[4,2,80,2048]{3,2,1,0:T(8,128)(2,1)} %get-tuple-element.67), channel_id=1, source_target_pairs={{0,16},{16,0},{1,17},{17,1},{2,18},{18,2},{3,19},{19,3},{4,20},{20... | collective-permute-start | bytes 7864328 | tf_op jit(solution)/shard_map/ppermute | solution.py:24
  315.0 24.3 %collective-permute-start.76 = (bf16[1,80,2176]{2,1,0:T(8,128)(2,1)}, bf16[1,80,2176]{2,1,0:T(8,128)(2,1)}, u32[]{:S(2)}, u32[]{:S(2)}) collective-permute-start(bf16[1,80,2176]{2,1,0:T(8,128)(2,1)} %get-tuple-element.105), channel_id=1, source_target_pairs={{0,2},{1,3},{2,0},{3,1},{4,6},{5,7},{6,4},{7,5},{8,10},{9,11},{10,... | collective-permute-start | bytes 1044488 | tf_op jit(solution)/shard_map/ppermute | solution.py:24
  326.6 22.5 %collective-permute-start.84 = (bf16[1,80,2176]{2,1,0:T(8,128)(2,1)}, bf16[1,80,2176]{2,1,0:T(8,128)(2,1)}, u32[]{:S(2)}, u32[]{:S(2)}) collective-permute-start(bf16[1,80,2176]{2,1,0:T(8,128)(2,1)} %get-tuple-element.112), channel_id=1, source_target_pairs={{0,1},{1,0},{2,3},{3,2},{4,5},{5,4},{6,7},{7,6},{8,9},{9,8},{10,11... | collective-permute-start | bytes 1044488 | tf_op jit(solution)/shard_map/ppermute | solution.py:24
  328.9 55.5 %collective-permute-start.56 = (bf16[4,2,80,2048]{3,2,1,0:T(8,128)(2,1)}, bf16[4,2,80,2048]{3,2,1,0:T(8,128)(2,1)}, u32[]{:S(2)}, u32[]{:S(2)}) collective-permute-start(bf16[4,2,80,2048]{3,2,1,0:T(8,128)(2,1)} %get-tuple-element.80), channel_id=1, source_target_pairs={{0,16},{16,0},{1,17},{17,1},{2,18},{18,2},{3,19},{19,3},{4,20},{20... | collective-permute-start | bytes 7864328 | tf_op jit(solution)/shard_map/ppermute | solution.py:24
  339.2 51.9 %collective-permute-start.70 = (bf16[4,2,80,2048]{3,2,1,0:T(8,128)(2,1)}, bf16[4,2,80,2048]{3,2,1,0:T(8,128)(2,1)S(1)}, u32[]{:S(2)}, u32[]{:S(2)}) collective-permute-start(bf16[4,2,80,2048]{3,2,1,0:T(8,128)(2,1)} %get-tuple-element.86), channel_id=1, source_target_pairs={{0,16},{16,0},{1,17},{17,1},{2,18},{18,2},{3,19},{19,3},{4,20},{20... | collective-permute-start | bytes 7864328 | tf_op jit(solution)/shard_map/ppermute | solution.py:24
  343.1 22.4 %collective-permute-start.77 = (bf16[2,80,2176]{2,1,0:T(8,128)(2,1)S(1)}, bf16[2,80,2176]{2,1,0:T(8,128)(2,1)S(1)}, u32[]{:S(2)}, u32[]{:S(2)}) collective-permute-start(bf16[2,80,2176]{2,1,0:T(8,128)(2,1)S(1)} %pad_maximum_fusion.16), channel_id=1, source_target_pairs={{0,1},{1,0},{2,3},{3,2},{4,5},{5,4},{6,7},{7,6},{8,9},{9,8},{10,11... | collective-permute-start | bytes 2088968 | tf_op jit(solution)/shard_map/ppermute | solution.py:24
  351.4 28.4 %collective-permute-start.83 = (bf16[2,80,2176]{2,1,0:T(8,128)(2,1)S(1)}, bf16[2,80,2176]{2,1,0:T(8,128)(2,1)S(1)}, u32[]{:S(2)}, u32[]{:S(2)}) collective-permute-start(bf16[2,80,2176]{2,1,0:T(8,128)(2,1)S(1)} %pad_maximum_fusion.18), channel_id=1, source_target_pairs={{0,1},{1,0},{2,3},{3,2},{4,5},{5,4},{6,7},{7,6},{8,9},{9,8},{10,11... | collective-permute-start | bytes 2088968 | tf_op jit(solution)/shard_map/ppermute | solution.py:24
  367.6 76.3 %collective-permute-start.80 = (bf16[80,2176]{1,0:T(8,128)(2,1)}, bf16[80,2176]{1,0:T(8,128)(2,1)}, u32[]{:S(2)}, u32[]{:S(2)}) collective-permute-start(bf16[80,2176]{1,0:T(8,128)(2,1)} %get-tuple-element.141), channel_id=1, source_target_pairs={{0,8},{4,12},{8,0},{12,4},{1,9},{5,13},{9,1},{13,5},{2,10},{6,14},... | collective-permute-start | bytes 1044488 | tf_op jit(solution)/shard_map/ppermute | solution.py:148
  379.8 67.2 %collective-permute-start.81 = (bf16[80,2176]{1,0:T(8,128)(2,1)}, bf16[80,2176]{1,0:T(8,128)(2,1)}, u32[]{:S(2)}, u32[]{:S(2)}) collective-permute-start(bf16[80,2176]{1,0:T(8,128)(2,1)} %get-tuple-element.142), channel_id=1, source_target_pairs={{0,12},{4,0},{8,4},{12,8},{1,13},{5,1},{9,5},{13,9},{2,14},{6,2},{... | collective-permute-start | bytes 1044488 | tf_op jit(solution)/shard_map/ppermute | solution.py:148
  404.1 23.7 %collective-permute-start.65 = (bf16[2,80,2176]{2,1,0:T(8,128)(2,1)}, bf16[2,80,2176]{2,1,0:T(8,128)(2,1)}, u32[]{:S(2)}, u32[]{:S(2)}) collective-permute-start(bf16[2,80,2176]{2,1,0:T(8,128)(2,1)} %pad_maximum_fusion.12.refs_1_), channel_id=1, source_target_pairs={{0,1},{1,0},{2,3},{3,2},{4,5},{5,4},{6,7},{7,6},{8,9},{9,8},{10,11... | collective-permute-start | bytes 2088968 | tf_op jit(solution)/shard_map/ppermute | solution.py:24
  406.4 20.3 %collective-permute-start.67 = (bf16[2,80,2176]{2,1,0:T(8,128)(2,1)S(1)}, bf16[2,80,2176]{2,1,0:T(8,128)(2,1)S(1)}, u32[]{:S(2)}, u32[]{:S(2)}) collective-permute-start(bf16[2,80,2176]{2,1,0:T(8,128)(2,1)S(1)} %pad_maximum_fusion.13), channel_id=1, source_target_pairs={{0,2},{1,3},{2,0},{3,1},{4,6},{5,7},{6,4},{7,5},{8,10},{9,11},{10,... | collective-permute-start | bytes 2088968 | tf_op jit(solution)/shard_map/ppermute | solution.py:24
  426.6 20.5 %collective-permute-start.86 = (bf16[80,2176]{1,0:T(8,128)(2,1)S(1)}, bf16[80,2176]{1,0:T(8,128)(2,1)S(1)}, u32[]{:S(2)}, u32[]{:S(2)}) collective-permute-start(bf16[80,2176]{1,0:T(8,128)(2,1)S(1)} %copy-done.42), channel_id=1, source_target_pairs={{0,4},{4,8},{8,12},{12,0},{1,5},{5,9},{9,13},{13,1},{2,6},{6,10},{... | collective-permute-start | bytes 1044488 | tf_op jit(solution)/shard_map/ppermute | solution.py:148
  439.8 24.1 %collective-permute-start.68 = (bf16[80,2176]{1,0:T(8,128)(2,1)S(1)}, bf16[80,2176]{1,0:T(8,128)(2,1)S(1)}, u32[]{:S(2)}, u32[]{:S(2)}) collective-permute-start(bf16[80,2176]{1,0:T(8,128)(2,1)S(1)} %get-tuple-element.143), channel_id=1, source_target_pairs={{0,8},{4,12},{8,0},{12,4},{1,9},{5,13},{9,1},{13,5},{2,10},{6,14},... | collective-permute-start | bytes 1044488 | tf_op jit(solution)/shard_map/ppermute | solution.py:148
  443.9 20.0 %collective-permute-start.69 = (bf16[80,2176]{1,0:T(8,128)(2,1)S(1)}, bf16[80,2176]{1,0:T(8,128)(2,1)S(1)}, u32[]{:S(2)}, u32[]{:S(2)}) collective-permute-start(bf16[80,2176]{1,0:T(8,128)(2,1)S(1)} %get-tuple-element.144), channel_id=1, source_target_pairs={{0,12},{4,0},{8,4},{12,8},{1,13},{5,1},{9,5},{13,9},{2,14},{6,2},{... | collective-permute-start | bytes 1044488 | tf_op jit(solution)/shard_map/ppermute | solution.py:148
  (115 other events, 1316.0 us)

commit v4 on v3

--- a/solution.py
+++ b/solution.py
@@ -16,6 +16,7 @@
 HEAD = "tensor"
 CORES = 2
 HEADS = 4
+EXTRA = 128
 VMEM_BYTES = 56 * 1024 * 1024
 
 
@@ -155,6 +156,16 @@
     return jnp.where(section == 0, own, other), jnp.where(section == 0, other, own)
 
 
+def gains_in(pieces, count, first):
+    ranks = lax.axis_size(DATA)
+    data = lax.axis_index(DATA)
+    full = jnp.zeros((ranks, count), LOW)
+    for step in range(ranks):
+        lines = pieces[2 * step][0, : count // EXTRA, first : first + EXTRA]
+        full = lax.dynamic_update_slice(full, lines.reshape(1, -1), ((data - step) % ranks, 0))
+    return full
+
+
 def gather_gains(gains):
     ranks = lax.axis_size(DATA)
     data = lax.axis_index(DATA)
@@ -167,6 +178,20 @@
             if step < ranks - 1:
                 gains = ring(gains)
     return by_section(full, flip(full, SECTION, 1))
+
+
+def gains_beside(pairs, gains, ranks):
+    data = lax.axis_index(DATA)
+    width = pairs[0].shape[-1]
+    rows = pairs[0].shape[2]
+    gains = gains.reshape(ranks, -1, 128).astype(LOW)
+    gains = jnp.pad(gains, ((0, 0), (0, rows - gains.shape[1]), (0, 0)))
+    order = sum(groups_of(ranks), ())
+    block = jnp.stack(
+        [lax.dynamic_index_in_dim(gains, (data + k) % ranks, 0, keepdims=False) for k in order]
+    )
+    block = jnp.broadcast_to(block, (HEADS,) + block.shape)
+    return tuple(jnp.concatenate([pair, block], axis=-1) for pair in pairs)
 
 
 def scatter_gains(first, second):
@@ -538,7 +563,7 @@
 
 def sizes_of(pieces, own):
     columns = pieces[0].shape[2]
-    rest = columns - own - own // HEADS
+    rest = columns - own - own // HEADS - EXTRA
     return columns, rest
 
 
@@ -614,7 +639,11 @@
     gain_grads = (
         more[0], gains[3, : own // 2], more[1, : own // 2], gains[0], gains[1], gains[2],
     )
-    return input_grad, grads + tuple(result[: len(pair_shapes)]), gain_grads
+    pairs = tuple(result[: len(pair_shapes)])
+    gain_grads = jnp.concatenate([gain.reshape(ranks, -1) for gain in gain_grads], axis=1)
+    if ranks <= 4:
+        pairs = gains_beside(pairs, gain_grads, ranks)
+    return input_grad, grads + pairs, gain_grads
 
 
 def body(
@@ -646,12 +675,24 @@
     back = min(-(-(WINDOW - 1) // rows), HEADS - 1)
     quarter = 2 * head_width // HEADS
 
+    gain_list = (before_gain, query_gain, key_gain, after_gain, feed_gain, final_gain)
+    sizes = [gain.shape[1] for gain in gain_list]
+    gain_flat = jnp.concatenate([gain[0] for gain in gain_list])
+    gain_block = jnp.zeros((depth, EXTRA), LOW)
+    if ranks > 4:
+        gain_both = gather_gains(gain_flat)
+    else:
+        lines = gain_flat.reshape(-1, EXTRA)
+        for first in (0, depth // CORES):
+            gain_block = lax.dynamic_update_slice(gain_block, lines, (first, 0))
+
     shared = jnp.concatenate([key_matrix[0], value_matrix[0]], axis=1)
     slab = jnp.concatenate(
         [
             query_matrix[0],
             output_matrix[0].T,
             lax.dynamic_slice_in_dim(shared, head * quarter, quarter, 1),
+            gain_block,
             gate_matrix[0],
             up_matrix[0],
             down_matrix[0].T,
@@ -666,12 +707,8 @@
     first_pieces, chunks = gather_slab(halves[0])
     second_pieces, unused = gather_slab(after(halves[1], chunks[3]))
     pieces = first_pieces, second_pieces
-
-    gain_list = (before_gain, query_gain, key_gain, after_gain, feed_gain, final_gain)
-    sizes = [gain.shape[1] for gain in gain_list]
-    gain_both = gather_gains(
-        after(jnp.concatenate([gain[0] for gain in gain_list]), chunks[2])
-    )
+    if ranks <= 4:
+        gain_both = [gains_in(held, sum(sizes), 2 * head_width + quarter) for held in pieces]
 
     first_input = lax.dynamic_index_in_dim(inputs, section, 0, keepdims=False)
     last_cot = lax.dynamic_index_in_dim(out_grad, section, 0, keepdims=False)
@@ -721,24 +758,23 @@
         after(grad_second.astype(LOW), *sums_second), first_input, pair_first, kept_first, layers[0], bias, turns, table, ranks
     )
     total_second, unused = scatter_sums(sums_second, ranks)
-    total_first, mark = scatter_sums(first_sums(slab_first, ranks), ranks)
+    total_first, unused = scatter_sums(first_sums(slab_first, ranks), ranks)
 
     def settle(first, second):
         own, sent = by_section(first, second)
         return jnp.stack(by_section(own, flip(sent, SECTION, 1)))[None]
 
-    gain_own = scatter_gains(
-        *(
-            after(jnp.concatenate([gain.reshape(ranks, -1) for gain in gains], axis=1), mark)
-            for gains in (gains_first, gains_second)
-        )
+    own, sent = by_section(total_first, total_second)
+    gain_own = (
+        scatter_gains(gains_first, gains_second)
+        if ranks > 4
+        else own[: sum(sizes) // 128, slab.shape[1] - EXTRA :].reshape(-1)
     )
     gain_grads, first = [], 0
     for size in sizes:
         gain_grads.append(gain_own[None, first : first + size])
         first += size
 
-    own, sent = by_section(total_first, total_second)
     own = jnp.concatenate(by_section(own, flip(sent, SECTION, 1)))
     starts = [0]
     for step in (head_width, head_width, hidden_width, hidden_width, hidden_width, quarter):

time: 490 us -> 475 us (0.969)
  the two profiles are of different devices: /device:TPU:0 before, /device:TPU:8 now
where the time goes in v4:
time: 475 us; the launch traced here: 467 us
  waiting for transfers between devices  171 us (36%)
  starting transfers between devices  98.8 us (21%)
  Pallas kernels  98 us (21%)
  other arithmetic  58.1 us (12%)
  local copies, waits for them, and re-layouts  38.8 us (8%)
    ppermute x61, waiting for transfers between devices, flip(): return lax.ppermute(value, axis, [(i, i ^ bit) for i in range(count)])  123 us
    pallas_call x8, Pallas kernels, call(): pl.pallas_call(kernel, name=name, out_shape=[jax.ShapeDtypeStruct(shape,...  98 us
    ppermute x61, starting transfers between devices, flip(): return lax.ppermute(value, axis, [(i, i ^ bit) for i in range(count)])  60.4 us
    ppermute x6, waiting for transfers between devices, scatter_sums(): piece = lax.ppermute(piece.astype(LOW), DATA, pairs)  25.4 us
    ppermute x8, waiting for transfers between devices, shifted(): return lax.ppermute(value, axis, pairs)  21.6 us
    ppermute x8, starting transfers between devices, shifted(): return lax.ppermute(value, axis, pairs)  18.6 us
    unnamed x106, local copies, waits for them, and re-layouts  14.4 us
    another operation x8, other arithmetic, gather_slab(): own = jnp.stack([chunk, near, far, across])  14.1 us
  transfers between devices with their start and end apart: 81, of which 34 were waited for; matrix products, arithmetic and copies ran while one was open for 14% of the time, Pallas kernels for 7%

profile of v4, /device:TPU:8, one launch (start us, length us, event | category | flops | bytes accessed | tf_op | source)
XLA Modules:
  0.0 467.2 jit_solution(17612223903095002778)
XLA Ops:
  24.5 3.4 collective-permute-start.2
  28.0 3.4 collective-permute-start.3
  33.8 8.0 %collective-permute-done.2 = bf16[256,640]{1,0:T(8,128)(2,1)S(1)} collective-permute-done((bf16[256,640]{1,0:T(8,128)(2,1)}, bf16[256,640]{1,0:T(8,128)(2,1)S(1)}, u32[]{:S(2)}, u32[]{:S(2)}) %collective-permute-start.2) | collective-permute-done | bytes 327712 | tf_op jit(solution)/shard_map/ppermute | solution.py:36
  59.0 4.9 %collective-permute-done.12 = bf16[80,2304]{1,0:T(8,128)(2,1)} collective-permute-done((bf16[80,2304]{1,0:T(8,128)(2,1)}, bf16[80,2304]{1,0:T(8,128)(2,1)}, u32[]{:S(2)}, u32[]{:S(2)}) %collective-permute-start.12) | collective-permute-done | bytes 368672 | tf_op jit(solution)/shard_map/ppermute | solution.py:25
  93.5 5.5 %collective-permute-done.30 = bf16[80,2304]{1,0:T(8,128)(2,1)S(1)} collective-permute-done((bf16[80,2304]{1,0:T(8,128)(2,1)S(1)}, bf16[80,2304]{1,0:T(8,128)(2,1)S(1)}, u32[]{:S(2)}, u32[]{:S(2)}) %collective-permute-start.30) | collective-permute-done | bytes 368672 | tf_op jit(solution)/shard_map/ppermute | solution.py:25
  114.9 6.4 %collective-permute-done.31 = bf16[80,2304]{1,0:T(8,128)(2,1)S(1)} collective-permute-done((bf16[80,2304]{1,0:T(8,128)(2,1)S(1)}, bf16[80,2304]{1,0:T(8,128)(2,1)S(1)}, u32[]{:S(2)}, u32[]{:S(2)}) %collective-permute-start.31) | collective-permute-done | bytes 368672 | tf_op jit(solution)/shard_map/ppermute | solution.py:25
  121.2 5.0 %collective-permute-done.37 = bf16[80,2304]{1,0:T(8,128)(2,1)S(1)} collective-permute-done((bf16[80,2304]{1,0:T(8,128)(2,1)S(1)}, bf16[80,2304]{1,0:T(8,128)(2,1)S(1)}, u32[]{:S(2)}, u32[]{:S(2)}) %collective-permute-start.37) | collective-permute-done | bytes 368672 | tf_op jit(solution)/shard_map/ppermute | solution.py:25
  128.0 3.3 collective-permute-done.38
  131.4 5.3 %collective-permute-done.35 = bf16[80,2304]{1,0:T(8,128)(2,1)S(1)} collective-permute-done((bf16[80,2304]{1,0:T(8,128)(2,1)S(1)}, bf16[80,2304]{1,0:T(8,128)(2,1)S(1)}, u32[]{:S(2)}, u32[]{:S(2)}) %collective-permute-start.35) | collective-permute-done | bytes 368672 | tf_op jit(solution)/shard_map/ppermute | solution.py:25
  138.0 6.7 %collective-permute-done.39 = bf16[80,2304]{1,0:T(8,128)(2,1)S(1)} collective-permute-done((bf16[80,2304]{1,0:T(8,128)(2,1)S(1)}, bf16[80,2304]{1,0:T(8,128)(2,1)S(1)}, u32[]{:S(2)}, u32[]{:S(2)}) %collective-permute-start.39) | collective-permute-done | bytes 368672 | tf_op jit(solution)/shard_map/ppermute | solution.py:25
  150.1 4.6 keys.2.pair_ref
  154.7 14.4 %forward.2 = (bf16[256,640]{1,0:T(8,128)(2,1)}, bf16[256,1024]{1,0:T(8,128)(2,1)}, f32[256,640]{1,0:T(8,128)}, f32[256,640]{1,0:T(8,128)}, f32[256,640]{1,0:T(8,128)}) custom-call(s32[28]{0:T(128)} %stack.255.table, bf16[256,640]{1,0:T(8,128)(2,1)} %copy-done.14, bf16[768,512]{1,0:T(8,128)(2,1)} %keys.2.pair_ref, f32[256,768]{1,0:T(8,128)} %fusion.8.bias_ref, ...), custom_call_target="tpu_custom_call" | custom-call | flops 6039797760 | bytes 11796480 | tf_op jit(solution)/shard_map/forward/pallas_call | solution.py:536
  170.2 3.7 keys.3
  173.9 3.0 collective-permute-start.41
  176.8 3.2 collective-permute-start.42
  183.4 5.5 %collective-permute-done.41 = bf16[256,512]{1,0:T(8,128)(2,1)S(1)} collective-permute-done((bf16[256,512]{1,0:T(8,128)(2,1)}, bf16[256,512]{1,0:T(8,128)(2,1)S(1)}, u32[]{:S(2)}, u32[]{:S(2)}) %collective-permute-start.41) | collective-permute-done | bytes 262176 | tf_op jit(solution)/shard_map/ppermute | solution.py:36
  190.9 14.3 %forward.3 = (bf16[256,640]{1,0:T(8,128)(2,1)}, bf16[256,1024]{1,0:T(8,128)(2,1)}, f32[256,640]{1,0:T(8,128)}, f32[256,640]{1,0:T(8,128)}, f32[256,640]{1,0:T(8,128)}) custom-call(s32[28]{0:T(128)} %stack.255.table, bf16[256,640]{1,0:T(8,128)(2,1)} %get-tuple-element.51.x_ref, bf16[768,512]{1,0:T(8,128)(2,1)} %pad_maximum_fusion.13.pair_ref, ...), custom_call_target="tpu_custom_call" | custom-call | flops 6039797760 | bytes 11796480 | tf_op jit(solution)/shard_map/forward/pallas_call | solution.py:536
  205.2 24.4 %backward.2 = (bf16[4,2,80,2048]{3,2,1,0:T(8,128)(2,1)}, bf16[4,2,80,2048]{3,2,1,0:T(8,128)(2,1)}, bf16[4,2,80,2048]{3,2,1,0:T(8,128)(2,1)}, bf16[4,2,80,2048]{3...) custom-call(s32[28]{0:T(128)} %stack.255.table, ...), custom_call_target="tpu_custom_call" | custom-call | flops 12079595520 | bytes 23592960 | tf_op jit(solution)/shard_map/backward/pallas_call | solution.py:536
  235.2 6.2 %collective-permute-done.44 = bf16[256,512]{1,0:T(8,128)(2,1)S(1)} collective-permute-done((bf16[256,512]{1,0:T(8,128)(2,1)S(1)}, bf16[256,512]{1,0:T(8,128)(2,1)S(1)}, u32[]{:S(2)}, u32[]{:S(2)}) %collective-permute-start.44) | collective-permute-done | bytes 262176 | tf_op jit(solution)/shard_map/ppermute | solution.py:36
  244.2 6.1 %closing.2 = (bf16[4,4,80,128]{3,2,1,0:T(8,128)(2,1)}, bf16[4,4,80,128]{3,2,1,0:T(8,128)(2,1)}, f32[256,640]{1,0:T(8,128)}, f32[8,640]{1,0:T(8,128)}) custom-call(s32[28]{0:T(128)} %stack.255.table, f32[256,512]{1,0:T(8,128)} %get-tuple-element.57.own_ref, bf16[2,256,512]{2,1,0:T(8,128)(2,1)} %pad_maximum_fusion.22.arrived_ref, ...), custom_call_target="tpu_custom_call" | custom-call | flops 503316480 | bytes 1310720 | tf_op jit(solution)/shard_map/closing/pallas_call | solution.py:536
  267.3 24.3 %backward.3 = (bf16[4,2,80,2048]{3,2,1,0:T(8,128)(2,1)}, bf16[4,2,80,2048]{3,2,1,0:T(8,128)(2,1)}, bf16[4,2,80,2048]{3,2,1,0:T(8,128)(2,1)}, bf16[4,2,80,2048]{3...) custom-call(s32[28]{0:T(128)} %stack.255.table, ...), custom_call_target="tpu_custom_call" | custom-call | flops 12079595520 | bytes 23592960 | tf_op jit(solution)/shard_map/backward/pallas_call | solution.py:536
  297.4 8.5 %collective-permute-start.66 = (bf16[1,80,2304]{2,1,0:T(8,128)(2,1)}, bf16[1,80,2304]{2,1,0:T(8,128)(2,1)}, u32[]{:S(2)}, u32[]{:S(2)}) collective-permute-start(bf16[1,80,2304]{2,1,0:T(8,128)(2,1)} %get-tuple-element.100), channel_id=1, source_target_pairs={{0,2},{1,3},{2,0},{3,1},{4,6},{5,7},{6,4},{7,5},{8,10},{9,11},{10,... | collective-permute-start | bytes 1105928 | tf_op jit(solution)/shard_map/ppermute | solution.py:25
  313.9 6.2 %closing.3 = (bf16[4,4,80,128]{3,2,1,0:T(8,128)(2,1)}, bf16[4,4,80,128]{3,2,1,0:T(8,128)(2,1)}, f32[256,640]{1,0:T(8,128)}, f32[8,640]{1,0:T(8,128)}) custom-call(s32[28]{0:T(128)} %stack.255.table, f32[256,512]{1,0:T(8,128)} %get-tuple-element.74.own_ref, bf16[2,256,512]{2,1,0:T(8,128)(2,1)} %pad_maximum_fusion.23.arrived_ref, bf16[256,640]{1,0:T(8,128)(2,1)} %copy-done.14, ...), custom_call_target="tpu_custom_call" | custom-call | flops 503316480 | bytes 1310720 | tf_op jit(solution)/shard_map/closing/pallas_call | solution.py:536
  326.3 5.8 %collective-permute-start.67 = (bf16[2,80,2304]{2,1,0:T(8,128)(2,1)S(1)}, bf16[2,80,2304]{2,1,0:T(8,128)(2,1)S(1)}, u32[]{:S(2)}, u32[]{:S(2)}) collective-permute-start(bf16[2,80,2304]{2,1,0:T(8,128)(2,1)S(1)} %pad_maximum_fusion.18), channel_id=1, source_target_pairs={{0,1},{1,0},{2,3},{3,2},{4,5},{5,4},{6,7},{7,6},{8,9},{9,8},{10,11... | collective-permute-start | bytes 2211848 | tf_op jit(solution)/shard_map/ppermute | solution.py:25
  334.7 14.6 %collective-permute-done.67 = bf16[2,80,2304]{2,1,0:T(8,128)(2,1)S(1)} collective-permute-done((bf16[2,80,2304]{2,1,0:T(8,128)(2,1)S(1)}, bf16[2,80,2304]{2,1,0:T(8,128)(2,1)S(1)}, u32[]{:S(2)}, u32[]{:S(2)}) %collective-permute-start.67) | collective-permute-done | bytes 737312 | tf_op jit(solution)/shard_map/ppermute | solution.py:25
  353.2 11.3 %collective-permute-done.73 = bf16[2,80,2304]{2,1,0:T(8,128)(2,1)S(1)} collective-permute-done((bf16[2,80,2304]{2,1,0:T(8,128)(2,1)S(1)}, bf16[2,80,2304]{2,1,0:T(8,128)(2,1)S(1)}, u32[]{:S(2)}, u32[]{:S(2)}) %collective-permute-start.73) | collective-permute-done | bytes 737312 | tf_op jit(solution)/shard_map/ppermute | solution.py:25
  374.6 6.7 %collective-permute-done.54 = bf16[1,80,2304]{2,1,0:T(8,128)(2,1)S(1)} collective-permute-done((bf16[1,80,2304]{2,1,0:T(8,128)(2,1)S(1)}, bf16[1,80,2304]{2,1,0:T(8,128)(2,1)S(1)}, u32[]{:S(2)}, u32[]{:S(2)}) %collective-permute-start.54) | collective-permute-done | bytes 368672 | tf_op jit(solution)/shard_map/ppermute | solution.py:25
  383.3 6.7 %collective-permute-done.61 = bf16[1,80,2304]{2,1,0:T(8,128)(2,1)S(1)} collective-permute-done((bf16[1,80,2304]{2,1,0:T(8,128)(2,1)S(1)}, bf16[1,80,2304]{2,1,0:T(8,128)(2,1)S(1)}, u32[]{:S(2)}, u32[]{:S(2)}) %collective-permute-start.61) | collective-permute-done | bytes 368672 | tf_op jit(solution)/shard_map/ppermute | solution.py:25
  393.6 13.1 %collective-permute-done.55 = bf16[2,80,2304]{2,1,0:T(8,128)(2,1)S(1)} collective-permute-done((bf16[2,80,2304]{2,1,0:T(8,128)(2,1)S(1)}, bf16[2,80,2304]{2,1,0:T(8,128)(2,1)S(1)}, u32[]{:S(2)}, u32[]{:S(2)}) %collective-permute-start.55) | collective-permute-done | bytes 737312 | tf_op jit(solution)/shard_map/ppermute | solution.py:25
  409.1 12.6 %collective-permute-done.62 = bf16[2,80,2304]{2,1,0:T(8,128)(2,1)S(1)} collective-permute-done((bf16[2,80,2304]{2,1,0:T(8,128)(2,1)S(1)}, bf16[2,80,2304]{2,1,0:T(8,128)(2,1)S(1)}, u32[]{:S(2)}, u32[]{:S(2)}) %collective-permute-start.62) | collective-permute-done | bytes 737312 | tf_op jit(solution)/shard_map/ppermute | solution.py:25
  427.0 15.4 %collective-permute-done.58 = bf16[80,2304]{1,0:T(8,128)(2,1)S(1)} collective-permute-done((bf16[80,2304]{1,0:T(8,128)(2,1)S(1)}, bf16[80,2304]{1,0:T(8,128)(2,1)S(1)}, u32[]{:S(2)}, u32[]{:S(2)}) %collective-permute-start.58) | collective-permute-done | bytes 368672 | tf_op jit(solution)/shard_map/ppermute | solution.py:149
  442.4 10.0 %collective-permute-done.59 = bf16[80,2304]{1,0:T(8,128)(2,1)S(1)} collective-permute-done((bf16[80,2304]{1,0:T(8,128)(2,1)S(1)}, bf16[80,2304]{1,0:T(8,128)(2,1)S(1)}, u32[]{:S(2)}, u32[]{:S(2)}) %collective-permute-start.59) | collective-permute-done | bytes 368672 | tf_op jit(solution)/shard_map/ppermute | solution.py:149
  (401 shorter events, 192.3 us)
Async XLA Ops:
  14.7 18.3 %collective-permute-start.7 = (bf16[80,2304]{1,0:T(8,128)(2,1)S(1)}, bf16[80,2304]{1,0:T(8,128)(2,1)}, u32[]{:S(2)}, u32[]{:S(2)}) collective-permute-start(bf16[80,2304]{1,0:T(8,128)(2,1)S(1)} %get-tuple-element.135), channel_id=1, source_target_pairs={{0,2},{1,3},{2,0},{3,1},{4,6},{5,7},{6,4},{7,5},{8,10},{9,11},{10,... | collective-permute-start | bytes 1105928 | tf_op jit(solution)/shard_map/ppermute | solution.py:25
  21.0 25.9 %collective-permute-start.6 = (bf16[80,2304]{1,0:T(8,128)(2,1)S(1)}, bf16[80,2304]{1,0:T(8,128)(2,1)}, u32[]{:S(2)}, u32[]{:S(2)}) collective-permute-start(bf16[80,2304]{1,0:T(8,128)(2,1)S(1)} %get-tuple-element.135), channel_id=1, source_target_pairs={{0,1},{1,0},{2,3},{3,2},{4,5},{5,4},{6,7},{7,6},{8,9},{9,8},{10,11... | collective-permute-start | bytes 1105928 | tf_op jit(solution)/shard_map/ppermute | solution.py:25
  52.4 19.4 %collective-permute-start.14 = (bf16[80,2304]{1,0:T(8,128)(2,1)S(1)}, bf16[80,2304]{1,0:T(8,128)(2,1)}, u32[]{:S(2)}, u32[]{:S(2)}) collective-permute-start(bf16[80,2304]{1,0:T(8,128)(2,1)S(1)} %collective-permute-done.4), channel_id=1, source_target_pairs={{0,1},{1,0},{2,3},{3,2},{4,5},{5,4},{6,7},{7,6},{8,9},{9,8},{10,11... | collective-permute-start | bytes 1105928 | tf_op jit(solution)/shard_map/ppermute | solution.py:25
  53.9 23.6 %collective-permute-start.15 = (bf16[80,2304]{1,0:T(8,128)(2,1)S(1)}, bf16[80,2304]{1,0:T(8,128)(2,1)}, u32[]{:S(2)}, u32[]{:S(2)}) collective-permute-start(bf16[80,2304]{1,0:T(8,128)(2,1)S(1)} %collective-permute-done.4), channel_id=1, source_target_pairs={{0,2},{1,3},{2,0},{3,1},{4,6},{5,7},{6,4},{7,5},{8,10},{9,11},{10,... | collective-permute-start | bytes 1105928 | tf_op jit(solution)/shard_map/ppermute | solution.py:25
  56.4 20.3 %collective-permute-start.22 = (bf16[80,2304]{1,0:T(8,128)(2,1)}, bf16[80,2304]{1,0:T(8,128)(2,1)S(1)}, u32[]{:S(2)}, u32[]{:S(2)}) collective-permute-start(bf16[80,2304]{1,0:T(8,128)(2,1)} %after.4), channel_id=1, source_target_pairs={{0,4},{4,8},{8,12},{12,0},{1,5},{5,9},{9,13},{13,1},{2,6},{6,10},{... | collective-permute-start | bytes 1105928 | tf_op jit(solution)/shard_map/ppermute | solution.py:30
  58.7 20.9 %collective-permute-start.26 = (bf16[80,2304]{1,0:T(8,128)(2,1)}, bf16[80,2304]{1,0:T(8,128)(2,1)}, u32[]{:S(2)}, u32[]{:S(2)}) collective-permute-start(bf16[80,2304]{1,0:T(8,128)(2,1)} %after.4), channel_id=1, source_target_pairs={{0,2},{1,3},{2,0},{3,1},{4,6},{5,7},{6,4},{7,5},{8,10},{9,11},{10,... | collective-permute-start | bytes 1105928 | tf_op jit(solution)/shard_map/ppermute | solution.py:25
  83.3 18.2 %collective-permute-start.27 = (bf16[80,2304]{1,0:T(8,128)(2,1)}, bf16[80,2304]{1,0:T(8,128)(2,1)S(1)}, u32[]{:S(2)}, u32[]{:S(2)}) collective-permute-start(bf16[80,2304]{1,0:T(8,128)(2,1)} %collective-permute-done.26), channel_id=1, source_target_pairs={{0,1},{1,0},{2,3},{3,2},{4,5},{5,4},{6,7},{7,6},{8,9},{9,8},{10,11... | collective-permute-start | bytes 1105928 | tf_op jit(solution)/shard_map/ppermute | solution.py:25
  104.0 41.9 %collective-permute-start.9 = (bf16[4,80,2304]{2,1,0:T(8,128)(2,1)S(1)}, bf16[4,80,2304]{2,1,0:T(8,128)(2,1)S(1)}, u32[]{:S(2)}, u32[]{:S(2)}) collective-permute-start(bf16[4,80,2304]{2,1,0:T(8,128)(2,1)S(1)} %pad_maximum_fusion.2.refs_0_), channel_id=1, source_target_pairs={{0,16},{16,0},{1,17},{17,1},{2,18},{18,2},{3,19},{19,3},{4,20},{20... | collective-permute-start | bytes 4423688 | tf_op jit(solution)/shard_map/ppermute | solution.py:25
  106.9 39.6 %collective-permute-start.13 = (bf16[4,80,2304]{2,1,0:T(8,128)(2,1)S(1)}, bf16[4,80,2304]{2,1,0:T(8,128)(2,1)S(1)}, u32[]{:S(2)}, u32[]{:S(2)}) collective-permute-start(bf16[4,80,2304]{2,1,0:T(8,128)(2,1)S(1)} %copy-done.5), channel_id=1, source_target_pairs={{0,16},{16,0},{1,17},{17,1},{2,18},{18,2},{3,19},{19,3},{4,20},{20... | collective-permute-start | bytes 4423688 | tf_op jit(solution)/shard_map/ppermute | solution.py:25
  106.9 39.7 %collective-permute-start.17 = (bf16[4,80,2304]{2,1,0:T(8,128)(2,1)S(1)}, bf16[4,80,2304]{2,1,0:T(8,128)(2,1)S(1)}, u32[]{:S(2)}, u32[]{:S(2)}) collective-permute-start(bf16[4,80,2304]{2,1,0:T(8,128)(2,1)S(1)} %pad_maximum_fusion.4.refs_4_), channel_id=1, source_target_pairs={{0,16},{16,0},{1,17},{17,1},{2,18},{18,2},{3,19},{19,3},{4,20},{20... | collective-permute-start | bytes 4423688 | tf_op jit(solution)/shard_map/ppermute | solution.py:25
  131.4 18.7 %collective-permute-start.21 = (bf16[4,80,2304]{2,1,0:T(8,128)(2,1)}, bf16[4,80,2304]{2,1,0:T(8,128)(2,1)}, u32[]{:S(2)}, u32[]{:S(2)}) collective-permute-start(bf16[4,80,2304]{2,1,0:T(8,128)(2,1)} %pad_maximum_fusion.5.refs_6_), channel_id=1, source_target_pairs={{0,16},{16,0},{1,17},{17,1},{2,18},{18,2},{3,19},{19,3},{4,20},{20... | collective-permute-start | bytes 4423688 | tf_op jit(solution)/shard_map/ppermute | solution.py:25
  144.6 24.4 %collective-permute-start.28 = (bf16[4,80,2304]{2,1,0:T(8,128)(2,1)}, bf16[4,80,2304]{2,1,0:T(8,128)(2,1)}, u32[]{:S(2)}, u32[]{:S(2)}) collective-permute-start(bf16[4,80,2304]{2,1,0:T(8,128)(2,1)} %pad_maximum_fusion.6.refs_0_), channel_id=1, source_target_pairs={{0,16},{16,0},{1,17},{17,1},{2,18},{18,2},{3,19},{19,3},{4,20},{20... | collective-permute-start | bytes 4423688 | tf_op jit(solution)/shard_map/ppermute | solution.py:25
  146.0 23.1 %collective-permute-start.32 = (bf16[4,80,2304]{2,1,0:T(8,128)(2,1)}, bf16[4,80,2304]{2,1,0:T(8,128)(2,1)S(1)}, u32[]{:S(2)}, u32[]{:S(2)}) collective-permute-start(bf16[4,80,2304]{2,1,0:T(8,128)(2,1)} %pad_maximum_fusion.7.refs_2_), channel_id=1, source_target_pairs={{0,16},{16,0},{1,17},{17,1},{2,18},{18,2},{3,19},{19,3},{4,20},{20... | collective-permute-start | bytes 4423688 | tf_op jit(solution)/shard_map/ppermute | solution.py:25
  146.5 22.6 %collective-permute-start.36 = (bf16[4,80,2304]{2,1,0:T(8,128)(2,1)}, bf16[4,80,2304]{2,1,0:T(8,128)(2,1)}, u32[]{:S(2)}, u32[]{:S(2)}) collective-permute-start(bf16[4,80,2304]{2,1,0:T(8,128)(2,1)} %pad_maximum_fusion.8.refs_4_), channel_id=1, source_target_pairs={{0,16},{16,0},{1,17},{17,1},{2,18},{18,2},{3,19},{19,3},{4,20},{20... | collective-permute-start | bytes 4423688 | tf_op jit(solution)/shard_map/ppermute | solution.py:25
  147.2 22.0 %collective-permute-start.40 = (bf16[4,80,2304]{2,1,0:T(8,128)(2,1)}, bf16[4,80,2304]{2,1,0:T(8,128)(2,1)}, u32[]{:S(2)}, u32[]{:S(2)}) collective-permute-start(bf16[4,80,2304]{2,1,0:T(8,128)(2,1)} %pad_maximum_fusion.9.refs_6_), channel_id=1, source_target_pairs={{0,16},{16,0},{1,17},{17,1},{2,18},{18,2},{3,19},{19,3},{4,20},{20... | collective-permute-start | bytes 4423688 | tf_op jit(solution)/shard_map/ppermute | solution.py:25
  229.6 25.4 %collective-permute-start.46 = (bf16[4,2,80,2048]{3,2,1,0:T(8,128)(2,1)}, bf16[4,2,80,2048]{3,2,1,0:T(8,128)(2,1)}, u32[]{:S(2)}, u32[]{:S(2)}) collective-permute-start(bf16[4,2,80,2048]{3,2,1,0:T(8,128)(2,1)} %get-tuple-element.63), channel_id=1, source_target_pairs={{0,16},{16,0},{1,17},{17,1},{2,18},{18,2},{3,19},{19,3},{4,20},{20... | collective-permute-start | bytes 7864328 | tf_op jit(solution)/shard_map/ppermute | solution.py:25
  234.7 27.0 %collective-permute-start.48 = (bf16[4,2,80,2048]{3,2,1,0:T(8,128)(2,1)}, bf16[4,2,80,2048]{3,2,1,0:T(8,128)(2,1)}, u32[]{:S(2)}, u32[]{:S(2)}) collective-permute-start(bf16[4,2,80,2048]{3,2,1,0:T(8,128)(2,1)} %get-tuple-element.69), channel_id=1, source_target_pairs={{0,16},{16,0},{1,17},{17,1},{2,18},{18,2},{3,19},{19,3},{4,20},{20... | collective-permute-start | bytes 7864328 | tf_op jit(solution)/shard_map/ppermute | solution.py:25
  297.4 24.9 %collective-permute-start.66 = (bf16[1,80,2304]{2,1,0:T(8,128)(2,1)}, bf16[1,80,2304]{2,1,0:T(8,128)(2,1)}, u32[]{:S(2)}, u32[]{:S(2)}) collective-permute-start(bf16[1,80,2304]{2,1,0:T(8,128)(2,1)} %get-tuple-element.100), channel_id=1, source_target_pairs={{0,2},{1,3},{2,0},{3,1},{4,6},{5,7},{6,4},{7,5},{8,10},{9,11},{10,... | collective-permute-start | bytes 1105928 | tf_op jit(solution)/shard_map/ppermute | solution.py:25
  307.1 19.1 %collective-permute-start.72 = (bf16[1,80,2304]{2,1,0:T(8,128)(2,1)}, bf16[1,80,2304]{2,1,0:T(8,128)(2,1)}, u32[]{:S(2)}, u32[]{:S(2)}) collective-permute-start(bf16[1,80,2304]{2,1,0:T(8,128)(2,1)} %get-tuple-element.106), channel_id=1, source_target_pairs={{0,2},{1,3},{2,0},{3,1},{4,6},{5,7},{6,4},{7,5},{8,10},{9,11},{10,... | collective-permute-start | bytes 1105928 | tf_op jit(solution)/shard_map/ppermute | solution.py:25
  311.2 20.8 %collective-permute-start.74 = (bf16[1,80,2304]{2,1,0:T(8,128)(2,1)}, bf16[1,80,2304]{2,1,0:T(8,128)(2,1)}, u32[]{:S(2)}, u32[]{:S(2)}) collective-permute-start(bf16[1,80,2304]{2,1,0:T(8,128)(2,1)} %get-tuple-element.107), channel_id=1, source_target_pairs={{0,1},{1,0},{2,3},{3,2},{4,5},{5,4},{6,7},{7,6},{8,9},{9,8},{10,11... | collective-permute-start | bytes 1105928 | tf_op jit(solution)/shard_map/ppermute | solution.py:25
  312.1 56.5 %collective-permute-start.52 = (bf16[4,2,80,2048]{3,2,1,0:T(8,128)(2,1)}, bf16[4,2,80,2048]{3,2,1,0:T(8,128)(2,1)}, u32[]{:S(2)}, u32[]{:S(2)}) collective-permute-start(bf16[4,2,80,2048]{3,2,1,0:T(8,128)(2,1)} %get-tuple-element.80), channel_id=1, source_target_pairs={{0,16},{16,0},{1,17},{17,1},{2,18},{18,2},{3,19},{19,3},{4,20},{20... | collective-permute-start | bytes 7864328 | tf_op jit(solution)/shard_map/ppermute | solution.py:25
  322.3 49.5 %collective-permute-start.60 = (bf16[4,2,80,2048]{3,2,1,0:T(8,128)(2,1)}, bf16[4,2,80,2048]{3,2,1,0:T(8,128)(2,1)S(1)}, u32[]{:S(2)}, u32[]{:S(2)}) collective-permute-start(bf16[4,2,80,2048]{3,2,1,0:T(8,128)(2,1)} %get-tuple-element.86), channel_id=1, source_target_pairs={{0,16},{16,0},{1,17},{17,1},{2,18},{18,2},{3,19},{19,3},{4,20},{20... | collective-permute-start | bytes 7864328 | tf_op jit(solution)/shard_map/ppermute | solution.py:25
  326.3 23.1 %collective-permute-start.67 = (bf16[2,80,2304]{2,1,0:T(8,128)(2,1)S(1)}, bf16[2,80,2304]{2,1,0:T(8,128)(2,1)S(1)}, u32[]{:S(2)}, u32[]{:S(2)}) collective-permute-start(bf16[2,80,2304]{2,1,0:T(8,128)(2,1)S(1)} %pad_maximum_fusion.18), channel_id=1, source_target_pairs={{0,1},{1,0},{2,3},{3,2},{4,5},{5,4},{6,7},{7,6},{8,9},{9,8},{10,11... | collective-permute-start | bytes 2211848 | tf_op jit(solution)/shard_map/ppermute | solution.py:25
  334.4 30.1 %collective-permute-start.73 = (bf16[2,80,2304]{2,1,0:T(8,128)(2,1)S(1)}, bf16[2,80,2304]{2,1,0:T(8,128)(2,1)S(1)}, u32[]{:S(2)}, u32[]{:S(2)}) collective-permute-start(bf16[2,80,2304]{2,1,0:T(8,128)(2,1)S(1)} %pad_maximum_fusion.20), channel_id=1, source_target_pairs={{0,1},{1,0},{2,3},{3,2},{4,5},{5,4},{6,7},{7,6},{8,9},{9,8},{10,11... | collective-permute-start | bytes 2211848 | tf_op jit(solution)/shard_map/ppermute | solution.py:25
  350.5 74.6 %collective-permute-start.70 = (bf16[80,2304]{1,0:T(8,128)(2,1)S(1)}, bf16[80,2304]{1,0:T(8,128)(2,1)S(1)}, u32[]{:S(2)}, u32[]{:S(2)}) collective-permute-start(bf16[80,2304]{1,0:T(8,128)(2,1)S(1)} %get-tuple-element.138), channel_id=1, source_target_pairs={{0,8},{4,12},{8,0},{12,4},{1,9},{5,13},{9,1},{13,5},{2,10},{6,14},... | collective-permute-start | bytes 1105928 | tf_op jit(solution)/shard_map/ppermute | solution.py:149
  364.5 61.8 %collective-permute-start.71 = (bf16[80,2304]{1,0:T(8,128)(2,1)S(1)}, bf16[80,2304]{1,0:T(8,128)(2,1)S(1)}, u32[]{:S(2)}, u32[]{:S(2)}) collective-permute-start(bf16[80,2304]{1,0:T(8,128)(2,1)S(1)} %get-tuple-element.139), channel_id=1, source_target_pairs={{0,12},{4,0},{8,4},{12,8},{1,13},{5,1},{9,5},{13,9},{2,14},{6,2},{... | collective-permute-start | bytes 1105928 | tf_op jit(solution)/shard_map/ppermute | solution.py:149
  367.2 59.3 %collective-permute-start.76 = (bf16[80,2304]{1,0:T(8,128)(2,1)S(1)}, bf16[80,2304]{1,0:T(8,128)(2,1)S(1)}, u32[]{:S(2)}, u32[]{:S(2)}) collective-permute-start(bf16[80,2304]{1,0:T(8,128)(2,1)S(1)} %fusion.50), channel_id=1, source_target_pairs={{0,4},{4,8},{8,12},{12,0},{1,5},{5,9},{9,13},{13,1},{2,6},{6,10},{... | collective-permute-start | bytes 1105928 | tf_op jit(solution)/shard_map/ppermute | solution.py:149
  421.7 20.7 %collective-permute-start.58 = (bf16[80,2304]{1,0:T(8,128)(2,1)S(1)}, bf16[80,2304]{1,0:T(8,128)(2,1)S(1)}, u32[]{:S(2)}, u32[]{:S(2)}) collective-permute-start(bf16[80,2304]{1,0:T(8,128)(2,1)S(1)} %get-tuple-element.140), channel_id=1, source_target_pairs={{0,8},{4,12},{8,0},{12,4},{1,9},{5,13},{9,1},{13,5},{2,10},{6,14},... | collective-permute-start | bytes 1105928 | tf_op jit(solution)/shard_map/ppermute | solution.py:149
  423.5 28.9 %collective-permute-start.59 = (bf16[80,2304]{1,0:T(8,128)(2,1)S(1)}, bf16[80,2304]{1,0:T(8,128)(2,1)S(1)}, u32[]{:S(2)}, u32[]{:S(2)}) collective-permute-start(bf16[80,2304]{1,0:T(8,128)(2,1)S(1)} %get-tuple-element.141), channel_id=1, source_target_pairs={{0,12},{4,0},{8,4},{12,8},{1,13},{5,1},{9,5},{13,9},{2,14},{6,2},{... | collective-permute-start | bytes 1105928 | tf_op jit(solution)/shard_map/ppermute | solution.py:149
  425.1 27.3 %collective-permute-start.65 = (bf16[80,2304]{1,0:T(8,128)(2,1)S(1)}, bf16[80,2304]{1,0:T(8,128)(2,1)S(1)}, u32[]{:S(2)}, u32[]{:S(2)}) collective-permute-start(bf16[80,2304]{1,0:T(8,128)(2,1)S(1)} %fusion.49), channel_id=1, source_target_pairs={{0,4},{4,8},{8,12},{12,0},{1,5},{5,9},{9,13},{13,1},{2,6},{6,10},{... | collective-permute-start | bytes 1105928 | tf_op jit(solution)/shard_map/ppermute | solution.py:149
  426.4 26.5 %collective-permute-start.43 = (bf16[256,640]{1,0:T(8,128)(2,1)S(1)}, bf16[256,640]{1,0:T(8,128)(2,1)S(1)}, u32[]{:S(2)}, u32[]{:S(2)}) collective-permute-start(bf16[256,640]{1,0:T(8,128)(2,1)S(1)} %broadcast_select_fusion.9), channel_id=1, source_target_pairs={{0,16},{16,0},{1,17},{17,1},{2,18},{18,2},{3,19},{19,3},{4,20},{20... | collective-permute-start | bytes 983048 | tf_op jit(solution)/shard_map/ppermute | solution.py:25
  426.5 27.4 %collective-permute-start.51 = (f32[256,640]{1,0:T(8,128)S(1)}, f32[256,640]{1,0:T(8,128)S(1)}, u32[]{:S(2)}, u32[]{:S(2)}) collective-permute-start(f32[256,640]{1,0:T(8,128)S(1)} %broadcast_select_fusion.7), channel_id=1, source_target_pairs={{0,16},{16,0},{1,17},{17,1},{2,18},{18,2},{3,19},{19,3},{4,20},{20... | collective-permute-start | bytes 1966088 | tf_op jit(solution)/shard_map/ppermute | solution.py:25
  (91 other events, 982.5 us)
